TPU v7x, 32 devices: a whole 2x2x4 slice. The times are simulated.
32 devices in a mesh: dp: 8 (over z, y), mp: 4 (over x, core).
Axes of the slice: x: 2, y: 2, z: 4, core: 2. Of those that a mesh axis runs over, the one named last changes fastest.
Arguments:
- images: bfloat16 [48, 3072], P('dp'), may hold values from -1 to 1
- noises: bfloat16 [3, 16, 3072], P(None, 'dp'), may hold values from -6 to 6
- order: int32 [48], P('dp'), may hold values from 0 to 5, as said below
- time_index: int32 [3, 16], P(None, 'dp'), may hold values from 0 to 999
- io_weight: float32 [6144], P(('mp', 'dp')), may hold values from -0.875 to 0.875
- conv_weight: float32 [4, 9, 256, 256], P(None, None, 'dp', 'mp'), may hold values from -0.125 to 0.125
- time_weight: float32 [2, 256, 256], P(None, 'dp', 'mp'), may hold values from -0.375 to 0.375
- attn_weight: float32 [256, 4, 256], P('dp', None, 'mp'), may hold values from -0.375 to 0.375
- norm_param: float32 [3072], P(('mp', 'dp'))
- io_first: float32 [6144], P(('mp', 'dp')), may hold values from -0.00390625 to 0.00390625
- conv_first: float32 [4, 9, 256, 256], P(None, None, 'dp', 'mp'), may hold values from -0.00390625 to 0.00390625
- time_first: float32 [2, 256, 256], P(None, 'dp', 'mp'), may hold values from -0.00390625 to 0.00390625
- attn_first: float32 [256, 4, 256], P('dp', None, 'mp'), may hold values from -0.00390625 to 0.00390625
- norm_first: float32 [3072], P(('mp', 'dp')), may hold values from -0.015625 to 0.015625
- io_second: float32 [6144], P(('mp', 'dp')), may hold values from 3.6209215e-07 to 1.4483686e-06
- conv_second: float32 [4, 9, 256, 256], P(None, None, 'dp', 'mp'), may hold values from 3.6209215e-07 to 1.4483686e-06
- time_second: float32 [2, 256, 256], P(None, 'dp', 'mp'), may hold values from 3.6209215e-07 to 1.4483686e-06
- attn_second: float32 [256, 4, 256], P('dp', None, 'mp'), may hold values from 3.6209215e-07 to 1.4483686e-06
- norm_second: float32 [3072], P(('mp', 'dp')), may hold values from 5.7934744e-06 to 2.3173898e-05
- io_average: float32 [6144], P(('mp', 'dp')), may hold values from -0.875 to 0.875
- conv_average: float32 [4, 9, 256, 256], P(None, None, 'dp', 'mp'), may hold values from -0.125 to 0.125
- time_average: float32 [2, 256, 256], P(None, 'dp', 'mp'), may hold values from -0.375 to 0.375
- attn_average: float32 [256, 4, 256], P('dp', None, 'mp'), may hold values from -0.375 to 0.375
- norm_average: float32 [3072], P(('mp', 'dp'))
Outputs:
- io_new: float32 [6144], P(('mp', 'dp'))
- conv_new: float32 [4, 9, 256, 256], P(None, None, 'dp', 'mp')
- time_new: float32 [2, 256, 256], P(None, 'dp', 'mp')
- attn_new: float32 [256, 4, 256], P('dp', None, 'mp')
- norm_new: float32 [3072], P(('mp', 'dp'))
- io_first_new: float32 [6144], P(('mp', 'dp'))
- conv_first_new: float32 [4, 9, 256, 256], P(None, None, 'dp', 'mp')
- time_first_new: float32 [2, 256, 256], P(None, 'dp', 'mp')
- attn_first_new: float32 [256, 4, 256], P('dp', None, 'mp')
- norm_first_new: float32 [3072], P(('mp', 'dp'))
- io_second_new: float32 [6144], P(('mp', 'dp'))
- conv_second_new: float32 [4, 9, 256, 256], P(None, None, 'dp', 'mp')
- time_second_new: float32 [2, 256, 256], P(None, 'dp', 'mp')
- attn_second_new: float32 [256, 4, 256], P('dp', None, 'mp')
- norm_second_new: float32 [3072], P(('mp', 'dp'))
- io_average_new: float32 [6144], P(('mp', 'dp'))
- conv_average_new: float32 [4, 9, 256, 256], P(None, None, 'dp', 'mp')
- time_average_new: float32 [2, 256, 256], P(None, 'dp', 'mp')
- attn_average_new: float32 [256, 4, 256], P('dp', None, 'mp')
- norm_average_new: float32 [3072], P(('mp', 'dp'))
- loss_sums: float32 [3], replicated
- transport_cost: float32 [3], replicated
- grad_norm: float32 [], replicated
Inputs may be any that keep to these rules, and one draw needn't show every extreme that they name: `order`: each aligned block of 6 entries is a permutation of 0 to 5.
All inputs are finite; a program needn't handle non-finite values.
Results may differ from a plain program's by a relative error of at most 0.0018.
The roundings to bfloat16 on the way count: a program that leaves them out, or rounds other values in their place, can miss the bound.
Values may be sent and summed in bfloat16 or wider, within the bound.
A program may use at most 128 MiB of HBM per device.

v0:
```python
from functools import partial
import math

import jax
import jax.numpy as jnp
from jax import lax
from jax.sharding import PartitionSpec as P

CH = 256
GROUPS = 32
HD = 64
SUB = 12
SINK = 10
NT = 1000
STEP = 5


EPS_NORM = 1e-05
SINK_EPS = 0.01
CLIP_NORM = 1.0
BETA_ONE = 0.5
BETA_TWO = 0.5
ADAM_EPS = 1e-08
WEIGHT_DECAY = 0.01
EMA_DECAY = 0.9
RATES = (0.06, 0.01, 0.03, 0.03, 0.3)
HIGH = lax.Precision.HIGHEST
OFFSETS = [(row_off, col_off) for row_off in (-1, 0, 1) for col_off in (-1, 0, 1)]


def shifted(field, row_step, col_step):
    side = math.isqrt(field.shape[-1])
    leading = field.shape[:-1]
    grid = field.reshape(leading + (side, side))
    padded = jnp.pad(grid, [(0, 0)] * len(leading) + [(1, 1), (1, 1)])
    moved = padded[..., 1 + row_step : 1 + row_step + side, 1 + col_step : 1 + col_step + side]
    return moved.reshape(leading + (side * side,))


def stacked_shifts(inputs):
    return jnp.stack([shifted(inputs, row_off, col_off) for row_off, col_off in OFFSETS], axis=1)


def conv_apply(inputs, kernel):
    return jnp.einsum(
        "nkcp,kco->nop", stacked_shifts(inputs), kernel, preferred_element_type=jnp.float32
    )


def conv_weight_grad(inputs, grads_low):
    return jnp.einsum(
        "nkcp,nop->kco", stacked_shifts(inputs), grads_low, preferred_element_type=jnp.float32
    )


def conv_transpose(grads_low, kernel):
    terms = jnp.einsum("nop,kco->nkcp", grads_low, kernel, preferred_element_type=jnp.float32)
    total = jnp.zeros_like(terms[:, 0])
    for place, (row_off, col_off) in enumerate(OFFSETS):
        total = total + shifted(terms[:, place], -row_off, -col_off)
    return total


def norm_act(field, gain, bias, active):
    count, channels, spots = field.shape
    grouped = field.reshape(count, channels // (CH // GROUPS), CH // GROUPS, spots)
    center = jnp.mean(grouped, axis=(2, 3), keepdims=True)
    centred = grouped - center
    spread = jnp.mean(centred * centred, axis=(2, 3), keepdims=True)
    normed = (centred * lax.rsqrt(spread + EPS_NORM)).reshape(field.shape)
    normed = normed * gain[None, :, None] + bias[None, :, None]
    if active:
        return jax.nn.silu(normed)
    return normed


def time_features(time_index):
    times = (time_index.astype(jnp.float32) + 0.5) / NT
    half = CH // 2
    frequency = jnp.exp(-math.log(10000.0) * jnp.arange(half, dtype=jnp.float32) / half)
    angles = 1000.0 * times[:, None] * frequency[None, :]
    return jnp.concatenate([jnp.sin(angles), jnp.cos(angles)], axis=1)


def gather_channels(field):
    return lax.all_gather(field, "mp", axis=1, tiled=True)


def sum_channels(field):
    return lax.psum_scatter(
        field.astype(jnp.bfloat16), "mp", scatter_dimension=1, tiled=True
    ).astype(jnp.float32)


def adam_update(weight, first, second, average, gradient, rate):
    first = BETA_ONE * first + (1 - BETA_ONE) * gradient
    second = BETA_TWO * second + (1 - BETA_TWO) * gradient * gradient
    ratio = first / (1 - BETA_ONE**STEP) / (jnp.sqrt(second / (1 - BETA_TWO**STEP)) + ADAM_EPS)
    weight = weight - rate * (ratio + WEIGHT_DECAY * weight)
    average = EMA_DECAY * average + (1 - EMA_DECAY) * weight
    return (weight, first, second, average)


def body(
    images,
    noises,
    order,
    time_index,
    io_weight,
    conv_weight,
    time_weight,
    attn_weight,
    norm_param,
    io_first,
    conv_first,
    time_first,
    attn_first,
    norm_first,
    io_second,
    conv_second,
    time_second,
    attn_second,
    norm_second,
    io_average,
    conv_average,
    time_average,
    attn_average,
    norm_average,
):
    rank = lax.axis_index("mp")
    io_all, conv, temb, attn, norms = (
        lax.all_gather(io_weight.astype(jnp.bfloat16), "dp", axis=0, tiled=True),
        lax.all_gather(conv_weight.astype(jnp.bfloat16), "dp", axis=2, tiled=True),
        lax.all_gather(time_weight.astype(jnp.bfloat16), "dp", axis=1, tiled=True),
        lax.all_gather(attn_weight.astype(jnp.bfloat16), "dp", axis=0, tiled=True),
        lax.all_gather(norm_param.astype(jnp.bfloat16), "dp", axis=0, tiled=True),
    )
    width = conv.shape[3]
    io_all = io_all.reshape(width, 2, SUB)
    norm_table = norms.astype(jnp.float32).reshape(width, 12)
    heads_here = width // HD
    scale_attn = HD ** (-0.5)
    whole_kernel = lax.all_gather(conv, "mp", axis=3, tiled=True)
    flip_kernel = lax.dynamic_slice_in_dim(whole_kernel, rank * width, width, 2)
    micro = noises.shape[0]
    count = noises.shape[1]
    depth = noises.shape[2]
    noise_all = lax.all_gather(noises, "dp", axis=1, tiled=True)
    batch_size = noise_all.shape[1]
    picked = jnp.take(images, order, axis=0).reshape(micro, count, depth)
    gram = jnp.einsum("mid,mjd->mij", picked, noise_all, preferred_element_type=jnp.float32)
    own_sq = jnp.einsum("mid,mid->mi", picked, picked, preferred_element_type=jnp.float32)
    far_sq = jnp.einsum("mjd,mjd->mj", noise_all, noise_all, preferred_element_type=jnp.float32)
    cost = (own_sq[:, :, None] + far_sq[:, None, :] - 2.0 * gram) / depth
    affinity = 2.0 * gram / (depth * SINK_EPS)
    kernel_mat = jnp.exp(affinity - jnp.max(affinity, axis=2, keepdims=True))
    share = 1.0 / batch_size

    def sweep(turn, carry):
        left, right = carry
        left = share / jnp.einsum("mij,mj->mi", kernel_mat, right, precision=HIGH)
        column = lax.psum(jnp.einsum("mi,mij->mj", left, kernel_mat, precision=HIGH), "dp")
        return (left, share / column)

    left, right = lax.fori_loop(
        0,
        SINK,
        sweep,
        (jnp.ones((micro, count), jnp.float32), jnp.ones((micro, batch_size), jnp.float32)),
    )
    scaled = kernel_mat * right[:, None, :]
    mixing = (scaled / jnp.sum(scaled, axis=2, keepdims=True)).astype(jnp.bfloat16)
    paired = jnp.einsum("mij,mjd->mid", mixing, noise_all, preferred_element_type=jnp.float32)
    plan_cost = jnp.sum(left[:, :, None] * scaled * cost, axis=(1, 2))
    times = ((time_index.astype(jnp.float32) + 0.5) / NT)[:, :, None]
    pixels = picked.astype(jnp.float32)
    inputs = ((1 - times) * paired + times * pixels).reshape(micro, count, SUB, -1)
    target = (pixels - paired).reshape(micro, count, SUB, -1)
    positions = target.shape[3] // lax.axis_size("mp")
    target = lax.dynamic_slice_in_dim(target, rank * positions, positions, 3)

    def gain_bias(slot):
        return (norm_table[:, 2 * slot], norm_table[:, 2 * slot + 1])

    def norm_back(field, slot, active, upstream):
        gain, bias = gain_bias(slot)
        unused, back = jax.vjp(partial(norm_act, active=active), field, gain, bias)
        return back(upstream)

    def input_grad(grads_low, place):
        return conv_transpose(
            lax.all_gather(grads_low, "mp", axis=1, tiled=True), flip_kernel[place]
        )

    def residual_forward(field, layer, slot, features):
        gain, bias = gain_bias(slot)
        first = gather_channels(norm_act(field, gain, bias, True).astype(jnp.bfloat16))
        added = jnp.dot(features, temb[layer], preferred_element_type=jnp.float32)
        mixed = conv_apply(first, conv[2 * layer]) + added[:, :, None]
        gain, bias = gain_bias(slot + 1)
        second = gather_channels(norm_act(mixed, gain, bias, True).astype(jnp.bfloat16))
        return (field + conv_apply(second, conv[2 * layer + 1]), (field, first, mixed, second))

    def residual_backward(back_flow, saved, layer, slot, features):
        field, first, mixed, second = saved
        late = back_flow.astype(jnp.bfloat16)
        late_kernel = conv_weight_grad(second, late)
        grad_second = input_grad(late, 2 * layer + 1)
        grad_mixed, gain_late, bias_late = norm_back(mixed, slot + 1, True, grad_second)
        early = grad_mixed.astype(jnp.bfloat16)
        time_grad = jnp.einsum("ni,nop->io", features, early, preferred_element_type=jnp.float32)
        early_kernel = conv_weight_grad(first, early)
        grad_first = input_grad(early, 2 * layer)
        grad_field, gain_early, bias_early = norm_back(field, slot, True, grad_first)
        return (
            back_flow + grad_field,
            [early_kernel, late_kernel],
            time_grad,
            [gain_early, bias_early, gain_late, bias_late],
        )

    proj = attn[:, :3].reshape(CH, 3, heads_here, HD)
    out_proj = attn[:, 3].reshape(CH, heads_here, HD)

    def attention_backward(back_flow, saved):
        field, normal, qkv, log_total, mixed = saved
        flow_all = gather_channels(back_flow.astype(jnp.bfloat16))
        out_grad = jnp.einsum("ncp,nhpd->chd", flow_all, mixed, preferred_element_type=jnp.float32)
        grad_mixed = jnp.einsum(
            "ncp,chd->nhpd", flow_all, out_proj, preferred_element_type=jnp.float32
        ).astype(jnp.bfloat16)
        scores = (
            jnp.einsum("nhpd,nhqd->nhpq", qkv[0], qkv[1], preferred_element_type=jnp.float32)
            * scale_attn
        )
        probs = jnp.exp(scores - log_total)
        grad_probs = jnp.einsum(
            "nhpd,nhqd->nhpq", grad_mixed, qkv[2], preferred_element_type=jnp.float32
        )
        grad_scores = (
            probs * (grad_probs - jnp.sum(probs * grad_probs, axis=3, keepdims=True))
        ).astype(jnp.bfloat16)
        grad_query = (
            jnp.einsum("nhpq,nhqd->nhpd", grad_scores, qkv[1], preferred_element_type=jnp.float32)
            * scale_attn
        )
        grad_key = (
            jnp.einsum("nhpq,nhpd->nhqd", grad_scores, qkv[0], preferred_element_type=jnp.float32)
            * scale_attn
        )
        grad_value = jnp.einsum(
            "nhpq,nhpd->nhqd",
            probs.astype(jnp.bfloat16),
            grad_mixed,
            preferred_element_type=jnp.float32,
        )
        grad_qkv = jnp.stack([grad_query, grad_key, grad_value]).astype(jnp.bfloat16)
        proj_grad = jnp.einsum(
            "ncp,jnhpd->cjhd", normal, grad_qkv, preferred_element_type=jnp.float32
        )
        grad_normal = sum_channels(
            jnp.einsum("jnhpd,cjhd->ncp", grad_qkv, proj, preferred_element_type=jnp.float32)
        )
        grad_field, gain_grad, bias_grad = norm_back(field, 2, False, grad_normal)
        weight_grad = jnp.concatenate([proj_grad.reshape(CH, 3, width), out_grad], axis=1)
        return (back_flow + grad_field, weight_grad, gain_grad, bias_grad)

    summed = None
    loss_terms = []
    for slot_micro in range(micro):
        features = time_features(time_index[slot_micro]).astype(jnp.bfloat16)
        start = inputs[slot_micro].astype(jnp.bfloat16)
        field = jnp.einsum("nkp,ck->ncp", start, io_all[:, 0], preferred_element_type=jnp.float32)
        field, saved_one = residual_forward(field, 0, 0, features)
        attention_gain, attention_bias = gain_bias(2)
        attention_normal = gather_channels(
            norm_act(field, attention_gain, attention_bias, False).astype(jnp.bfloat16)
        )
        attention_qkv = jnp.einsum(
            "ncp,cjhd->jnhpd", attention_normal, proj, preferred_element_type=jnp.float32
        ).astype(jnp.bfloat16)
        attention_scores = (
            jnp.einsum(
                "nhpd,nhqd->nhpq",
                attention_qkv[0],
                attention_qkv[1],
                preferred_element_type=jnp.float32,
            )
            * scale_attn
        )
        peak = jnp.max(attention_scores, axis=3, keepdims=True)
        expo = jnp.exp(attention_scores - peak)
        total = jnp.sum(expo, axis=3, keepdims=True)
        attention_probs = expo / total
        attention_mixed = jnp.einsum(
            "nhpq,nhqd->nhpd",
            attention_probs.astype(jnp.bfloat16),
            attention_qkv[2],
            preferred_element_type=jnp.float32,
        ).astype(jnp.bfloat16)
        branch = sum_channels(
            jnp.einsum(
                "nhpd,chd->ncp", attention_mixed, out_proj, preferred_element_type=jnp.float32
            )
        )
        field, saved_attn = (
            field + branch,
            (field, attention_normal, attention_qkv, peak + jnp.log(total), attention_mixed),
        )
        field, saved_two = residual_forward(field, 1, 3, features)
        gain, bias = gain_bias(5)
        last = norm_act(field, gain, bias, True).astype(jnp.bfloat16)
        partial_pred = jnp.einsum(
            "ncp,ck->nkp", last, io_all[:, 1], preferred_element_type=jnp.float32
        )
        pred = lax.psum_scatter(partial_pred, "mp", scatter_dimension=2, tiled=True)
        error = pred - target[slot_micro]
        loss_terms.append(jnp.sum(error * error))
        grad_pred = lax.all_gather(
            (error * (2.0 / (micro * batch_size))).astype(jnp.bfloat16), "mp", axis=2, tiled=True
        )
        out_grad = jnp.einsum("ncp,nkp->ck", last, grad_pred, preferred_element_type=jnp.float32)
        grad_last = jnp.einsum(
            "nkp,ck->ncp", grad_pred, io_all[:, 1], preferred_element_type=jnp.float32
        )
        back_flow, gain_final, bias_final = norm_back(field, 5, True, grad_last)
        back_flow, kernels_two, time_two, norms_two = residual_backward(
            back_flow, saved_two, 1, 3, features
        )
        back_flow, attn_grad, gain_attn, bias_attn = attention_backward(back_flow, saved_attn)
        back_flow, kernels_one, time_one, norms_one = residual_backward(
            back_flow, saved_one, 0, 0, features
        )
        in_grad = jnp.einsum(
            "nkp,ncp->ck", start, back_flow.astype(jnp.bfloat16), preferred_element_type=jnp.float32
        )
        columns = norms_one + [gain_attn, bias_attn] + norms_two + [gain_final, bias_final]
        parts = (
            jnp.stack([in_grad, out_grad], axis=1),
            jnp.stack(kernels_one + kernels_two),
            jnp.stack([time_one, time_two]),
            attn_grad,
            jnp.stack(columns, axis=1),
        )
        summed = parts if summed is None else jax.tree.map(jnp.add, summed, parts)
    reduced = (
        lax.psum_scatter(summed[0].reshape(-1), "dp", scatter_dimension=0, tiled=True),
        lax.psum_scatter(summed[1], "dp", scatter_dimension=2, tiled=True),
        lax.psum_scatter(summed[2], "dp", scatter_dimension=1, tiled=True),
        lax.psum_scatter(summed[3], "dp", scatter_dimension=0, tiled=True),
        lax.psum_scatter(summed[4].reshape(-1), "dp", scatter_dimension=0, tiled=True),
    )
    squares = sum((jnp.sum(part * part) for part in reduced))
    cost_term = jnp.where(rank == 0, plan_cost, jnp.zeros_like(plan_cost))
    total_sq, loss_sum, cost_sum = lax.psum(
        (squares, jnp.stack(loss_terms), cost_term), ("dp", "mp")
    )
    grad_norm = jnp.sqrt(total_sq)
    scale = CLIP_NORM / jnp.maximum(grad_norm, CLIP_NORM)
    weights = (io_weight, conv_weight, time_weight, attn_weight, norm_param)
    firsts = (io_first, conv_first, time_first, attn_first, norm_first)
    seconds = (io_second, conv_second, time_second, attn_second, norm_second)
    averages = (io_average, conv_average, time_average, attn_average, norm_average)
    results = [
        adam_update(
            weights[kind],
            firsts[kind],
            seconds[kind],
            averages[kind],
            reduced[kind] * scale,
            RATES[kind],
        )
        for kind in range(5)
    ]
    return (
        results[0][0],
        results[1][0],
        results[2][0],
        results[3][0],
        results[4][0],
        results[0][1],
        results[1][1],
        results[2][1],
        results[3][1],
        results[4][1],
        results[0][2],
        results[1][2],
        results[2][2],
        results[3][2],
        results[4][2],
        results[0][3],
        results[1][3],
        results[2][3],
        results[3][3],
        results[4][3],
        loss_sum,
        cost_sum,
        grad_norm,
    )


def solution(mesh):
    return jax.shard_map(
        body,
        mesh=mesh,
        in_specs=(
            P("dp", None),
            P(None, "dp", None),
            P("dp"),
            P(None, "dp"),
            P(("mp", "dp")),
            P(None, None, "dp", "mp"),
            P(None, "dp", "mp"),
            P("dp", None, "mp"),
            P(("mp", "dp")),
            P(("mp", "dp")),
            P(None, None, "dp", "mp"),
            P(None, "dp", "mp"),
            P("dp", None, "mp"),
            P(("mp", "dp")),
            P(("mp", "dp")),
            P(None, None, "dp", "mp"),
            P(None, "dp", "mp"),
            P("dp", None, "mp"),
            P(("mp", "dp")),
            P(("mp", "dp")),
            P(None, None, "dp", "mp"),
            P(None, "dp", "mp"),
            P("dp", None, "mp"),
            P(("mp", "dp")),
        ),
        out_specs=(
            P(("mp", "dp")),
            P(None, None, "dp", "mp"),
            P(None, "dp", "mp"),
            P("dp", None, "mp"),
            P(("mp", "dp")),
            P(("mp", "dp")),
            P(None, None, "dp", "mp"),
            P(None, "dp", "mp"),
            P("dp", None, "mp"),
            P(("mp", "dp")),
            P(("mp", "dp")),
            P(None, None, "dp", "mp"),
            P(None, "dp", "mp"),
            P("dp", None, "mp"),
            P(("mp", "dp")),
            P(("mp", "dp")),
            P(None, None, "dp", "mp"),
            P(None, "dp", "mp"),
            P("dp", None, "mp"),
            P(("mp", "dp")),
            P(),
            P(),
            P(),
        ),
        check_vma=False,
    )
```

profile of v0, /device:TPU:0, one launch (start us, length us, event | category | flops | bytes accessed | tf_op | source)
XLA Modules:
  0.0 1682.1 jit_solution(3039383807194452999)
XLA Ops:
  14.2 33.5 %all_gather.120 = bf16[3,16,3072]{2,0,1:T(4,128)(2,1)S(1)} all-gather(bf16[3,2,3072]{2,0,1:T(4,128)(2,1)S(1)} %copy.1451), channel_id=1, replica_groups=mesh['dp'=8,'mp'=4] {'dp'}, dimensions={1}, use_global_device_ids=true | all-gather | bytes 331776 | tf_op jit(solution)/shard_map/all_gather | solution.py:148
  51.0 21.7 %all-reduce.118 = (bf16[768]{0:T(1024)(128)(2,1)S(1)}, bf16[1536]{0:T(1024)(128)(2,1)S(1)}) all-reduce(bf16[768]{0:T(1024)(128)(2,1)S(1)} %dynamic-update-slice.1, bf16[1536]{0:T(1024)(128)(2,1)S(1)} %dynamic-update-slice), channel_id=1, replica_groups=mesh['dp'=8,'mp'=4] {'dp'}, use_global_device_ids=true, to_apply=%add.109 | all-reduce | flops 2304 | bytes 9216
  74.0 32.8 %all_gather.128 = bf16[256,4,64]{2,1,0:T(4,128)(2,1)} all-gather(bf16[32,4,64]{2,1,0:T(4,128)(2,1)S(1)} %convert_element_type.718), channel_id=1, replica_groups=mesh['dp'=8,'mp'=4] {'dp'}, dimensions={0}, use_global_device_ids=true | all-gather | bytes 147456 | tf_op jit(solution)/shard_map/all_gather | solution.py:135
  106.9 190.9 %while.14 = (s32[]{:T(128)}, f32[3,2]{1,0:T(4,128)}, f32[3,16]{1,0:T(4,128)S(1)}, f32[3,2,16]{2,1,0:T(2,128)S(1)}) while((s32[]{:T(128)}, f32[3,2]{1,0:T(4,128)}, f32[3,16]{1,0:T(4,128)S(1)}, f32[3,2,16]{2,1,0:T(2,128)S(1)}) %tuple.410), condition=%wide.region_3.4_spmd.clone.clone, body=%wide.region_1.3_spmd.clone.sunk.clone | while | flops 2463 | bytes 2895 | solution.py:165
  107.2 17.2 %psum.34 = f32[3,16]{1,0:T(4,128)S(1)} all-reduce(f32[3,16]{1,0:T(4,128)S(1)} %bitcast.1532), channel_id=1, replica_groups=mesh['dp'=8,'mp'=4] {'dp'}, use_global_device_ids=true, to_apply=%region_2.2 | all-reduce | flops 48 | bytes 384 | tf_op jit(solution)/shard_map/while/body/eval_jaxpr/psum | solution.py:162
  125.4 19.1 %psum.34 = f32[3,16]{1,0:T(4,128)S(1)} all-reduce(f32[3,16]{1,0:T(4,128)S(1)} %bitcast.1532), channel_id=1, replica_groups=mesh['dp'=8,'mp'=4] {'dp'}, use_global_device_ids=true, to_apply=%region_2.2 | all-reduce | flops 48 | bytes 384 | tf_op jit(solution)/shard_map/while/body/eval_jaxpr/psum | solution.py:162
  145.4 17.2 %psum.34 = f32[3,16]{1,0:T(4,128)S(1)} all-reduce(f32[3,16]{1,0:T(4,128)S(1)} %bitcast.1532), channel_id=1, replica_groups=mesh['dp'=8,'mp'=4] {'dp'}, use_global_device_ids=true, to_apply=%region_2.2 | all-reduce | flops 48 | bytes 384 | tf_op jit(solution)/shard_map/while/body/eval_jaxpr/psum | solution.py:162
  163.6 19.1 %psum.34 = f32[3,16]{1,0:T(4,128)S(1)} all-reduce(f32[3,16]{1,0:T(4,128)S(1)} %bitcast.1532), channel_id=1, replica_groups=mesh['dp'=8,'mp'=4] {'dp'}, use_global_device_ids=true, to_apply=%region_2.2 | all-reduce | flops 48 | bytes 384 | tf_op jit(solution)/shard_map/while/body/eval_jaxpr/psum | solution.py:162
  183.6 17.2 %psum.34 = f32[3,16]{1,0:T(4,128)S(1)} all-reduce(f32[3,16]{1,0:T(4,128)S(1)} %bitcast.1532), channel_id=1, replica_groups=mesh['dp'=8,'mp'=4] {'dp'}, use_global_device_ids=true, to_apply=%region_2.2 | all-reduce | flops 48 | bytes 384 | tf_op jit(solution)/shard_map/while/body/eval_jaxpr/psum | solution.py:162
  201.7 19.1 %psum.34 = f32[3,16]{1,0:T(4,128)S(1)} all-reduce(f32[3,16]{1,0:T(4,128)S(1)} %bitcast.1532), channel_id=1, replica_groups=mesh['dp'=8,'mp'=4] {'dp'}, use_global_device_ids=true, to_apply=%region_2.2 | all-reduce | flops 48 | bytes 384 | tf_op jit(solution)/shard_map/while/body/eval_jaxpr/psum | solution.py:162
  221.8 17.1 %psum.34 = f32[3,16]{1,0:T(4,128)S(1)} all-reduce(f32[3,16]{1,0:T(4,128)S(1)} %bitcast.1532), channel_id=1, replica_groups=mesh['dp'=8,'mp'=4] {'dp'}, use_global_device_ids=true, to_apply=%region_2.2 | all-reduce | flops 48 | bytes 384 | tf_op jit(solution)/shard_map/while/body/eval_jaxpr/psum | solution.py:162
  239.9 19.1 %psum.34 = f32[3,16]{1,0:T(4,128)S(1)} all-reduce(f32[3,16]{1,0:T(4,128)S(1)} %bitcast.1532), channel_id=1, replica_groups=mesh['dp'=8,'mp'=4] {'dp'}, use_global_device_ids=true, to_apply=%region_2.2 | all-reduce | flops 48 | bytes 384 | tf_op jit(solution)/shard_map/while/body/eval_jaxpr/psum | solution.py:162
  260.0 17.1 %psum.34 = f32[3,16]{1,0:T(4,128)S(1)} all-reduce(f32[3,16]{1,0:T(4,128)S(1)} %bitcast.1532), channel_id=1, replica_groups=mesh['dp'=8,'mp'=4] {'dp'}, use_global_device_ids=true, to_apply=%region_2.2 | all-reduce | flops 48 | bytes 384 | tf_op jit(solution)/shard_map/while/body/eval_jaxpr/psum | solution.py:162
  278.1 19.1 %psum.34 = f32[3,16]{1,0:T(4,128)S(1)} all-reduce(f32[3,16]{1,0:T(4,128)S(1)} %bitcast.1532), channel_id=1, replica_groups=mesh['dp'=8,'mp'=4] {'dp'}, use_global_device_ids=true, to_apply=%region_2.2 | all-reduce | flops 48 | bytes 384 | tf_op jit(solution)/shard_map/while/body/eval_jaxpr/psum | solution.py:162
  305.6 5.8 all_gather.149
  311.4 5.9 all_gather.123
  317.3 5.9 all_gather.138
  360.3 32.8 %all_gather.125 = bf16[2,256,64]{2,1,0:T(8,128)(2,1)} all-gather(bf16[2,32,64]{2,1,0:T(8,128)(2,1)S(1)} %convert_element_type.715), channel_id=1, replica_groups=mesh['dp'=8,'mp'=4] {'dp'}, dimensions={1}, use_global_device_ids=true | all-gather | bytes 73728 | tf_op jit(solution)/shard_map/all_gather | solution.py:134
  409.0 9.2 fusion.405
  428.0 5.8 all_gather.150
  433.8 5.8 all_gather.126
  439.6 5.8 all_gather.139
  491.5 5.9 all_gather.151
  497.3 5.8 all_gather.140
  503.2 5.8 all_gather.127
  521.0 7.5 reduce-scatter.16.cloned.1.call-done
  530.7 21.1 %reduce-scatter.20.cloned.1.call-done = bf16[2,64,256]{2,1,0:T(8,128)(2,1)} async-done(((bf16[2,256,256]{2,1,0:T(8,128)(2,1)}), bf16[2,64,256]{2,1,0:T(8,128)(2,1)}) %reduce-scatter.20.cloned.1.call-update) | async-done | bytes 65552 | tf_op jit(solution)/shard_map/reduce_scatter | solution.py:90
  553.6 21.2 %reduce-scatter.24.cloned.1.call-done = bf16[2,64,256]{2,1,0:T(8,128)(2,1)} async-done(((bf16[2,256,256]{2,1,0:T(8,128)(2,1)}), bf16[2,64,256]{2,1,0:T(8,128)(2,1)}) %reduce-scatter.24.cloned.1.call-update) | async-done | bytes 65552 | tf_op jit(solution)/shard_map/reduce_scatter | solution.py:90
  578.0 6.3 all_gather.152
  584.3 5.9 all_gather.129
  590.1 5.8 all_gather.141
  615.7 3.9 pad_slice_fusion.72
  675.1 5.9 all_gather.153
  681.0 5.8 all_gather.130
  686.9 6.0 all_gather.142
  780.5 5.1 reduce-scatter.30.cloned.1.call-done
  786.5 21.5 %reduce-scatter.28.cloned.1.call-done = f32[64,24]{1,0:T(8,128)} async-done(((f32[256,24]{1,0:T(8,128)}), f32[64,24]{1,0:T(8,128)}) %reduce-scatter.28.cloned.1.call-update) | async-done | bytes 6160
  808.9 21.2 %reduce-scatter.32.cloned.1.call-done = f32[64,24]{1,0:T(8,128)} async-done(((f32[256,24]{1,0:T(8,128)}), f32[64,24]{1,0:T(8,128)}) %reduce-scatter.32.cloned.1.call-update) | async-done | bytes 6160
  832.2 5.4 all_gather.131
  837.8 5.5 all_gather.154
  843.3 6.2 all_gather.143
  885.4 6.5 all_gather.155
  892.8 6.3 all_gather.133
  900.2 6.7 all_gather.144
  919.7 10.9 constant_dynamic-slice_fusion.1
  1031.5 5.9 all_gather.145
  1042.3 5.8 all_gather.134
  1048.2 5.8 all_gather.156
  1117.3 5.8 all_gather.135
  1125.0 5.9 all_gather.157
  1131.9 5.9 all_gather.146
  1166.4 7.3 reduce-scatter.22.cloned.1.call-done
  1173.7 23.1 %reduce-scatter.26.cloned.1.call-done = bf16[2,64,256]{2,1,0:T(8,128)(2,1)} async-done(((bf16[2,256,256]{2,1,0:T(8,128)(2,1)}), bf16[2,64,256]{2,1,0:T(8,128)(2,1)}) %reduce-scatter.26.cloned.1.call-update) | async-done | bytes 65552 | tf_op jit(solution)/shard_map/reduce_scatter | solution.py:90
  1201.7 17.7 %reduce-scatter.18.cloned.1.call-done = bf16[2,64,256]{2,1,0:T(8,128)(2,1)} async-done(((bf16[2,256,256]{2,1,0:T(8,128)(2,1)}), bf16[2,64,256]{2,1,0:T(8,128)(2,1)}) %reduce-scatter.18.cloned.1.call-update) | async-done | bytes 65552 | tf_op jit(solution)/shard_map/reduce_scatter | solution.py:90
  1226.5 5.9 all_gather.136
  1234.1 6.0 all_gather.158
  1241.7 5.9 all_gather.147
  1331.4 6.2 all_gather.137
  1339.4 6.5 all_gather.159
  1347.6 5.9 all_gather.148
  1420.0 4.1 copy.1757
  1440.0 39.3 %all-reduce.116 = (f32[1536]{0:T(1024)S(1)}, f32[768]{0:T(1024)S(1)}) all-reduce(f32[1536]{0:T(1024)S(1)} %add.1622, f32[768]{0:T(1024)S(1)} %add.1634), channel_id=11, replica_groups=mesh['dp'=8,'mp'=4] {'dp'}, use_global_device_ids=true, to_apply=%region_167.168.clone | all-reduce | flops 2304 | bytes 18432
  1480.6 135.8 %all-reduce.121.cloned.1.call-done = (f32[4,9,256,64]{3,0,1,2:T(4,128)}, f32[2,256,64]{2,0,1:T(2,128)}, f32[256,4,64]{2,1,0:T(4,128)}) async-done(((f32[4,9,256,64]{3,0,1,2:T(4,128)}, f32[2,256,64]{2,0,1:T(2,128)}, f32[256,4,64]{2,1,0:T(4,128)}), (f32[4,9,256,64]{3,0,1,2:T(4,128)}, f32[2,256,64]{2,0,1:T(2,128)}, f32[256,4,64]{2,1,0:T(4,128)})) %all-reduce.121.cloned.1.call-update) | async-done | bytes 2752528
  1624.5 39.6 %all-reduce.115 = (f32[]{:T(128)}, f32[3]{0:T(128)}, f32[3]{0:T(128)}) all-reduce(f32[]{:T(128)S(6)} %add.1635, f32[3]{0:T(128)} %get-tuple-element.675, f32[3]{0:T(128)} %get-tuple-element.674), channel_id=1, replica_groups=mesh['dp'=8,'mp'=4] {'dp','mp'}, use_global_device_ids=true, to_apply=%region_219.220 | all-reduce | flops 7 | bytes 56 | tf_op jit(solution)/shard_map/psum | solution.py:355
  (1948 shorter events, 765.2 us)
Async XLA Ops:
  7.2 41.4 %copy-start.383 = (u32[32]{0:T(128)S(1)}, u32[32]{0:T(128)}, u32[]{:S(2)}) copy-start(u32[32]{0:T(128)} %constant.462) | copy-start | bytes 388
  7.2 43.2 %copy-start.384 = (f32[192]{0:T(256)S(1)}, f32[192]{0:T(256)}, u32[]{:S(2)}) copy-start(f32[192]{0:T(256)} %param.30) | copy-start | bytes 2308
  7.2 43.2 %copy-start.385 = (f32[96]{0:T(128)S(1)}, f32[96]{0:T(128)}, u32[]{:S(2)}) copy-start(f32[96]{0:T(128)} %param.34) | copy-start | bytes 1156
  7.2 43.3 %copy-start.186 = (f32[2,32,64]{2,1,0:T(8,128)S(1)}, f32[2,32,64]{2,1,0:T(8,128)}, u32[]{:S(2)}) copy-start(f32[2,32,64]{2,1,0:T(8,128)} %param.32) | copy-start | bytes 49156
  7.3 66.6 %copy-start.170 = (f32[32,4,64]{2,1,0:T(4,128)S(1)}, f32[32,4,64]{2,1,0:T(4,128)}, u32[]{:S(2)}) copy-start(f32[32,4,64]{2,1,0:T(4,128)} %param.33) | copy-start | bytes 98308
  7.3 401.7 %all-gather.3.cloned.1.call-start = ((), (), s32[]{:S(2)}) async-start(), calls=%async_computation.9 | async-start | bytes 2654208 | tf_op jit(solution)/shard_map/all_gather | solution.py:133
  9.5 519.0 %reduce-scatter.16.cloned.1.call-start = ((), (), s32[]{:S(2)}) async-start(), calls=%async_computation.10 | async-start | bytes 327680 | tf_op jit(solution)/shard_map/reduce_scatter | solution.py:90
  12.8 287.8 %copy-start.380 = (pred[3,2]{1,0:T(4,128)(4,1)}, pred[3,2]{1,0:T(4,128)(4,1)S(1)}, u32[]{:S(2)}) copy-start(pred[3,2]{1,0:T(4,128)(4,1)S(1)} %broadcast_in_dim.369) | copy-start | bytes 22
  13.4 289.4 %copy-start.169 = (bf16[3,2,3072]{2,1,0:T(2,128)(2,1)}, bf16[3,2,3072]{2,1,0:T(2,128)(2,1)S(1)}, u32[]{:S(2)}) copy-start(bf16[3,2,3072]{2,1,0:T(2,128)(2,1)S(1)} %gather.7) | copy-start | bytes 110596
  73.7 237.8 %copy-start.296 = (f32[64]{0:T(128)}, f32[64]{0:T(128)S(1)}, u32[]{:S(2)}) copy-start(f32[64]{0:T(128)S(1)} %get-tuple-element.258) | copy-start | bytes 772
  73.7 249.6 %copy-start.265 = (f32[64]{0:T(128)}, f32[64]{0:T(128)S(1)}, u32[]{:S(2)}) copy-start(f32[64]{0:T(128)S(1)} %get-tuple-element.259) | copy-start | bytes 772
  73.7 354.0 %copy-start.231 = (f32[64]{0:T(128)}, f32[64]{0:T(128)S(1)}, u32[]{:S(2)}) copy-start(f32[64]{0:T(128)S(1)} %get-tuple-element.257) | copy-start | bytes 772
  73.7 354.0 %copy-start.298 = (f32[64]{0:T(128)}, f32[64]{0:T(128)S(1)}, u32[]{:S(2)}) copy-start(f32[64]{0:T(128)S(1)} %get-tuple-element.256) | copy-start | bytes 772
  73.7 417.5 %copy-start.262 = (f32[64]{0:T(128)}, f32[64]{0:T(128)S(1)}, u32[]{:S(2)}) copy-start(f32[64]{0:T(128)S(1)} %get-tuple-element.255) | copy-start | bytes 772
  300.6 183.7 %copy-start.60 = (f32[2,64,256]{2,1,0:T(8,128)}, f32[2,64,256]{2,1,0:T(8,128)S(1)}, u32[]{:S(2)}) copy-start(f32[2,64,256]{2,1,0:T(8,128)S(1)} %get-tuple-element.634) | copy-start | bytes 393220
  302.3 177.2 %copy-start.62 = (f32[2,64,256]{2,1,0:T(8,128)}, f32[2,64,256]{2,1,0:T(8,128)S(1)}, u32[]{:S(2)}) copy-start(f32[2,64,256]{2,1,0:T(8,128)S(1)} %get-tuple-element.636) | copy-start | bytes 393220
  304.0 183.6 %copy-start.64 = (f32[2,64,256]{2,1,0:T(8,128)}, f32[2,64,256]{2,1,0:T(8,128)S(1)}, u32[]{:S(2)}) copy-start(f32[2,64,256]{2,1,0:T(8,128)S(1)} %get-tuple-element.632) | copy-start | bytes 393220
  355.7 37.4 %copy-start.72 = (bf16[256,4,64]{2,1,0:T(4,128)(2,1)S(1)}, bf16[256,4,64]{2,1,0:T(4,128)(2,1)}, u32[]{:S(2)}) copy-start(bf16[256,4,64]{2,1,0:T(4,128)(2,1)} %all_gather.128) | copy-start | bytes 393220
  357.3 63.8 %copy-start.5 = (bf16[2,9,256,256]{3,2,0,1:T(8,128)(2,1)}, bf16[2,9,256,256]{3,2,0,1:T(8,128)(2,1)S(1)}, u32[]{:S(2)}) copy-start(bf16[2,9,256,256]{3,2,0,1:T(8,128)(2,1)S(1)} %constant_dynamic-update-slice_fusion.32) | copy-start | bytes 7077892
  357.3 41.6 %copy-start.86 = (bf16[2,256,16,16]{1,3,2,0:T(8,128)(2,1)S(1)}, bf16[2,256,16,16]{1,3,2,0:T(8,128)(2,1)}, u32[]{:S(2)}) copy-start(bf16[2,256,16,16]{1,3,2,0:T(8,128)(2,1)} %get-tuple-element.483) | copy-start | bytes 786436
  393.1 376.4 %copy-start.193 = (bf16[64,1,12]{0,2,1:T(8,128)(2,1)}, bf16[64,1,12]{0,2,1:T(8,128)(2,1)S(1)}, u32[]{:S(2)}) copy-start(bf16[64,1,12]{0,2,1:T(8,128)(2,1)S(1)} %copy.1837) | copy-start | bytes 4612
  481.6 70.2 %copy-start.27 = (f32[2,64,256]{2,1,0:T(8,128)}, f32[2,64,256]{2,1,0:T(8,128)S(1)}, u32[]{:S(2)}) copy-start(f32[2,64,256]{2,1,0:T(8,128)S(1)} %get-tuple-element.646) | copy-start | bytes 393220
  486.3 42.2 %copy-start.29 = (f32[2,64,256]{2,1,0:T(8,128)}, f32[2,64,256]{2,1,0:T(8,128)S(1)}, u32[]{:S(2)}) copy-start(f32[2,64,256]{2,1,0:T(8,128)S(1)} %get-tuple-element.648) | copy-start | bytes 393220
  489.8 85.0 %copy-start.31 = (f32[2,64,256]{2,1,0:T(8,128)}, f32[2,64,256]{2,1,0:T(8,128)S(1)}, u32[]{:S(2)}) copy-start(f32[2,64,256]{2,1,0:T(8,128)S(1)} %get-tuple-element.644) | copy-start | bytes 393220
  511.2 40.6 %reduce-scatter.20.cloned.1.call-start = ((), (), s32[]{:S(2)}) async-start(), calls=%async_computation.13 | async-start | bytes 327680 | tf_op jit(solution)/shard_map/reduce_scatter | solution.py:90
  514.5 60.3 %reduce-scatter.24.cloned.1.call-start = ((), (), s32[]{:S(2)}) async-start(), calls=%async_computation.15 | async-start | bytes 327680 | tf_op jit(solution)/shard_map/reduce_scatter | solution.py:90
  520.9 264.6 %reduce-scatter.30.cloned.1.call-start = ((), (), s32[]{:S(2)}) async-start(), calls=%async_computation.18 | async-start | bytes 163840
  529.5 220.4 %copy-start.37 = (f32[2,64,256]{2,1,0:T(8,128)}, f32[2,64,256]{2,1,0:T(8,128)S(1)}, u32[]{:S(2)}) copy-start(f32[2,64,256]{2,1,0:T(8,128)S(1)} %get-tuple-element.348) | copy-start | bytes 393220
  529.8 71.6 %copy-start.219 = (f32[2,64]{1,0:T(2,128)}, f32[2,64]{1,0:T(2,128)S(1)}, u32[]{:S(2)}) copy-start(f32[2,64]{1,0:T(2,128)S(1)} %sub.565) | copy-start | bytes 1540
  530.7 53.6 %copy-start.250 = (f32[2,64]{1,0:T(2,128)}, f32[2,64]{1,0:T(2,128)S(1)}, u32[]{:S(2)}) copy-start(f32[2,64]{1,0:T(2,128)S(1)} %mul.1959) | copy-start | bytes 1540
  552.7 189.1 %copy-start.33 = (f32[2,64,256]{2,1,0:T(8,128)}, f32[2,64,256]{2,1,0:T(8,128)S(1)}, u32[]{:S(2)}) copy-start(f32[2,64,256]{2,1,0:T(8,128)S(1)} %get-tuple-element.338) | copy-start | bytes 393220
  553.1 48.3 %copy-start.229 = (f32[2,64]{1,0:T(2,128)}, f32[2,64]{1,0:T(2,128)S(1)}, u32[]{:S(2)}) copy-start(f32[2,64]{1,0:T(2,128)S(1)} %sub.602) | copy-start | bytes 1540
  575.7 180.3 %copy-start.35 = (f32[2,64,256]{2,1,0:T(8,128)}, f32[2,64,256]{2,1,0:T(8,128)S(1)}, u32[]{:S(2)}) copy-start(f32[2,64,256]{2,1,0:T(8,128)S(1)} %get-tuple-element.328) | copy-start | bytes 393220
  765.8 42.2 %reduce-scatter.28.cloned.1.call-start = ((), (), s32[]{:S(2)}) async-start(), calls=%async_computation.17 | async-start | bytes 163840
  769.5 60.7 %reduce-scatter.32.cloned.1.call-start = ((), (), s32[]{:S(2)}) async-start(), calls=%async_computation.19 | async-start | bytes 163840
  773.2 146.5 %all-gather.5.cloned.1.call-start = ((), (), s32[]{:S(2)}) async-start(), calls=%async_computation.11 | async-start | bytes 5898240 | tf_op jit(solution)/shard_map/all_gather | solution.py:143
  777.2 72.4 %copy-start.69 = (f32[2,64,256]{2,1,0:T(8,128)S(1)}, f32[2,64,256]{2,1,0:T(8,128)}, u32[]{:S(2)}) copy-start(f32[2,64,256]{2,1,0:T(8,128)} %copy-done.68) | copy-start | bytes 393220
  777.2 72.4 %copy-start.194 = (bf16[64,1,12]{0,2,1:T(8,128)(2,1)S(1)}, bf16[64,1,12]{0,2,1:T(8,128)(2,1)}, u32[]{:S(2)}) copy-start(bf16[64,1,12]{0,2,1:T(8,128)(2,1)} %copy-done.193) | copy-start | bytes 4612
  777.2 72.4 %copy-start.292 = (f32[2,64]{1,0:T(2,128)S(1)}, f32[2,64]{1,0:T(2,128)}, u32[]{:S(2)}) copy-start(f32[2,64]{1,0:T(2,128)} %copy-done.291) | copy-start | bytes 1540
  777.2 72.5 %copy-start.339 = (f32[2,64]{1,0:T(2,128)S(1)}, f32[2,64]{1,0:T(2,128)}, u32[]{:S(2)}) copy-start(f32[2,64]{1,0:T(2,128)} %copy-done.338) | copy-start | bytes 1540
  777.2 73.4 %copy-start.71 = (f32[2,64,256]{2,1,0:T(8,128)S(1)}, f32[2,64,256]{2,1,0:T(8,128)}, u32[]{:S(2)}) copy-start(f32[2,64,256]{2,1,0:T(8,128)} %copy-done.70) | copy-start | bytes 393220
  777.2 73.4 %copy-start.294 = (f32[2,64]{1,0:T(2,128)S(1)}, f32[2,64]{1,0:T(2,128)}, u32[]{:S(2)}) copy-start(f32[2,64]{1,0:T(2,128)} %copy-done.293) | copy-start | bytes 1540
  777.2 73.4 %copy-start.341 = (f32[2,64]{1,0:T(2,128)S(1)}, f32[2,64]{1,0:T(2,128)}, u32[]{:S(2)}) copy-start(f32[2,64]{1,0:T(2,128)} %copy-done.340) | copy-start | bytes 1540
  777.3 396.4 %reduce-scatter.22.cloned.1.call-start = ((), (), s32[]{:S(2)}) async-start(), calls=%async_computation.14 | async-start | bytes 327680 | tf_op jit(solution)/shard_map/reduce_scatter | solution.py:90
  851.6 63.1 %copy-start.22 = (bf16[2,9,256,256]{3,2,0,1:T(8,128)(2,1)S(1)}, bf16[2,9,256,256]{3,2,0,1:T(8,128)(2,1)}, u32[]{:S(2)}) copy-start(bf16[2,9,256,256]{3,2,0,1:T(8,128)(2,1)} %copy-done.21) | copy-start | bytes 7077892
  933.0 74.9 %copy-start.44 = (f32[2,9,64,256]{3,2,0,1:T(8,128)}, f32[2,9,64,256]{3,2,0,1:T(8,128)S(1)}, u32[]{:S(2)}) copy-start(f32[2,9,64,256]{3,2,0,1:T(8,128)S(1)} %convolution_bitcast_fusion.7) | copy-start | bytes 3538948
  1153.5 43.3 %reduce-scatter.26.cloned.1.call-start = ((), (), s32[]{:S(2)}) async-start(), calls=%async_computation.16 | async-start | bytes 327680 | tf_op jit(solution)/shard_map/reduce_scatter | solution.py:90
  1162.5 56.8 %copy-start.30 = (f32[2,64,256]{2,1,0:T(8,128)S(1)}, f32[2,64,256]{2,1,0:T(8,128)}, u32[]{:S(2)}) copy-start(f32[2,64,256]{2,1,0:T(8,128)} %copy-done.29) | copy-start | bytes 393220
  1162.6 56.8 %copy-start.161 = (f32[2,64,256]{2,1,0:T(8,128)S(1)}, f32[2,64,256]{2,1,0:T(8,128)}, u32[]{:S(2)}) copy-start(f32[2,64,256]{2,1,0:T(8,128)} %get-tuple-element.606) | copy-start | bytes 393220
  1162.6 56.8 %copy-start.209 = (f32[2,64]{1,0:T(2,128)S(1)}, f32[2,64]{1,0:T(2,128)}, u32[]{:S(2)}) copy-start(f32[2,64]{1,0:T(2,128)} %copy-done.208) | copy-start | bytes 1540
  1162.6 56.8 %reduce-scatter.18.cloned.1.call-start = ((), (), s32[]{:S(2)}) async-start(), calls=%async_computation.12 | async-start | bytes 327680 | tf_op jit(solution)/shard_map/reduce_scatter | solution.py:90
  1164.6 56.8 %copy-start.322 = (f32[2,8]{1,0:T(2,128)S(1)}, f32[2,8]{1,0:T(2,128)}, u32[]{:S(2)}) copy-start(f32[2,8]{1,0:T(2,128)} %copy-done.321) | copy-start | bytes 196
  1164.6 57.0 %copy-start.278 = (f32[2,64]{1,0:T(2,128)S(1)}, f32[2,64]{1,0:T(2,128)}, u32[]{:S(2)}) copy-start(f32[2,64]{1,0:T(2,128)} %copy-done.277) | copy-start | bytes 1540
  1164.6 59.0 %copy-start.164 = (f32[2,64,256]{2,1,0:T(8,128)S(1)}, f32[2,64,256]{2,1,0:T(8,128)}, u32[]{:S(2)}) copy-start(f32[2,64,256]{2,1,0:T(8,128)} %get-tuple-element.342) | copy-start | bytes 393220
  1166.3 58.5 %copy-start.18 = (bf16[2,9,256,256]{3,2,0,1:T(8,128)(2,1)S(1)}, bf16[2,9,256,256]{3,2,0,1:T(8,128)(2,1)}, u32[]{:S(2)}) copy-start(bf16[2,9,256,256]{3,2,0,1:T(8,128)(2,1)} %copy-done.17) | copy-start | bytes 7077892
  1166.3 450.0 %all-reduce.121.cloned.1.call-start = ((), (), s32[]{:S(2)}) async-start(), calls=%async_computation.20 | async-start | bytes 11010048
  1355.3 59.4 %copy-start.43 = (f32[2,9,64,256]{3,2,0,1:T(8,128)}, f32[2,9,64,256]{3,2,0,1:T(8,128)S(1)}, u32[]{:S(2)}) copy-start(f32[2,9,64,256]{3,2,0,1:T(8,128)S(1)} %convolution_bitcast_fusion.4) | copy-start | bytes 3538948
  1430.6 234.2 %copy-start.171 = (f32[32,4,64]{2,1,0:T(4,128)S(1)}, f32[32,4,64]{2,1,0:T(4,128)}, u32[]{:S(2)}) copy-start(f32[32,4,64]{2,1,0:T(4,128)} %param.33) | copy-start | bytes 98308
  1430.6 234.2 %copy-start.189 = (f32[32,4,64]{2,1,0:T(4,128)S(1)}, f32[32,4,64]{2,1,0:T(4,128)}, u32[]{:S(2)}) copy-start(f32[32,4,64]{2,1,0:T(4,128)} %param.48) | copy-start | bytes 98308
  1430.6 234.2 %copy-start.190 = (f32[32,4,64]{2,1,0:T(4,128)S(1)}, f32[32,4,64]{2,1,0:T(4,128)}, u32[]{:S(2)}) copy-start(f32[32,4,64]{2,1,0:T(4,128)} %param.38) | copy-start | bytes 98308
  1430.6 234.2 %copy-start.191 = (f32[32,4,64]{2,1,0:T(4,128)S(1)}, f32[32,4,64]{2,1,0:T(4,128)}, u32[]{:S(2)}) copy-start(f32[32,4,64]{2,1,0:T(4,128)} %param.43) | copy-start | bytes 98308
  1431.4 237.7 %copy-start.187 = (f32[2,32,64]{2,1,0:T(8,128)S(1)}, f32[2,32,64]{2,1,0:T(8,128)}, u32[]{:S(2)}) copy-start(f32[2,32,64]{2,1,0:T(8,128)} %param.32) | copy-start | bytes 49156
  1436.5 234.1 %copy-start.67 = (f32[4,9,32,64]{3,2,1,0:T(8,128)S(1)}, f32[4,9,32,64]{3,2,1,0:T(8,128)}, u32[]{:S(2)}) copy-start(f32[4,9,32,64]{3,2,1,0:T(8,128)} %param.31) | copy-start | bytes 884740
  1436.5 234.1 %copy-start.154 = (f32[4,9,32,64]{3,2,1,0:T(8,128)S(1)}, f32[4,9,32,64]{3,2,1,0:T(8,128)}, u32[]{:S(2)}) copy-start(f32[4,9,32,64]{3,2,1,0:T(8,128)} %param.46) | copy-start | bytes 884740
  (334 other events, 3228.3 us)
Sparse Core Ops, SparseCore 0:
  10.9 56.5 all-gather.2
  511.3 17.2 reduce-scatter.15
  531.7 20.0 reduce-scatter.19
  554.7 20.0 reduce-scatter.23
  765.9 19.6 reduce-scatter.29
  788.4 19.5 reduce-scatter.27
  810.5 19.5 reduce-scatter.31
  831.7 38.1 all-gather.4
  1153.6 20.0 reduce-scatter.21
  1176.7 20.0 reduce-scatter.25
  1199.3 20.0 reduce-scatter.17
  1424.2 192.0 all-reduce.120
where the time goes:
time: 1700 us; the launch traced here: 1680 us
  blocking collectives  578 us (34%)
  local copies, waits for them, and re-layouts  560 us (33%)
  waiting for transfers between devices  282 us (17%)
  other arithmetic  141 us (8%)
  matrix products  90.7 us (5%)
  between operations  29.1 us (2%)
    unnamed x16, waiting for transfers between devices  184 us
    psum x10, blocking collectives, sweep(): lax.psum(jnp.einsum('mi,mij->mj', left, kernel_mat, precision=HIGH), 'dp')  181 us
    another operation x108, local copies, waits for them, and re-layouts, stacked_shifts(): jnp.stack([shifted(inputs, row_off, col_off) for row_off, col_off in OFFS...  128 us
    unnamed x900, local copies, waits for them, and re-layouts  110 us
    slice x108, local copies, waits for them, and re-layouts, conv_transpose(): total = total + shifted(terms[:, place], -row_off, -col_off)  108 us
    all_gather x18, blocking collectives, gather_channels(): return lax.all_gather(field, 'mp', axis=1, tiled=True)  106 us
    reduce_scatter x6, waiting for transfers between devices, sum_channels(): lax.psum_scatter(field.astype(jnp.bfloat16), 'mp', scatter_dimension=1, t...  97.9 us
    all_gather x12, blocking collectives, input_grad(): lax.all_gather(grads_low, 'mp', axis=1, tiled=True)  73.5 us
  transfers between devices with their start and end apart: 12, of which 10 were waited for; matrix products, arithmetic and copies ran while one was open for 11% of the time, Pallas kernels for 0%

commit v1 on v0

v1 whole, which is shorter than its diff:
```python
from functools import partial
import math

import jax
import jax.numpy as jnp
from jax import lax
from jax.experimental import pallas as pl
from jax.experimental.pallas import tpu as pltpu
from jax.sharding import PartitionSpec as P

CH = 256
GROUPS = 32
HEADS = 4
HD = 64
SUB = 12
POS = 256
SIDE = 16
SINK = 10
NT = 1000
STEP = 5
MATS = 42
TIME_AT = 36
ATTN_AT = 38


EPS_NORM = 1e-05
SINK_EPS = 0.01
CLIP_NORM = 1.0
BETA_ONE = 0.5
BETA_TWO = 0.5
ADAM_EPS = 1e-08
WEIGHT_DECAY = 0.01
EMA_DECAY = 0.9
RATES = (0.06, 0.01, 0.03, 0.03, 0.3)
F32 = jnp.float32
BF16 = jnp.bfloat16
ROWS = 32
PAD = SIDE
IMGS = 2
SPOTS = IMGS * POS


def dot(a, b, ca=1, cb=0):
    return lax.dot_general(a, b, (((ca,), (cb,)), ((), ())), preferred_element_type=F32)


def split3(v):
    one = v.astype(BF16)
    rest = v - one.astype(F32)
    two = rest.astype(BF16)
    three = (rest - two.astype(F32)).astype(BF16)
    return one, two, three


def group_sum(v):
    per = CH // GROUPS
    rows = lax.broadcasted_iota(jnp.int32, (CH, CH), 0) // per
    cols = lax.broadcasted_iota(jnp.int32, (CH, CH), 1) // per
    ones = jnp.where(rows == cols, 1.0, 0.0).astype(BF16)
    one, two, three = split3(v)
    got = dot(jnp.concatenate([one.astype(F32), two.astype(F32), three.astype(F32)], axis=0).astype(BF16), ones)
    n = v.shape[0]
    return got[:n] + got[n : 2 * n] + got[2 * n :]


def rows8(*rows):
    return jnp.concatenate(list(rows) + [jnp.zeros((8 - len(rows), CH), F32)], axis=0)


def for_blocks(step, init):
    return lax.fori_loop(0, POS // ROWS, lambda i, c: step(pl.multiple_of(i * ROWS, ROWS), c), init, unroll=2)


def norm_stats(field, stats, slot):
    zero = jnp.zeros((8, CH), F32)

    def fold(v):
        return v.reshape(ROWS // 8, 8, CH).sum(axis=0)

    sums = []
    for n in range(IMGS):
        acc = for_blocks(lambda at, c: c + fold(field[pl.ds(n * POS + at, ROWS), :]), zero)
        sums.append(jnp.sum(acc, axis=0, keepdims=True))
    scale = 1.0 / (POS * (CH // GROUPS))
    means = group_sum(rows8(*sums)) * scale
    sums = []
    for n in range(IMGS):
        mean = means[n : n + 1]

        def step(at, c):
            d = field[pl.ds(n * POS + at, ROWS), :] - mean
            return c + fold(d * d)

        sums.append(jnp.sum(for_blocks(step, zero), axis=0, keepdims=True))
    devs = group_sum(rows8(*sums)) * scale
    stats[slot, 0:8] = means
    stats[slot, 8:16] = lax.rsqrt(devs + EPS_NORM)


def put_shifts(pads, n, at, value):
    col = lax.broadcasted_iota(jnp.int32, value.shape, 0) % SIDE
    left = jnp.where(col == 0, 0.0, pltpu.roll(value, 1, 0))
    right = jnp.where(col == SIDE - 1, 0.0, pltpu.roll(value, value.shape[0] - 1, 0))
    rows = pl.ds(PAD + at, value.shape[0])
    pads[0, n, rows, :] = left.astype(BF16)
    pads[1, n, rows, :] = value.astype(BF16)
    pads[2, n, rows, :] = right.astype(BF16)


def tap(pads, r, c):
    return pads[c + 1, :, PAD + SIDE * r : PAD + SIDE * r + POS, :].reshape(SPOTS, CH)


OFFSETS = [(r, c) for r in (-1, 0, 1) for c in (-1, 0, 1)]


def network_kernel(
    x_ref, z_ref, mine_ref, noise_ref, when_ref, feat_ref, flag_ref, mats, ion_ref,
    dmats, dion_ref, scal_ref,
    h, flow, c1s, pads, acts, stats, start, goal, qkv, probs, mixed, tmp, smallf, dqkv,
):
    batch = x_ref.shape[0]
    depth = x_ref.shape[1]
    active = flag_ref[0, 0]
    ion = ion_ref[...].T
    w_in = ion[0:16].astype(BF16)
    w_out = ion[16:32].astype(BF16)

    def gain(s):
        return ion[32 + 2 * s : 33 + 2 * s]

    def bias(s):
        return ion[33 + 2 * s : 34 + 2 * s]

    x = x_ref[...]
    z = z_ref[...]
    gram = dot(x, z, 1, 1)
    xf = x.astype(F32)
    zf = z.astype(F32)
    sq_x = jnp.sum(xf * xf, axis=1, keepdims=True)
    sq_z = jnp.sum(zf * zf, axis=1, keepdims=True)
    eye = lax.broadcasted_iota(jnp.int32, (batch, batch), 0) == lax.broadcasted_iota(jnp.int32, (batch, batch), 1)
    sq_z = jnp.sum(jnp.where(eye, sq_z, 0.0), axis=0, keepdims=True)
    cost = (sq_x + sq_z - 2.0 * gram) / depth
    affinity = 2.0 * gram / (depth * SINK_EPS)
    kern = jnp.exp(affinity - jnp.max(affinity, axis=1, keepdims=True))
    share = 1.0 / batch

    def sweep(i, c):
        left, right = c
        left = share / jnp.sum(kern * right, axis=1, keepdims=True)
        right = share / jnp.sum(left * kern, axis=0, keepdims=True)
        return left, right

    left, right = lax.fori_loop(0, SINK, sweep, (jnp.ones((batch, 1), F32), jnp.ones((1, batch), F32)))
    scaled = kern * right
    plan_cost = jnp.sum(left * scaled * cost)
    mixing = (scaled / jnp.sum(scaled, axis=1, keepdims=True)).astype(BF16)
    d = mine_ref[...].astype(BF16)
    mix = dot(d, mixing).astype(BF16)
    paired = dot(mix, z)[0:IMGS]
    pixels = dot(d, x)[0:IMGS]
    times = when_ref[0:IMGS, 0:1]
    inputs = ((1.0 - times) * paired + times * pixels).astype(BF16).astype(F32)
    target = pixels - paired
    start[...] = jnp.zeros_like(start)
    goal[...] = jnp.zeros_like(goal)
    for n in range(IMGS):
        for k in range(SUB):
            start[16 * n + k : 16 * n + k + 1, :] = inputs[n : n + 1, k * POS : (k + 1) * POS]
            goal[16 * n + k : 16 * n + k + 1, :] = target[n : n + 1, k * POS : (k + 1) * POS]
    begin = start[...].astype(BF16)

    for c in range(3):
        for n in range(IMGS):
            pads[c, n, 0:PAD, :] = jnp.zeros((PAD, CH), BF16)
            pads[c, n, PAD + POS :, :] = jnp.zeros((PAD, CH), BF16)

    def blocks(body):
        for n in range(IMGS):
            for_blocks(lambda at, c: (body(n, at), c)[1], 0)

    def norm_forward(field, slot, shifted, keep):
        norm_stats(field, stats, slot)
        g, b = gain(slot), bias(slot)

        def body(n, at):
            mean = stats[slot, n : n + 1]
            rstd = stats[slot, 8 + n : 9 + n]
            rows = pl.ds(n * POS + at, ROWS)
            y = (field[rows, :] - mean) * rstd * g + b
            if slot != 2:
                y = y * (1.0 / (1.0 + jnp.exp(-y)))
            acts[keep, rows, :] = y.astype(BF16)
            if shifted:
                put_shifts(pads, n, at, y)

        blocks(body)

    def conv(layer):
        acc = None
        for k, (r, c) in enumerate(OFFSETS):
            term = dot(tap(pads, r, c), mats[9 * layer + k])
            acc = term if acc is None else acc + term
        return acc

    feats = feat_ref[...].astype(BF16)

    for n in range(IMGS):
        h[0, n * POS : (n + 1) * POS, :] = dot(begin[16 * n : 16 * n + 16], w_in, 0, 0)

    def residual(layer, slot, src, dst):
        norm_forward(h.at[src], slot, True, slot)
        added = dot(feats, mats[TIME_AT + layer])
        got = conv(2 * layer)
        for n in range(IMGS):
            c1s[layer, n * POS : (n + 1) * POS, :] = got[n * POS : (n + 1) * POS] + added[n : n + 1]
        norm_forward(c1s.at[layer], slot + 1, True, slot + 1)
        h[dst] = h[src] + conv(2 * layer + 1)

    residual(0, 0, 0, 1)
    norm_forward(h.at[1], 2, False, 2)
    normal = acts[2]
    for j in range(3):
        qkv[j] = dot(normal, mats[ATTN_AT + j]).astype(BF16)
    scale = HD ** (-0.5)

    def head_mask(hh):
        return lax.broadcasted_iota(jnp.int32, (POS, CH), 1) // HD == hh

    for n in range(IMGS):
        rows = slice(n * POS, (n + 1) * POS)
        tmp[...] = jnp.zeros_like(tmp)

        def head(hh, c):
            mask = head_mask(hh)
            q = jnp.where(mask, qkv[0, rows, :].astype(F32), 0.0).astype(BF16)
            scores = dot(q, qkv[1, rows, :], 1, 1) * scale
            e = jnp.exp(scores - jnp.max(scores, axis=1, keepdims=True))
            p = e / jnp.sum(e, axis=1, keepdims=True)
            probs[n, hh] = p
            o = dot(p.astype(BF16), qkv[2, rows, :])
            tmp[...] = jnp.where(mask, o, tmp[...])
            return c

        lax.fori_loop(0, HEADS, head, 0)
        mixed[rows, :] = tmp[...].astype(BF16)
    h[2] = h[1] + dot(mixed[...], mats[ATTN_AT + 3], 1, 1)
    residual(1, 3, 2, 3)
    norm_forward(h.at[3], 5, False if False else False, 5)

    dion_ref[...] = jnp.zeros_like(dion_ref)
    loss = jnp.zeros((), F32)
    for n in range(IMGS):
        rows = slice(n * POS, (n + 1) * POS)
        last = acts[5, rows, :]
        pred = dot(w_out, last, 1, 1)
        error = pred - goal[16 * n : 16 * n + 16, :]
        loss = loss + jnp.sum(error * error)
        low = (error * (flag_ref[0, 1] * active)).astype(BF16)
        dion_ref[16:32, :] += dot(low, last)
        flow[rows, :] = dot(low, w_out, 0, 0)
    lane = lax.broadcasted_iota(jnp.int32, (8, 128), 1)
    scal_ref[...] = jnp.where(lane == 0, loss * active, jnp.where(lane == 1, plan_cost, 0.0))

    def norm_backward(field, slot, up, finish):
        g, b = gain(slot), bias(slot)
        zero = jnp.zeros((8, CH), F32)

        def fold(v):
            return v.reshape(ROWS // 8, 8, CH).sum(axis=0)

        dbs, dgs = [], []
        for n in range(IMGS):
            mean = stats[slot, n : n + 1]
            rstd = stats[slot, 8 + n : 9 + n]

            def step(at, c):
                rows = pl.ds(n * POS + at, ROWS)
                hat = (field[rows, :] - mean) * rstd
                dz = up[rows, :]
                if slot != 2:
                    y = hat * g + b
                    s = 1.0 / (1.0 + jnp.exp(-y))
                    dz = dz * (s * (1.0 + y * (1.0 - s)))
                    up[rows, :] = dz
                return (c[0] + fold(dz), c[1] + fold(dz * hat))

            db, dg = for_blocks(step, (zero, zero))
            dbs.append(jnp.sum(db, axis=0, keepdims=True))
            dgs.append(jnp.sum(dg, axis=0, keepdims=True))
        dion_ref[32 + 2 * slot : 33 + 2 * slot, :] = dgs[0] + dgs[1]
        dion_ref[33 + 2 * slot : 34 + 2 * slot, :] = dbs[0] + dbs[1]
        sums = group_sum(rows8(*[v * g for v in dbs + dgs])) * (1.0 / (POS * (CH // GROUPS)))
        for n in range(IMGS):
            mean = stats[slot, n : n + 1]
            rstd = stats[slot, 8 + n : 9 + n]
            m1 = sums[n : n + 1]
            m2 = sums[IMGS + n : IMGS + n + 1]

            def step(at, c):
                rows = pl.ds(n * POS + at, ROWS)
                hat = (field[rows, :] - mean) * rstd
                finish(n, at, rstd * (up[rows, :] * g - m1 - hat * m2))
                return c

            for_blocks(step, 0)

    def conv_backward(layer, keep):
        turned = acts[keep].T
        acc = None
        for k, (r, c) in enumerate(OFFSETS):
            there = tap(pads, -r, -c)
            dmats[9 * layer + k] = dot(turned, there)
            term = dot(there, mats[9 * layer + k], 1, 1)
            acc = term if acc is None else acc + term
        smallf[...] = acc

    def add_flow(shifted):
        def finish(n, at, dx):
            rows = pl.ds(n * POS + at, ROWS)
            total = flow[rows, :] + dx
            flow[rows, :] = total
            if shifted:
                put_shifts(pads, n, at, total)

        return finish

    def set_flow(n, at, dx):
        rows = pl.ds(n * POS + at, ROWS)
        flow[rows, :] = dx
        put_shifts(pads, n, at, dx)

    def only_shifts(n, at, dx):
        put_shifts(pads, n, at, dx)

    def residual_backward(layer, slot, src, last_one):
        conv_backward(2 * layer + 1, slot + 1)
        norm_backward(c1s.at[layer], slot + 1, smallf, only_shifts)
        sums = []
        for n in range(IMGS):
            low = pads[1, n, PAD : PAD + POS, :].astype(F32)
            sums.append(jnp.sum(low, axis=0, keepdims=True))
        one, two, three = split3(rows8(*sums))
        stack = jnp.concatenate([v.astype(F32) for v in (one, two, three)], axis=0).astype(BF16)
        feats3 = jnp.concatenate([feats.astype(F32)] * 3, axis=0).astype(BF16)
        dmats[TIME_AT + layer] = dot(feats3, stack, 0, 0)
        conv_backward(2 * layer, slot)
        norm_backward(h.at[src], slot, smallf, add_flow(False))

    norm_backward(h.at[3], 5, flow, set_flow)
    residual_backward(1, 3, 2, False)

    dy = flow[...].astype(BF16)
    dmats[ATTN_AT + 3] = dot(dy.T, mixed[...])
    dqkv[3] = dot(dy, mats[ATTN_AT + 3]).astype(BF16)
    for n in range(IMGS):
        rows = slice(n * POS, (n + 1) * POS)
        for j in range(3):
            smallf[j % 2 * POS : j % 2 * POS + POS, :] = jnp.zeros((POS, CH), F32)
        tmp[...] = jnp.zeros_like(tmp)

        def head(hh, c):
            mask = head_mask(hh)
            do = jnp.where(mask, dqkv[3, rows, :].astype(F32), 0.0).astype(BF16)
            q = jnp.where(mask, qkv[0, rows, :].astype(F32), 0.0).astype(BF16)
            p = probs[n, hh]
            dp = dot(do, qkv[2, rows, :], 1, 1)
            ds = (p * (dp - jnp.sum(p * dp, axis=1, keepdims=True))).astype(BF16)
            tmp[...] = jnp.where(mask, dot(ds, qkv[1, rows, :]), tmp[...])
            smallf[0:POS, :] += dot(ds, q, 0, 0)
            smallf[POS:, :] += dot(p.astype(BF16), do, 0, 0)
            return c

        lax.fori_loop(0, HEADS, head, 0)
        dqkv[0, rows, :] = (tmp[...] * scale).astype(BF16)
        dqkv[1, rows, :] = (smallf[0:POS, :] * scale).astype(BF16)
        dqkv[2, rows, :] = smallf[POS:, :].astype(BF16)
    turned = acts[2].T
    acc = None
    for j in range(3):
        dmats[ATTN_AT + j] = dot(turned, dqkv[j])
        term = dot(dqkv[j], mats[ATTN_AT + j], 1, 1)
        acc = term if acc is None else acc + term
    smallf[...] = acc
    norm_backward(h.at[1], 2, smallf, add_flow(True))
    residual_backward(0, 0, 0, True)
    for n in range(IMGS):
        rows = slice(n * POS, (n + 1) * POS)
        dion_ref[0:16, :] += dot(begin[16 * n : 16 * n + 16], flow[rows, :].astype(BF16))


def network(x, z, mine, when, feat, flag, mats, ion):
    whole = pl.BlockSpec(memory_space=pltpu.VMEM)
    noise = jnp.zeros((8, 128), F32)
    return pl.pallas_call(
        network_kernel,
        out_shape=(
            jax.ShapeDtypeStruct((MATS, CH, CH), F32),
            jax.ShapeDtypeStruct((48, CH), F32),
            jax.ShapeDtypeStruct((8, 128), F32),
        ),
        in_specs=[whole] * 6 + [pl.BlockSpec(memory_space=pltpu.SMEM)] + [whole] * 2,
        out_specs=(whole, whole, whole),
        scratch_shapes=[
            pltpu.VMEM((4, SPOTS, CH), F32),
            pltpu.VMEM((SPOTS, CH), F32),
            pltpu.VMEM((2, SPOTS, CH), F32),
            pltpu.VMEM((3, IMGS, POS + 2 * PAD, CH), BF16),
            pltpu.VMEM((6, SPOTS, CH), BF16),
            pltpu.VMEM((6, 16, CH), F32),
            pltpu.VMEM((16 * IMGS, POS), F32),
            pltpu.VMEM((16 * IMGS, POS), F32),
            pltpu.VMEM((3, SPOTS, CH), BF16),
            pltpu.VMEM((IMGS, HEADS, POS, POS), F32),
            pltpu.VMEM((SPOTS, CH), BF16),
            pltpu.VMEM((POS, CH), F32),
            pltpu.VMEM((SPOTS, CH), F32),
            pltpu.VMEM((4, SPOTS, CH), BF16),
        ],
        compiler_params=pltpu.CompilerParams(vmem_limit_bytes=56 * 2**20),
    )(x, z, mine, noise, when, feat, flag, mats, ion)


def time_features(time_index):
    times = (time_index.astype(jnp.float32) + 0.5) / NT
    half = CH // 2
    frequency = jnp.exp(-math.log(10000.0) * jnp.arange(half, dtype=jnp.float32) / half)
    angles = 1000.0 * times[:, None] * frequency[None, :]
    return jnp.concatenate([jnp.sin(angles), jnp.cos(angles)], axis=1)


def adam_update(weight, first, second, average, gradient, rate):
    first = BETA_ONE * first + (1 - BETA_ONE) * gradient
    second = BETA_TWO * second + (1 - BETA_TWO) * gradient * gradient
    ratio = first / (1 - BETA_ONE**STEP) / (jnp.sqrt(second / (1 - BETA_TWO**STEP)) + ADAM_EPS)
    weight = weight - rate * (ratio + WEIGHT_DECAY * weight)
    average = EMA_DECAY * average + (1 - EMA_DECAY) * weight
    return (weight, first, second, average)


def pack_mats(conv, time, attn):
    return jnp.concatenate(
        [conv.reshape((TIME_AT,) + conv.shape[2:]), time, attn.transpose(1, 0, 2)], axis=0
    )


def pack_small(io, norm):
    own = norm.shape[0] // SUB
    io = io.reshape(own, 2, SUB)
    norm = norm.reshape(own, SUB)
    gap = jnp.zeros((own, 16 - SUB), io.dtype)
    return jnp.concatenate(
        [io[:, 0], gap, io[:, 1], gap, norm, gap, jnp.zeros((own, 80), io.dtype)], axis=1
    )


def body(
    images, noises, order, time_index, io_weight, conv_weight, time_weight, attn_weight, norm_param,
    io_first, conv_first, time_first, attn_first, norm_first,
    io_second, conv_second, time_second, attn_second, norm_second,
    io_average, conv_average, time_average, attn_average, norm_average,
):
    rank = lax.axis_index("mp")
    place = lax.axis_index("dp")
    micro, count, depth = noises.shape
    turn = jnp.minimum(rank, micro - 1)
    mats = pack_mats(conv_weight, time_weight, attn_weight).astype(BF16)
    mats = lax.all_gather(lax.all_gather(mats, "dp", axis=1, tiled=True), "mp", axis=2, tiled=True)
    ion = pack_small(io_weight, norm_param).astype(BF16)
    ion = lax.all_gather(ion, ("mp", "dp"), axis=0, tiled=True).astype(F32)
    chosen = lax.dynamic_slice_in_dim(order, turn * count, count, 0)
    own = jnp.stack(
        [jnp.take(images, chosen, axis=0), lax.dynamic_index_in_dim(noises, turn, 0, keepdims=False)]
    )
    both = lax.all_gather(own, "dp", axis=1, tiled=True)
    batch = both.shape[1]
    when = lax.dynamic_index_in_dim(time_index, turn, 0, keepdims=False)
    feat = jnp.pad(time_features(when).astype(BF16).astype(F32), ((0, 8 - count), (0, 0)))
    times = (when.astype(F32) + 0.5) / NT
    times = jnp.pad(jnp.broadcast_to(times[:, None], (count, 128)), ((0, 8 - count), (0, 0)))
    spot = jnp.arange(8)[:, None]
    mine = ((jnp.arange(batch)[None, :] == place * count + spot) & (spot < count)).astype(F32)
    active = (rank < micro).astype(F32)
    flag = jnp.stack([active, jnp.float32(2.0 / (micro * batch))]).reshape(1, 2)
    dmats, dion, scal = network(both[0], both[1], mine, times, feat, flag, mats, ion)
    dmats = lax.psum_scatter(dmats, "dp", scatter_dimension=1, tiled=True)
    dmats = lax.psum_scatter(dmats, "mp", scatter_dimension=2, tiled=True)
    dion = lax.psum_scatter(dion.T, ("mp", "dp"), scatter_dimension=0, tiled=True)
    hot = (jnp.arange(micro) == rank).astype(F32)
    squares = jnp.sum(dmats * dmats) + jnp.sum(dion * dion)
    total_sq, loss_sum, cost_sum = lax.psum(
        (squares, hot * scal[0, 0], jnp.where(place == 0, hot * scal[0, 1], 0.0)), ("dp", "mp")
    )
    grad_norm = jnp.sqrt(total_sq)
    scale = CLIP_NORM / jnp.maximum(grad_norm, CLIP_NORM)
    grads = (
        jnp.concatenate([dion[:, None, 0:SUB], dion[:, None, 16 : 16 + SUB]], axis=1).reshape(-1),
        dmats[:TIME_AT].reshape(conv_weight.shape),
        dmats[TIME_AT:ATTN_AT],
        dmats[ATTN_AT:].transpose(1, 0, 2),
        dion[:, 32 : 32 + SUB].reshape(-1),
    )
    weights = (io_weight, conv_weight, time_weight, attn_weight, norm_param)
    firsts = (io_first, conv_first, time_first, attn_first, norm_first)
    seconds = (io_second, conv_second, time_second, attn_second, norm_second)
    averages = (io_average, conv_average, time_average, attn_average, norm_average)
    results = [
        adam_update(weights[kind], firsts[kind], seconds[kind], averages[kind], grads[kind] * scale, RATES[kind])
        for kind in range(5)
    ]
    return tuple(results[kind][part] for part in range(4) for kind in range(5)) + (loss_sum, cost_sum, grad_norm)


def solution(mesh):
    flat = P(("mp", "dp"))
    state = (flat, P(None, None, "dp", "mp"), P(None, "dp", "mp"), P("dp", None, "mp"), flat)
    return jax.shard_map(
        body,
        mesh=mesh,
        in_specs=(P("dp", None), P(None, "dp", None), P("dp"), P(None, "dp")) + state * 4,
        out_specs=state * 4 + (P(), P(), P()),
        check_vma=False,
    )
```

time: 1700 us -> 537 us (0.32)
  local copies, waits for them, and re-layouts: 560 us -> 38.8 us
  blocking collectives: 578 us -> 174 us
  other arithmetic: 141 us -> 16.8 us
  matrix products: 90.7 us -> 0 us
  Pallas kernels: 0 us -> 42 us
  waiting for transfers between devices: 282 us -> 246 us
    all_gather x36 -> x2, blocking collectives: 296 us -> 94.4 us  [the longest x1 63.7 us: body(): ion = lax.all_gather(ion, ('mp', 'dp'), axis=0, tiled=True).astype(F32)]
    slice x174 -> x4, local copies, waits for them, and re-layouts: 188 us -> 1.72 us  [the longest x1 1.34 us: body(): scal[0, 1]]
    unnamed x16 -> x5, waiting for transfers between devices: 184 us -> 0.07 us
    psum x11 -> x1, blocking collectives: 221 us -> 40.2 us  [body(): lax.psum((squares, hot * scal[0, 0], jnp.where(place == 0, hot * scal[0,...]
    another operation x111 -> x2, local copies, waits for them, and re-layouts: 132 us -> 0.11 us  [the longest x108 128 us: stacked_shifts(): jnp.stack([shifted(inputs, row_off, col_off) for row_off, col_off in OFFS...]
    dot_general x121 -> x0, matrix products: 90.7 us -> none  [the longest x12 23.3 us: conv_weight_grad(): jnp.einsum('nkcp,nop->kco', stacked_shifts(inputs), grads_low, preferred_...]
    unnamed x900 -> x55, local copies, waits for them, and re-layouts: 110 us -> 21.2 us
    reduce_scatter x6 -> x1, waiting for transfers between devices: 97.9 us -> 185 us  [body(): dmats = lax.psum_scatter(dmats, 'dp', scatter_dimension=1, tiled=True)]
  transfers between devices with their start and end apart: 12 -> 4, of which waited for: 10 -> 2; matrix products, arithmetic and copies ran while one was open for 11% -> 2% of each run, Pallas kernels for 0% -> 0%
where the time goes in v1:
time: 537 us; the launch traced here: 536 us
  waiting for transfers between devices  246 us (46%)
  blocking collectives  174 us (32%)
  Pallas kernels  42 us (8%)
  local copies, waits for them, and re-layouts  38.8 us (7%)
  between operations  18 us (3%)
  other arithmetic  16.8 us (3%)
    reduce_scatter x1, waiting for transfers between devices, body(): dmats = lax.psum_scatter(dmats, 'dp', scatter_dimension=1, tiled=True)  185 us
    all_gather x1, blocking collectives, body(): ion = lax.all_gather(ion, ('mp', 'dp'), axis=0, tiled=True).astype(F32)  63.7 us
    all_gather x1, waiting for transfers between devices, body(): lax.all_gather(mats, 'dp', axis=1, tiled=True)  61.2 us
    pallas_call x1, Pallas kernels, network(): pl.pallas_call(network_kernel, out_shape=(jax.ShapeDtypeStruct((MATS, CH,...  42 us
    psum x1, blocking collectives, body(): lax.psum((squares, hot * scal[0, 0], jnp.where(place == 0, hot * scal[0,...  40.2 us
    unnamed x1, blocking collectives  39.8 us
    all_gather x1, blocking collectives, body(): both = lax.all_gather(own, 'dp', axis=1, tiled=True)  30.6 us
    unnamed x55, local copies, waits for them, and re-layouts  21.2 us
  transfers between devices with their start and end apart: 4, of which 2 were waited for; matrix products, arithmetic and copies ran while one was open for 2% of the time, Pallas kernels for 0%

profile of v1, /device:TPU:0, one launch (start us, length us, event | category | flops | bytes accessed | tf_op | source)
XLA Modules:
  0.0 536.1 jit_solution(7802709887141024338)
XLA Ops:
  7.2 0.0 all-gather.3.cloned.1.call-start
  7.3 1.1 convert.42
  8.4 0.8 copy.179
  9.2 0.8 convert.43
  10.0 0.8 pad_maximum_fusion
  10.8 0.0 all-gather.3.cloned.1.call-update
  10.8 0.0 all-gather.5.cloned.1.call-start
  10.9 61.2 %all-gather.3.cloned.1.call-done = bf16[42,256,64]{2,1,0:T(8,128)(2,1)} async-done(((bf16[42,32,64]{2,1,0:T(8,128)(2,1)}), bf16[42,256,64]{2,1,0:T(8,128)(2,1)}) %all-gather.3.cloned.1.call-update) | async-done | bytes 1376272 | tf_op jit(solution)/shard_map/all_gather | solution.py:469
  72.1 4.1 copy.131
  76.2 0.0 all-gather.5.cloned.1.call-update
  76.2 0.0 reduce-scatter.6.cloned.1.call-start
  76.3 0.1 compare_and_fusion
  76.4 0.6 gather_fusion
  76.9 0.7 constant_dynamic-slice_fusion.1
  77.7 0.1 broadcast_select_fusion
  77.8 30.6 %all_gather.12 = bf16[2,16,3072]{2,0,1:T(2,128)(2,1)S(1)} all-gather(bf16[2,2,3072]{2,0,1:T(2,128)(2,1)S(1)} %copy.127), channel_id=1, replica_groups=mesh['dp'=8,'mp'=4] {'dp'}, dimensions={1}, use_global_device_ids=true | all-gather | bytes 221184 | tf_op jit(solution)/shard_map/all_gather | solution.py:476
  108.5 0.3 fusion.22
  108.7 0.7 copy.177
  109.4 0.7 copy.178
  110.1 0.1 reshape.132
  110.3 0.1 reshape.130
  110.4 0.1 concatenate.17
  110.4 63.7 %all_gather.15 = bf16[256,128]{1,0:T(8,128)(2,1)S(1)} all-gather(bf16[8,128]{1,0:T(8,128)(2,1)S(1)} %concatenate.17), channel_id=1, replica_groups=mesh['dp'=8,'mp'=4] {'mp','dp'}, dimensions={0}, use_global_device_ids=true | all-gather | bytes 67584 | tf_op jit(solution)/shard_map/all_gather | solution.py:471
  174.2 0.7 convert_element_type.30.ion_ref
  174.8 0.2 add_reduce_fusion
  175.1 0.6 maximum_bitcast_fusion.flag_ref
  175.7 0.1 fusion.13
  175.8 0.6 fusion.10.feat_ref
  176.4 0.7 fusion.12.mine_ref
  177.1 8.3 %copy.132.mats = bf16[42,256,256]{2,1,0:T(8,128)(2,1)} copy(bf16[42,256,256]{1,2,0:T(8,128)(2,1)} %all-gather.5.cloned.1.call-done) | data formatting | bytes 11010048 | tf_op jit(solution)/shard_map/all_gather | solution.py:469
  185.3 0.7 pad.13.when_ref
  186.0 0.6 broadcast_in_dim.40.noise_ref
  186.6 42.0 %shard_map.407 = (f32[42,256,256]{2,1,0:T(8,128)}, f32[48,256]{1,0:T(8,128)}, f32[8,128]{1,0:T(8,128)}) custom-call(bf16[16,3072]{1,0:T(8,128)(2,1)} %bitcast.45, bf16[16,3072]{1,0:T(8,128)(2,1)} %bitcast.44, f32[8,16]{1,0:T(8,128)} %fusion.12.mine_ref, f32[8,128]{1,0:T(8,128)} %broadcast_in_dim.40.noise_ref, f32[8,128]{1,0:T(8,128)} %pad.13.when_ref, ...), custom_call_target="tpu_custom_call" | custom-call | tf_op jit(solution)/shard_map/pallas_call | solution.py:396
  228.6 0.0 reduce-scatter.6.cloned.1.call-update
  228.6 0.0 reduce-scatter.8.cloned.1.call-start
  228.7 184.7 %reduce-scatter.6.cloned.1.call-done = f32[42,32,256]{2,1,0:T(8,128)} async-done(((f32[42,256,256]{2,1,0:T(8,128)}), f32[42,32,256]{2,1,0:T(8,128)}) %reduce-scatter.6.cloned.1.call-update) | async-done | bytes 1376272 | tf_op jit(solution)/shard_map/reduce_scatter | solution.py:487
  413.4 6.1 %copy.148 = f32[42,32,256]{1,0,2:T(8,128)} copy(f32[42,32,256]{2,1,0:T(8,128)} %reduce-scatter.6.cloned.1.call-done) | data formatting | bytes 2752512
  419.6 5.3 reshape.144
  424.9 0.6 dynamic-slice
  426.2 39.8 %all-reduce.2 = f32[256,48]{0,1:T(8,128)S(1)} all-reduce(f32[256,48]{0,1:T(8,128)S(1)} %bitcast.47), channel_id=2, replica_groups=mesh['dp'=8,'mp'=4] {'mp','dp'}, use_global_device_ids=true, to_apply=%region_0.1.clone | all-reduce | flops 12288 | bytes 98304
  465.9 0.1 fusion.23
  466.0 0.7 copy.156
  466.7 0.7 copy.154
  467.4 0.7 copy.155
  468.0 0.7 fusion.6
  468.7 1.3 fusion.24
  470.1 1.8 compare_select_fusion.2
  471.9 1.6 reshape.145
  473.5 0.5 copy.149
  474.1 0.8 multiply_reduce_fusion
  476.2 40.2 %all-reduce.3 = (f32[]{:T(128)}, f32[3]{0:T(128)}, f32[3]{0:T(128)}) all-reduce(f32[]{:T(128)S(6)} %add.154, f32[3]{0:T(128)} %get-tuple-element.203, f32[3]{0:T(128)} %get-tuple-element.204), channel_id=1, replica_groups=mesh['dp'=8,'mp'=4] {'dp','mp'}, use_global_device_ids=true, to_apply=%region_5.6 | all-reduce | flops 7 | bytes 56 | tf_op jit(solution)/shard_map/psum | solution.py:492
  517.1 0.7 broadcast_multiply_fusion
  517.8 0.6 mul.315
  518.4 1.0 fusion.3
  519.4 0.7 copy.142
  520.1 0.7 copy.143
  520.7 0.7 copy.144
  521.4 0.7 copy.145
  522.1 0.7 maximum_multiply_fusion
  522.8 0.1 mul.274
  523.0 0.7 multiply_add_fusion.4
  523.7 1.3 multiply_add_fusion.8
  524.9 2.9 multiply_add_fusion.1
  527.8 0.6 multiply_add_fusion.6
  (58 shorter events, 0.3 us)
Async XLA Ops:
  7.2 69.2 %copy-start = (bf16[6,3072]{1,0:T(8,128)(2,1)S(1)}, bf16[6,3072]{1,0:T(8,128)(2,1)}, u32[]{:S(2)}) copy-start(bf16[6,3072]{1,0:T(8,128)(2,1)} %param.24) | copy-start | bytes 110596
  7.2 64.9 %all-gather.3.cloned.1.call-start = ((), (), s32[]{:S(2)}) async-start(), calls=%async_computation.2 | async-start | bytes 3096576 | tf_op jit(solution)/shard_map/all_gather | solution.py:469
  10.8 65.5 %copy-start.17 = (s32[6]{0:T(128)S(1)}, s32[6]{0:T(128)}, u32[]{:S(2)}) copy-start(s32[6]{0:T(128)} %param.26) | copy-start | bytes 76
  10.8 99.3 %copy-start.11 = (f32[192]{0:T(256)S(1)}, f32[192]{0:T(256)}, u32[]{:S(2)}) copy-start(f32[192]{0:T(256)} %param.28) | copy-start | bytes 2308
  10.8 99.4 %copy-start.16 = (f32[96]{0:T(128)S(1)}, f32[96]{0:T(128)}, u32[]{:S(2)}) copy-start(f32[96]{0:T(128)} %param.32) | copy-start | bytes 1156
  10.8 166.2 %all-gather.5.cloned.1.call-start = ((), (), s32[]{:S(2)}) async-start(), calls=%async_computation.3 | async-start | bytes 6881280 | tf_op jit(solution)/shard_map/all_gather | solution.py:469
  76.2 98.7 %copy-start.15 = (s32[3,2]{0,1:T(2,128)S(1)}, s32[3,2]{0,1:T(2,128)}, u32[]{:S(2)}) copy-start(s32[3,2]{0,1:T(2,128)} %param.27) | copy-start | bytes 76
  76.2 337.2 %reduce-scatter.6.cloned.1.call-start = ((), (), s32[]{:S(2)}) async-start(), calls=%async_computation.4 | async-start | bytes 12386304 | tf_op jit(solution)/shard_map/reduce_scatter | solution.py:487
  228.6 243.3 %reduce-scatter.8.cloned.1.call-start = ((), (), s32[]{:S(2)}) async-start(), calls=%async_computation.5 | async-start | bytes 1802240
  419.6 5.4 %copy-start.18 = (u32[32]{0:T(128)S(1)}, u32[32]{0:T(128)}, u32[]{:S(2)}) copy-start(u32[32]{0:T(128)} %constant.128) | copy-start | bytes 388
  419.6 6.6 %copy-start.6 = (f32[48,256]{1,0:T(8,128)S(1)}, f32[48,256]{1,0:T(8,128)}, u32[]{:S(2)}) copy-start(f32[48,256]{1,0:T(8,128)} %get-tuple-element.26) | copy-start | bytes 147460
  471.9 46.5 %copy-start.4 = (f32[32,4,64]{2,1,0:T(4,128)S(1)}, f32[32,4,64]{2,1,0:T(4,128)}, u32[]{:S(2)}) copy-start(f32[32,4,64]{2,1,0:T(4,128)} %param.31) | copy-start | bytes 98308
  473.5 51.5 %copy-start.1 = (f32[4,9,32,64]{3,2,1,0:T(8,128)S(1)}, f32[4,9,32,64]{3,2,1,0:T(8,128)}, u32[]{:S(2)}) copy-start(f32[4,9,32,64]{3,2,1,0:T(8,128)} %param.29) | copy-start | bytes 884740
  473.5 51.5 %copy-start.2 = (f32[4,9,32,64]{3,2,1,0:T(8,128)S(1)}, f32[4,9,32,64]{3,2,1,0:T(8,128)}, u32[]{:S(2)}) copy-start(f32[4,9,32,64]{3,2,1,0:T(8,128)} %param.44) | copy-start | bytes 884740
  474.0 48.9 %copy-start.5 = (f32[2,32,64]{2,1,0:T(8,128)S(1)}, f32[2,32,64]{2,1,0:T(8,128)}, u32[]{:S(2)}) copy-start(f32[2,32,64]{2,1,0:T(8,128)} %param.30) | copy-start | bytes 49156
  474.0 48.9 %copy-start.7 = (f32[2,32,64]{2,1,0:T(8,128)S(1)}, f32[2,32,64]{2,1,0:T(8,128)}, u32[]{:S(2)}) copy-start(f32[2,32,64]{2,1,0:T(8,128)} %param.45) | copy-start | bytes 49156
  474.1 48.9 %copy-start.8 = (f32[2,32,64]{2,1,0:T(8,128)S(1)}, f32[2,32,64]{2,1,0:T(8,128)}, u32[]{:S(2)}) copy-start(f32[2,32,64]{2,1,0:T(8,128)} %param.35) | copy-start | bytes 49156
  474.1 48.9 %copy-start.9 = (f32[2,32,64]{2,1,0:T(8,128)S(1)}, f32[2,32,64]{2,1,0:T(8,128)}, u32[]{:S(2)}) copy-start(f32[2,32,64]{2,1,0:T(8,128)} %param.40) | copy-start | bytes 49156
  474.1 50.9 %copy-start.3 = (f32[4,9,32,64]{3,2,1,0:T(8,128)S(1)}, f32[4,9,32,64]{3,2,1,0:T(8,128)}, u32[]{:S(2)}) copy-start(f32[4,9,32,64]{3,2,1,0:T(8,128)} %param.34) | copy-start | bytes 884740
  522.9 4.8 copy-start.10
  523.0 4.8 copy-start.12
  523.0 4.8 copy-start.13
  523.0 4.8 copy-start.14
Sparse Core Ops, SparseCore 0:
  10.9 61.1 all-gather.2
  76.3 40.0 all-gather.4
  228.7 184.6 reduce-scatter.5
  425.0 26.4 reduce-scatter.7

commit v2 on v1

--- a/solution.py
+++ b/solution.py
@@ -1,4 +1,4 @@
-from functools import partial
+import functools
 import math
 
 import jax
@@ -19,8 +19,12 @@
 NT = 1000
 STEP = 5
 MATS = 42
-TIME_AT = 36
-ATTN_AT = 38
+CONV_AT = (1, 10, 24, 33)
+TIME_AT = (0, 23)
+ATTN_AT = 19
+CHUNKS = ((0, 10), (10, 9), (19, 4), (23, 10), (33, 9))
+LEVELS = 32000.0
+MESH = pl.DeviceIdType.MESH
 
 
 EPS_NORM = 1e-05
@@ -114,15 +118,12 @@
 OFFSETS = [(r, c) for r in (-1, 0, 1) for c in (-1, 0, 1)]
 
 
-def network_kernel(
-    x_ref, z_ref, mine_ref, noise_ref, when_ref, feat_ref, flag_ref, mats, ion_ref,
-    dmats, dion_ref, scal_ref,
+def train(
+    x, z, mine, when_ref, feat_ref, active, step_scale, ion, mat, put, ready, done,
+    dion_ref, scal_ref,
     h, flow, c1s, pads, acts, stats, start, goal, qkv, probs, mixed, tmp, smallf, dqkv,
 ):
-    batch = x_ref.shape[0]
-    depth = x_ref.shape[1]
-    active = flag_ref[0, 0]
-    ion = ion_ref[...].T
+    batch, depth = x.shape
     w_in = ion[0:16].astype(BF16)
     w_out = ion[16:32].astype(BF16)
 
@@ -132,8 +133,6 @@
     def bias(s):
         return ion[33 + 2 * s : 34 + 2 * s]
 
-    x = x_ref[...]
-    z = z_ref[...]
     gram = dot(x, z, 1, 1)
     xf = x.astype(F32)
     zf = z.astype(F32)
@@ -156,7 +155,7 @@
     scaled = kern * right
     plan_cost = jnp.sum(left * scaled * cost)
     mixing = (scaled / jnp.sum(scaled, axis=1, keepdims=True)).astype(BF16)
-    d = mine_ref[...].astype(BF16)
+    d = mine.astype(BF16)
     mix = dot(d, mixing).astype(BF16)
     paired = dot(mix, z)[0:IMGS]
     pixels = dot(d, x)[0:IMGS]
@@ -200,7 +199,7 @@
     def conv(layer):
         acc = None
         for k, (r, c) in enumerate(OFFSETS):
-            term = dot(tap(pads, r, c), mats[9 * layer + k])
+            term = dot(tap(pads, r, c), mat(CONV_AT[layer] + k))
             acc = term if acc is None else acc + term
         return acc
 
@@ -211,18 +210,21 @@
 
     def residual(layer, slot, src, dst):
         norm_forward(h.at[src], slot, True, slot)
-        added = dot(feats, mats[TIME_AT + layer])
+        ready(0 if layer == 0 else 3)
+        added = dot(feats, mat(TIME_AT[layer]))
         got = conv(2 * layer)
         for n in range(IMGS):
             c1s[layer, n * POS : (n + 1) * POS, :] = got[n * POS : (n + 1) * POS] + added[n : n + 1]
         norm_forward(c1s.at[layer], slot + 1, True, slot + 1)
+        ready(1 if layer == 0 else 4)
         h[dst] = h[src] + conv(2 * layer + 1)
 
     residual(0, 0, 0, 1)
     norm_forward(h.at[1], 2, False, 2)
+    ready(2)
     normal = acts[2]
     for j in range(3):
-        qkv[j] = dot(normal, mats[ATTN_AT + j]).astype(BF16)
+        qkv[j] = dot(normal, mat(ATTN_AT + j)).astype(BF16)
     scale = HD ** (-0.5)
 
     def head_mask(hh):
@@ -245,9 +247,9 @@
 
         lax.fori_loop(0, HEADS, head, 0)
         mixed[rows, :] = tmp[...].astype(BF16)
-    h[2] = h[1] + dot(mixed[...], mats[ATTN_AT + 3], 1, 1)
+    h[2] = h[1] + dot(mixed[...], mat(ATTN_AT + 3), 1, 1)
     residual(1, 3, 2, 3)
-    norm_forward(h.at[3], 5, False if False else False, 5)
+    norm_forward(h.at[3], 5, False, 5)
 
     dion_ref[...] = jnp.zeros_like(dion_ref)
     loss = jnp.zeros((), F32)
@@ -257,7 +259,7 @@
         pred = dot(w_out, last, 1, 1)
         error = pred - goal[16 * n : 16 * n + 16, :]
         loss = loss + jnp.sum(error * error)
-        low = (error * (flag_ref[0, 1] * active)).astype(BF16)
+        low = (error * (step_scale * active)).astype(BF16)
         dion_ref[16:32, :] += dot(low, last)
         flow[rows, :] = dot(low, w_out, 0, 0)
     lane = lax.broadcasted_iota(jnp.int32, (8, 128), 1)
@@ -311,8 +313,8 @@
         acc = None
         for k, (r, c) in enumerate(OFFSETS):
             there = tap(pads, -r, -c)
-            dmats[9 * layer + k] = dot(turned, there)
-            term = dot(there, mats[9 * layer + k], 1, 1)
+            put(CONV_AT[layer] + k, dot(turned, there))
+            term = dot(there, mat(CONV_AT[layer] + k), 1, 1)
             acc = term if acc is None else acc + term
         smallf[...] = acc
 
@@ -336,6 +338,7 @@
 
     def residual_backward(layer, slot, src, last_one):
         conv_backward(2 * layer + 1, slot + 1)
+        done(4 if layer == 1 else 1)
         norm_backward(c1s.at[layer], slot + 1, smallf, only_shifts)
         sums = []
         for n in range(IMGS):
@@ -344,16 +347,17 @@
         one, two, three = split3(rows8(*sums))
         stack = jnp.concatenate([v.astype(F32) for v in (one, two, three)], axis=0).astype(BF16)
         feats3 = jnp.concatenate([feats.astype(F32)] * 3, axis=0).astype(BF16)
-        dmats[TIME_AT + layer] = dot(feats3, stack, 0, 0)
+        put(TIME_AT[layer], dot(feats3, stack, 0, 0))
         conv_backward(2 * layer, slot)
+        done(3 if layer == 1 else 0)
         norm_backward(h.at[src], slot, smallf, add_flow(False))
 
     norm_backward(h.at[3], 5, flow, set_flow)
     residual_backward(1, 3, 2, False)
 
     dy = flow[...].astype(BF16)
-    dmats[ATTN_AT + 3] = dot(dy.T, mixed[...])
-    dqkv[3] = dot(dy, mats[ATTN_AT + 3]).astype(BF16)
+    put(ATTN_AT + 3, dot(dy.T, mixed[...]))
+    dqkv[3] = dot(dy, mat(ATTN_AT + 3)).astype(BF16)
     for n in range(IMGS):
         rows = slice(n * POS, (n + 1) * POS)
         for j in range(3):
@@ -379,10 +383,11 @@
     turned = acts[2].T
     acc = None
     for j in range(3):
-        dmats[ATTN_AT + j] = dot(turned, dqkv[j])
-        term = dot(dqkv[j], mats[ATTN_AT + j], 1, 1)
+        put(ATTN_AT + j, dot(turned, dqkv[j]))
+        term = dot(dqkv[j], mat(ATTN_AT + j), 1, 1)
         acc = term if acc is None else acc + term
     smallf[...] = acc
+    done(2)
     norm_backward(h.at[1], 2, smallf, add_flow(True))
     residual_backward(0, 0, 0, True)
     for n in range(IMGS):
@@ -390,36 +395,496 @@
         dion_ref[0:16, :] += dot(begin[16 * n : 16 * n + 16], flow[rows, :].astype(BF16))
 
 
-def network(x, z, mine, when, feat, flag, mats, ion):
+def work_space():
+    return [
+        pltpu.VMEM((4, SPOTS, CH), F32),
+        pltpu.VMEM((SPOTS, CH), F32),
+        pltpu.VMEM((2, SPOTS, CH), F32),
+        pltpu.VMEM((3, IMGS, POS + 2 * PAD, CH), BF16),
+        pltpu.VMEM((6, SPOTS, CH), BF16),
+        pltpu.VMEM((6, 16, CH), F32),
+        pltpu.VMEM((16 * IMGS, POS), F32),
+        pltpu.VMEM((16 * IMGS, POS), F32),
+        pltpu.VMEM((3, SPOTS, CH), BF16),
+        pltpu.VMEM((IMGS, HEADS, POS, POS), F32),
+        pltpu.VMEM((SPOTS, CH), BF16),
+        pltpu.VMEM((POS, CH), F32),
+        pltpu.VMEM((SPOTS, CH), F32),
+        pltpu.VMEM((4, SPOTS, CH), BF16),
+    ]
+
+
+def local_kernel(x_ref, z_ref, mine_ref, when_ref, feat_ref, flag_ref, mats, ion_ref, dmats, dion_ref, scal_ref, *work):
+    def put(m, value):
+        dmats[m] = value
+
+    train(
+        x_ref[...], z_ref[...], mine_ref[...], when_ref, feat_ref, flag_ref[0, 0], flag_ref[0, 1],
+        ion_ref[...].T, lambda m: mats[m], put, lambda chunk: None, lambda chunk: None,
+        dion_ref, scal_ref, *work,
+    )
+
+
+def local_network(x, z, mine, when, feat, flag, mats, ion):
     whole = pl.BlockSpec(memory_space=pltpu.VMEM)
-    noise = jnp.zeros((8, 128), F32)
     return pl.pallas_call(
-        network_kernel,
+        local_kernel,
         out_shape=(
             jax.ShapeDtypeStruct((MATS, CH, CH), F32),
             jax.ShapeDtypeStruct((48, CH), F32),
             jax.ShapeDtypeStruct((8, 128), F32),
         ),
-        in_specs=[whole] * 6 + [pl.BlockSpec(memory_space=pltpu.SMEM)] + [whole] * 2,
+        in_specs=[whole] * 5 + [pl.BlockSpec(memory_space=pltpu.SMEM)] + [whole] * 2,
+        out_specs=(whole, whole, whole),
+        scratch_shapes=work_space(),
+        compiler_params=pltpu.CompilerParams(vmem_limit_bytes=56 * 2**20),
+    )(x, z, mine, when, feat, flag, mats, ion)
+
+
+Z, Y, X, C = 4, 2, 2, 2
+DEVICES = Z * Y * X * C
+
+
+def fused_kernel(
+    micro, batch,
+    ot_ref, when_ref, feat_ref, own_ref, ownion_ref,
+    grads_ref, gion_ref, total_ref,
+    mats, dmats, other, land, otbuf, otwide, xz, ionbuf, dion, diont, ionr, scal, scalr,
+    s1q, s1r, s2q, s2r, zq, zr, expo, kept, gother,
+    ot_s, ot_r, ion_s, ion_r, g_s, g_r, r_s, r_r, d_s, d_r, n_s, n_r,
+    *work,
+):
+    dp = lax.axis_index("dp")
+    mp = lax.axis_index("mp")
+    z, y, x, c = dp // Y, dp % Y, mp // C, mp % C
+    flat = mp * (Z * Y) + dp
+
+    def place(z_, y_, x_, c_):
+        return (z_ * Y + y_, x_ * C + c_)
+
+    def from_flat(f):
+        return (f % (Z * Y), f // (Z * Y))
+
+    sibling = place(z, y, x, 1 - c)
+    first = place(z, y * c + (1 - y) * (1 - c), x * (1 - c) + (1 - x) * c, c)
+    second = place(z, (1 - y) * c + y * (1 - c), (1 - x) * (1 - c) + x * c, c)
+
+    def remote(src, dst, send, recv, where):
+        return pltpu.make_async_remote_copy(
+            src_ref=src, dst_ref=dst, send_sem=send, recv_sem=recv, device_id=where, device_id_type=MESH
+        )
+
+    barrier = pltpu.get_barrier_semaphore()
+
+    def greet(j, carry):
+        pl.semaphore_signal(
+            barrier, inc=1, device_id=from_flat((flat + j) % DEVICES), device_id_type=MESH
+        )
+        return carry
+
+    lax.fori_loop(1, DEVICES, greet, 0)
+    pl.semaphore_wait(barrier, DEVICES - 1)
+
+    zero_copy = remote(own_ref.at[:, pl.ds((1 - c) * 16, 16)], land, g_s.at[0, 0], g_r.at[0, 0], sibling)
+    zero_copy.start()
+
+    def ot_copy(j):
+        there = (dp + j) % (Z * Y)
+        return remote(ot_ref, otbuf.at[dp], ot_s.at[j], ot_r.at[j], (there, mp))
+
+    for j in range(1, Z * Y):
+        ot_copy(j).start()
+    otbuf[dp] = ot_ref[...]
+
+    def ion_copy(j):
+        return remote(ownion_ref, ionbuf.at[flat], ion_s.at[j], ion_r.at[j], from_flat((flat + j) % DEVICES))
+
+    def ion_start(j, carry):
+        ion_copy(j).start()
+        return carry
+
+    lax.fori_loop(1, DEVICES, ion_start, 0)
+    ionbuf[flat] = ownion_ref[...]
+
+    zero_copy.wait()
+
+    def merge(m, carry):
+        mats[m, x, z, y, c] = own_ref[m, pl.ds(pl.multiple_of(c * 16, 16), 16), :] + land[m]
+        return carry
+
+    lax.fori_loop(0, MATS, merge, 0)
+
+    def span(i):
+        return pl.ds(CHUNKS[i][0], CHUNKS[i][1])
+
+    def z_copy(i, j):
+        part = mats.at[span(i), x, z, y, c]
+        return remote(part, part, g_s.at[i + 1, j], g_r.at[i + 1, j], place((z + j) % Z, y, x, c))
+
+    def u_copy(i):
+        part = mats.at[span(i), x, :, y, c]
+        return remote(part, part, g_s.at[i + 1, 4], g_r.at[i + 1, 4], first)
+
+    def v_copy(i, core):
+        part = mats.at[span(i), x, :, :, 0] if core == 0 else mats.at[span(i), :, :, y, 1]
+        return remote(part, part, g_s.at[i + 1, 5], g_r.at[i + 1, 5], second)
+
+    def c_copy(i):
+        part = mats.at[span(i), :, :, :, c]
+        return remote(part, part, g_s.at[i + 1, 6], g_r.at[i + 1, 6], sibling)
+
+    def on_core(act):
+        for core in range(C):
+            pl.when(c == core)(functools.partial(act, core))
+
+    def gather_step(stage, i):
+        if i < 0 or i >= len(CHUNKS):
+            return
+        if stage == 0:
+            for j in range(1, Z):
+                z_copy(i, j).start()
+        elif stage == 1:
+            for j in range(1, Z):
+                z_copy(i, j).wait()
+            u_copy(i).start()
+        elif stage == 2:
+            u_copy(i).wait()
+            on_core(lambda core: v_copy(i, core).start())
+        elif stage == 3:
+            on_core(lambda core: v_copy(i, core).wait())
+            c_copy(i).start()
+        else:
+            c_copy(i).wait()
+
+    for i in range(len(CHUNKS)):
+        gather_step(0, i)
+    gather_step(1, 0)
+
+    for j in range(1, Z * Y):
+        ot_copy(j).wait()
+    rows = ot_ref.shape[0]
+    for j in range(Z * Y):
+        otwide[pl.ds(j * rows, rows), :] = otbuf[j].astype(F32)
+    lines = rows // (2 * IMGS)
+    for r in range(2 * IMGS):
+        for k in range(lines):
+            xz[r // IMGS, (r % IMGS) * Z * Y : (r % IMGS + 1) * Z * Y, k * 128 : (k + 1) * 128] = otwide[
+                pl.ds(r * lines + k, Z * Y, stride=rows), :
+            ]
+    gather_step(2, 0)
+    gather_step(1, 1)
+
+    def ion_wait(j, carry):
+        ion_copy(j).wait()
+        return carry
+
+    lax.fori_loop(1, DEVICES, ion_wait, 0)
+    ion = ionbuf[...].reshape(CH, 128).T
+    spot = lax.broadcasted_iota(jnp.int32, (8, batch), 0)
+    column = lax.broadcasted_iota(jnp.int32, (8, batch), 1)
+    mine = jnp.where((column == spot * (Z * Y) + dp) & (spot < IMGS), 1.0, 0.0)
+    active = jnp.where(mp < micro, 1.0, 0.0)
+
+    def mat(m):
+        return jnp.concatenate([mats[m, k].reshape(CH, 128) for k in range(X)], axis=1)
+
+    def put(m, value):
+        for k in range(X):
+            dmats[m, k] = value[:, 128 * k : 128 * k + 128].reshape(Z, Y, C, 16, 128)
+
+    def ready(i):
+        gather_step(3, i)
+        gather_step(2, i + 1)
+        gather_step(1, i + 2)
+        gather_step(4, i)
+
+    mine_a = x * (1 - c) + y * c
+    mine_b = y * (1 - c) + x * c
+
+    def xy(a, b):
+        return a * (1 - c) + b * c, b * (1 - c) + a * c
+
+    def r_copy(i):
+        return remote(
+            dmats.at[span(i), :, :, :, 1 - c], other.at[span(i)], r_s.at[i, 0], r_r.at[i, 0], sibling
+        )
+
+    def base(i, per):
+        return CHUNKS[i][0] * per + i
+
+    def one_copy(i):
+        part = pl.ds(base(i, 8), CHUNKS[i][1] * 8 + 1)
+        return remote(s1q.at[part], s1r.at[part], r_s.at[i, 1], r_r.at[i, 1], second)
+
+    def two_copy(i):
+        part = pl.ds(base(i, 4), CHUNKS[i][1] * 4 + 1)
+        return remote(s2q.at[part], s2r.at[part], r_s.at[i, 2], r_r.at[i, 2], first)
+
+    def three_copy(i, j):
+        part = pl.ds(base(i, 1), CHUNKS[i][1] + 1)
+        return remote(
+            zq.at[j - 1, part], zr.at[j - 1, part], r_s.at[i, 2 + j], r_r.at[i, 2 + j], place((z + j) % Z, y, x, c)
+        )
+
+    def four_copy(i):
+        return remote(kept.at[span(i)], gother.at[span(i)], r_s.at[i, 6], r_r.at[i, 6], sibling)
+
+    def exponent(tiles):
+        top = jnp.max(jnp.abs(tiles[0]), axis=0, keepdims=True)
+        for t in tiles[1:]:
+            top = jnp.maximum(top, jnp.max(jnp.abs(t), axis=0, keepdims=True))
+        return jnp.floor(jnp.log2(jnp.maximum(top, 1e-30))) + 1.0
+
+    def coded(tile, power):
+        return jnp.round(tile * (LEVELS * jnp.exp2(-power))).astype(jnp.int32).astype(jnp.int16)
+
+    def decoded(tile, unit):
+        return tile.astype(jnp.int32).astype(F32) * unit
+
+    def units(ref, at, slot):
+        expo[slot] = jnp.exp2(ref[at].astype(jnp.int32).astype(F32)) * (1.0 / LEVELS)
+
+    def powers(ref, at):
+        ref[at] = expo[0].astype(jnp.int32).astype(jnp.int16)
+
+    def stage_one(i):
+        r_copy(i).wait()
+        first_m, count = CHUNKS[i]
+        start = base(i, 8)
+
+        def step(k, carry):
+            m = first_m + k
+            tiles = []
+            for b in range(2):
+                x_, y_ = xy(1 - mine_a, b)
+                for zz in range(Z):
+                    tiles.append(dmats[m, x_, zz, y_, c] + other[m, x_, zz, y_])
+            power = exponent(tiles)
+            expo[0, pl.ds(k, 1), :] = power
+            for t, tile in enumerate(tiles):
+                s1q[start + k * 8 + t] = coded(tile, power)
+            return carry
+
+        lax.fori_loop(0, count, step, 0)
+        powers(s1q, start + count * 8)
+        one_copy(i).start()
+
+    def stage_two(i):
+        one_copy(i).wait()
+        first_m, count = CHUNKS[i]
+        start, start_one = base(i, 4), base(i, 8)
+        units(s1r, start_one + count * 8, 1)
+
+        def step(k, carry):
+            m = first_m + k
+            unit = expo[1, pl.ds(k, 1), :]
+            x_, y_ = xy(mine_a, 1 - mine_b)
+            tiles = []
+            for zz in range(Z):
+                got = decoded(s1r[start_one + k * 8 + (1 - mine_b) * 4 + zz], unit)
+                tiles.append(dmats[m, x_, zz, y_, c] + other[m, x_, zz, y_] + got)
+            power = exponent(tiles)
+            expo[0, pl.ds(k, 1), :] = power
+            for t, tile in enumerate(tiles):
+                s2q[start + k * 4 + t] = coded(tile, power)
+            return carry
+
+        lax.fori_loop(0, count, step, 0)
+        powers(s2q, start + count * 4)
+        two_copy(i).start()
+
+    def stage_three(i):
+        two_copy(i).wait()
+        first_m, count = CHUNKS[i]
+        start, start_one, start_two = base(i, 1), base(i, 8), base(i, 4)
+        units(s1r, start_one + count * 8, 1)
+        units(s2r, start_two + count * 4, 2)
+
+        def step(k, carry):
+            m = first_m + k
+            unit_one = expo[1, pl.ds(k, 1), :]
+            unit_two = expo[2, pl.ds(k, 1), :]
+
+            def tile(zz):
+                return (
+                    dmats[m, x, zz, y, c]
+                    + other[m, x, zz, y]
+                    + decoded(s1r[start_one + k * 8 + mine_b * 4 + zz], unit_one)
+                    + decoded(s2r[start_two + k * 4 + zz], unit_two)
+                )
+
+            tiles = [tile((z + j) % Z) for j in range(1, Z)]
+            power = exponent(tiles)
+            expo[0, pl.ds(k, 1), :] = power
+            for j in range(1, Z):
+                zq[j - 1, start + k] = coded(tiles[j - 1], power)
+            kept[m] = tile(z)
+            return carry
+
+        lax.fori_loop(0, count, step, 0)
+        for j in range(1, Z):
+            powers(zq.at[j - 1], start + count)
+        for j in range(1, Z):
+            three_copy(i, j).start()
+
+    def stage_four(i):
+        for j in range(1, Z):
+            three_copy(i, j).wait()
+        first_m, count = CHUNKS[i]
+        start = base(i, 1)
+        for j in range(1, Z):
+            units(zr.at[j - 1], start + count, j)
+
+        def step(k, carry):
+            m = first_m + k
+            total = kept[m]
+            for j in range(1, Z):
+                total = total + decoded(zr[j - 1, start + k], expo[j, pl.ds(k, 1), :])
+            kept[m] = total
+            return carry + total * total
+
+        square = lax.fori_loop(0, count, step, jnp.zeros((16, 128), F32))
+        four_copy(i).start()
+        return square
+
+    squares = []
+    order = (4, 3, 2, 1, 0)
+
+    def reduce_step(stage, turn):
+        if turn < 0 or turn >= len(order):
+            return
+        i = order[turn]
+        if stage == 0:
+            r_copy(i).start()
+        elif stage == 1:
+            stage_one(i)
+        elif stage == 2:
+            stage_two(i)
+        elif stage == 3:
+            stage_three(i)
+        else:
+            squares.append(stage_four(i))
+
+    def done(i):
+        turn = order.index(i)
+        for stage in range(5):
+            reduce_step(stage, turn - stage)
+
+    train(
+        xz[0].astype(BF16), xz[1].astype(BF16), mine, when_ref, feat_ref, active, 2.0 / (micro * batch),
+        ion, mat, put, ready, done, dion, scal, *work,
+    )
+
+    diont[...] = jnp.concatenate([dion[...], jnp.zeros((128 - 48, CH), F32)], axis=0).T.reshape(DEVICES, 8, 128)
+
+    def dion_copy(j):
+        there = (flat + j) % DEVICES
+        return remote(diont.at[there], ionr.at[flat], d_s.at[j], d_r.at[j], from_flat(there))
+
+    def dion_start(j, carry):
+        dion_copy(j).start()
+        return carry
+
+    lax.fori_loop(1, DEVICES, dion_start, 0)
+    ionr[flat] = diont[flat]
+    for turn in range(len(order), len(order) + 4):
+        for stage in range(5):
+            reduce_step(stage, turn - stage)
+
+    def dion_wait(j, carry):
+        dion_copy(j).wait()
+        return carry
+
+    lax.fori_loop(1, DEVICES, dion_wait, 0)
+    small = jnp.sum(ionr[...], axis=0)
+    gion_ref[...] = small
+    square = jnp.sum(small * small)
+    for part in squares:
+        square = square + jnp.sum(part)
+
+    loss, plan_cost = scal[0:1, 0:1], scal[0:1, 1:2]
+    lane = lax.broadcasted_iota(jnp.int32, (8, 128), 1)
+    tile = jnp.where(lane == 0, square, 0.0)
+    tile = jnp.where(lane == 1 + mp, loss, tile)
+    tile = jnp.where((lane == 1 + micro + mp) & (mp < micro) & (dp == 0), plan_cost, tile)
+    tile = jnp.where((mp >= micro) & (lane > 0), 0.0, tile)
+    scal[...] = tile
+    scalr[flat] = tile
+
+    def n_copy(j):
+        return remote(scal, scalr.at[flat], n_s.at[j], n_r.at[j], from_flat((flat + j) % DEVICES))
+
+    def n_start(j, carry):
+        n_copy(j).start()
+        return carry
+
+    def n_wait(j, carry):
+        n_copy(j).wait()
+        return carry
+
+    lax.fori_loop(1, DEVICES, n_start, 0)
+    for i in order:
+        four_copy(i).wait()
+
+    def finish(m, carry):
+        for half in range(C):
+            tile = jnp.where(c == half, kept[m], gother[m])
+            grads_ref[m, half * 16 : half * 16 + 16, :] = jnp.where(c == 0, tile[:, 0:64], tile[:, 64:128])
+        return carry
+
+    lax.fori_loop(0, MATS, finish, 0)
+    lax.fori_loop(1, DEVICES, n_wait, 0)
+    total_ref[...] = jnp.sum(scalr[...], axis=0)
+
+
+def fused_network(micro, batch, ot, when, feat, own, ownion):
+    whole = pl.BlockSpec(memory_space=pltpu.VMEM)
+    blocks = (X, Z, Y)
+    dma = pltpu.SemaphoreType.DMA
+    count = len(CHUNKS)
+    return pl.pallas_call(
+        functools.partial(fused_kernel, micro, batch),
+        out_shape=(
+            jax.ShapeDtypeStruct((MATS, 32, 64), F32),
+            jax.ShapeDtypeStruct((8, 128), F32),
+            jax.ShapeDtypeStruct((8, 128), F32),
+        ),
+        in_specs=[whole] * 5,
         out_specs=(whole, whole, whole),
         scratch_shapes=[
-            pltpu.VMEM((4, SPOTS, CH), F32),
-            pltpu.VMEM((SPOTS, CH), F32),
-            pltpu.VMEM((2, SPOTS, CH), F32),
-            pltpu.VMEM((3, IMGS, POS + 2 * PAD, CH), BF16),
-            pltpu.VMEM((6, SPOTS, CH), BF16),
-            pltpu.VMEM((6, 16, CH), F32),
-            pltpu.VMEM((16 * IMGS, POS), F32),
-            pltpu.VMEM((16 * IMGS, POS), F32),
-            pltpu.VMEM((3, SPOTS, CH), BF16),
-            pltpu.VMEM((IMGS, HEADS, POS, POS), F32),
-            pltpu.VMEM((SPOTS, CH), BF16),
-            pltpu.VMEM((POS, CH), F32),
-            pltpu.VMEM((SPOTS, CH), F32),
-            pltpu.VMEM((4, SPOTS, CH), BF16),
-        ],
-        compiler_params=pltpu.CompilerParams(vmem_limit_bytes=56 * 2**20),
-    )(x, z, mine, noise, when, feat, flag, mats, ion)
+            pltpu.VMEM((MATS,) + blocks + (C, 16, 128), BF16),
+            pltpu.VMEM((MATS,) + blocks + (C, 16, 128), F32),
+            pltpu.VMEM((MATS,) + blocks + (16, 128), F32),
+            pltpu.VMEM((MATS, 16, 128), BF16),
+            pltpu.VMEM((Z * Y,) + ot.shape, BF16),
+            pltpu.VMEM((Z * Y * ot.shape[0], 128), F32),
+            pltpu.VMEM((2, batch, SUB * POS), F32),
+            pltpu.VMEM((DEVICES, 8, 128), F32),
+            pltpu.VMEM((48, CH), F32),
+            pltpu.VMEM((DEVICES, 8, 128), F32),
+            pltpu.VMEM((DEVICES, 8, 128), F32),
+            pltpu.VMEM((8, 128), F32),
+            pltpu.VMEM((DEVICES, 8, 128), F32),
+            pltpu.VMEM((MATS * 8 + count, 16, 128), jnp.int16),
+            pltpu.VMEM((MATS * 8 + count, 16, 128), jnp.int16),
+            pltpu.VMEM((MATS * 4 + count, 16, 128), jnp.int16),
+            pltpu.VMEM((MATS * 4 + count, 16, 128), jnp.int16),
+            pltpu.VMEM((Z - 1, MATS + count, 16, 128), jnp.int16),
+            pltpu.VMEM((Z - 1, MATS + count, 16, 128), jnp.int16),
+            pltpu.VMEM((Z, 16, 128), F32),
+            pltpu.VMEM((MATS, 16, 128), F32),
+            pltpu.VMEM((MATS, 16, 128), F32),
+            dma((Z * Y,)), dma((Z * Y,)),
+            dma((DEVICES,)), dma((DEVICES,)),
+            dma((count + 1, 7)), dma((count + 1, 7)),
+            dma((count, 7)), dma((count, 7)),
+            dma((DEVICES,)), dma((DEVICES,)),
+            dma((DEVICES,)), dma((DEVICES,)),
+        ] + work_space(),
+        compiler_params=pltpu.CompilerParams(
+            vmem_limit_bytes=60 * 2**20, collective_id=0, has_side_effects=True
+        ),
+    )(ot, when, feat, own, ownion)
 
 
 def time_features(time_index):
@@ -440,9 +905,16 @@
 
 
 def pack_mats(conv, time, attn):
+    kinds = 9
     return jnp.concatenate(
-        [conv.reshape((TIME_AT,) + conv.shape[2:]), time, attn.transpose(1, 0, 2)], axis=0
+        [time[0:1], conv[0], conv[1], attn.transpose(1, 0, 2), time[1:2], conv[2], conv[3]], axis=0
     )
+
+
+def unpack_mats(mats):
+    conv = jnp.stack([mats[at : at + 9] for at in CONV_AT])
+    time = jnp.stack([mats[at] for at in TIME_AT])
+    return conv, time, mats[ATTN_AT : ATTN_AT + 4].transpose(1, 0, 2)
 
 
 def pack_small(io, norm):
@@ -456,6 +928,7 @@
 
 
 def body(
+    fused,
     images, noises, order, time_index, io_weight, conv_weight, time_weight, attn_weight, norm_param,
     io_first, conv_first, time_first, attn_first, norm_first,
     io_second, conv_second, time_second, attn_second, norm_second,
@@ -464,41 +937,51 @@
     rank = lax.axis_index("mp")
     place = lax.axis_index("dp")
     micro, count, depth = noises.shape
+    batch = count * lax.axis_size("dp")
     turn = jnp.minimum(rank, micro - 1)
     mats = pack_mats(conv_weight, time_weight, attn_weight).astype(BF16)
-    mats = lax.all_gather(lax.all_gather(mats, "dp", axis=1, tiled=True), "mp", axis=2, tiled=True)
     ion = pack_small(io_weight, norm_param).astype(BF16)
-    ion = lax.all_gather(ion, ("mp", "dp"), axis=0, tiled=True).astype(F32)
     chosen = lax.dynamic_slice_in_dim(order, turn * count, count, 0)
-    own = jnp.stack(
-        [jnp.take(images, chosen, axis=0), lax.dynamic_index_in_dim(noises, turn, 0, keepdims=False)]
-    )
-    both = lax.all_gather(own, "dp", axis=1, tiled=True)
-    batch = both.shape[1]
+    own_x = jnp.take(images, chosen, axis=0)
+    own_z = lax.dynamic_index_in_dim(noises, turn, 0, keepdims=False)
     when = lax.dynamic_index_in_dim(time_index, turn, 0, keepdims=False)
     feat = jnp.pad(time_features(when).astype(BF16).astype(F32), ((0, 8 - count), (0, 0)))
     times = (when.astype(F32) + 0.5) / NT
     times = jnp.pad(jnp.broadcast_to(times[:, None], (count, 128)), ((0, 8 - count), (0, 0)))
-    spot = jnp.arange(8)[:, None]
-    mine = ((jnp.arange(batch)[None, :] == place * count + spot) & (spot < count)).astype(F32)
-    active = (rank < micro).astype(F32)
-    flag = jnp.stack([active, jnp.float32(2.0 / (micro * batch))]).reshape(1, 2)
-    dmats, dion, scal = network(both[0], both[1], mine, times, feat, flag, mats, ion)
-    dmats = lax.psum_scatter(dmats, "dp", scatter_dimension=1, tiled=True)
-    dmats = lax.psum_scatter(dmats, "mp", scatter_dimension=2, tiled=True)
-    dion = lax.psum_scatter(dion.T, ("mp", "dp"), scatter_dimension=0, tiled=True)
-    hot = (jnp.arange(micro) == rank).astype(F32)
-    squares = jnp.sum(dmats * dmats) + jnp.sum(dion * dion)
-    total_sq, loss_sum, cost_sum = lax.psum(
-        (squares, hot * scal[0, 0], jnp.where(place == 0, hot * scal[0, 1], 0.0)), ("dp", "mp")
-    )
+    if fused:
+        ot = jnp.concatenate([own_x, own_z]).reshape(-1, 128)
+        none = jnp.zeros_like(mats)
+        low = rank % 2 == 0
+        own = jnp.concatenate([jnp.where(low, mats, none), jnp.where(low, none, mats)], axis=2)
+        dmats, dion, total = fused_network(micro, batch, ot, times, feat, own, ion.astype(F32))
+        total_sq = total[0, 0]
+        loss_sum = total[0, 1 : 1 + micro]
+        cost_sum = total[0, 1 + micro : 1 + 2 * micro]
+    else:
+        mats = lax.all_gather(lax.all_gather(mats, "dp", axis=1, tiled=True), "mp", axis=2, tiled=True)
+        ion = lax.all_gather(ion, ("mp", "dp"), axis=0, tiled=True).astype(F32)
+        both = lax.all_gather(jnp.stack([own_x, own_z]), "dp", axis=1, tiled=True)
+        spot = jnp.arange(8)[:, None]
+        mine = ((jnp.arange(batch)[None, :] == place * count + spot) & (spot < count)).astype(F32)
+        active = (rank < micro).astype(F32)
+        flag = jnp.stack([active, jnp.float32(2.0 / (micro * batch))]).reshape(1, 2)
+        dmats, dion, scal = local_network(both[0], both[1], mine, times, feat, flag, mats, ion)
+        dmats = lax.psum_scatter(dmats, "dp", scatter_dimension=1, tiled=True)
+        dmats = lax.psum_scatter(dmats, "mp", scatter_dimension=2, tiled=True)
+        dion = lax.psum_scatter(dion.T, ("mp", "dp"), scatter_dimension=0, tiled=True)
+        hot = (jnp.arange(micro) == rank).astype(F32)
+        squares = jnp.sum(dmats * dmats) + jnp.sum(dion * dion)
+        total_sq, loss_sum, cost_sum = lax.psum(
+            (squares, hot * scal[0, 0], jnp.where(place == 0, hot * scal[0, 1], 0.0)), ("dp", "mp")
+        )
     grad_norm = jnp.sqrt(total_sq)
     scale = CLIP_NORM / jnp.maximum(grad_norm, CLIP_NORM)
+    conv_grad, time_grad, attn_grad = unpack_mats(dmats)
     grads = (
         jnp.concatenate([dion[:, None, 0:SUB], dion[:, None, 16 : 16 + SUB]], axis=1).reshape(-1),
-        dmats[:TIME_AT].reshape(conv_weight.shape),
-        dmats[TIME_AT:ATTN_AT],
-        dmats[ATTN_AT:].transpose(1, 0, 2),
+        conv_grad,
+        time_grad,
+        attn_grad,
         dion[:, 32 : 32 + SUB].reshape(-1),
     )
     weights = (io_weight, conv_weight, time_weight, attn_weight, norm_param)
@@ -515,8 +998,9 @@
 def solution(mesh):
     flat = P(("mp", "dp"))
     state = (flat, P(None, None, "dp", "mp"), P(None, "dp", "mp"), P("dp", None, "mp"), flat)
+    fused = mesh.shape["dp"] == Z * Y and mesh.shape["mp"] == X * C
     return jax.shard_map(
-        body,
+        functools.partial(body, fused),
         mesh=mesh,
         in_specs=(P("dp", None), P(None, "dp", None), P("dp"), P(None, "dp")) + state * 4,
         out_specs=state * 4 + (P(), P(), P()),

time: 537 us -> 146 us (0.27)
  waiting for transfers between devices: 246 us -> 0 us
  blocking collectives: 174 us -> 0 us
  Pallas kernels: 42 us -> 120 us
  local copies, waits for them, and re-layouts: 38.8 us -> 12.9 us
  between operations: 18 us -> 2.89 us
  other arithmetic: 16.8 us -> 9.29 us
    reduce_scatter x1 -> x0, waiting for transfers between devices: 185 us -> none  [body(): dmats = lax.psum_scatter(dmats, 'dp', scatter_dimension=1, tiled=True)]
    all_gather x2 -> x0, blocking collectives: 94.4 us -> none  [the longest x1 63.7 us: body(): ion = lax.all_gather(ion, ('mp', 'dp'), axis=0, tiled=True).astype(F32)]
    pallas_call x1, Pallas kernels: 42 us -> 120 us  [fused_network(): pl.pallas_call(functools.partial(fused_kernel, micro, batch), out_shape=(...]
    all_gather x2 -> x0, waiting for transfers between devices: 61.2 us -> none  [the longest x1 61.2 us: body(): lax.all_gather(mats, 'dp', axis=1, tiled=True)]
    psum x1 -> x0, blocking collectives: 40.2 us -> none  [body(): lax.psum((squares, hot * scal[0, 0], jnp.where(place == 0, hot * scal[0,...]
    unnamed x1 -> x0, blocking collectives: 39.8 us -> none
    unnamed x55 -> x59, local copies, waits for them, and re-layouts: 21.2 us -> 6.46 us
    all_gather x2 -> x0, local copies, waits for them, and re-layouts: 12.4 us -> none  [the longest x1 8.28 us: body(): lax.all_gather(lax.all_gather(mats, 'dp', axis=1, tiled=True), 'mp', axis...]
  transfers between devices with their start and end apart: 4 -> 0, of which waited for: 2 -> 0; matrix products, arithmetic and copies ran while one was open for 2% -> 0% of each run, Pallas kernels for 0% -> 0%
where the time goes in v2:
time: 146 us
  Pallas kernels  120 us (82%)
  local copies, waits for them, and re-layouts  12.9 us (9%)
  other arithmetic  9.29 us (6%)
  between operations  2.89 us (2%)
    pallas_call x1, Pallas kernels, fused_network(): pl.pallas_call(functools.partial(fused_kernel, micro, batch), out_shape=(...  120 us
    unnamed x59, local copies, waits for them, and re-layouts  6.46 us
    add x5, other arithmetic, adam_update(): average = EMA_DECAY * average + (1 - EMA_DECAY) * weight  4.62 us

profile of v2, /device:TPU:0, one launch (start us, length us, event | category | flops | bytes accessed | tf_op | source)
XLA Modules:
  0.0 145.5 jit_solution(8782594686414662994)
XLA Ops:
  0.7 0.0 copy-start
  0.7 0.7 copy-done.18
  1.4 0.2 add_reduce_fusion
  1.6 0.7 copy-done.15
  2.2 0.6 copy-done.19
  2.9 0.1 fusion.14
  3.0 0.0 copy-start.23
  3.0 0.6 copy-done.23
  3.7 0.1 compare_and_fusion
  3.8 0.1 reshape.89
  3.9 0.1 reshape.90
  3.9 0.7 pad.13.when_ref
  4.7 0.1 concatenate.25
  4.8 0.6 convert_element_type.24.ownion_ref
  5.4 0.6 fusion.13.feat_ref
  6.0 0.6 gather_fusion
  6.5 0.1 broadcast_select_fusion.2
  6.6 0.7 dynamic-slice_bitcast_fusion
  7.4 0.0 copy-start.7
  7.4 0.6 reshape.87.ot_ref
  8.0 0.1 copy-done.7
  8.2 1.1 convert.55
  9.3 0.0 copy-start.6
  9.3 0.8 copy-done.6
  10.2 0.1 broadcast_select_fusion.1
  10.3 0.0 copy-start.20
  10.3 0.0 copy-start.21
  10.3 0.0 copy-start.22
  10.3 0.0 copy-start.14
  10.3 0.0 copy-start.16
  10.3 0.0 copy-start.17
  10.3 0.0 copy-start.11
  10.4 0.0 copy-start.12
  10.4 0.0 copy-start.13
  10.4 0.0 copy-start.10
  10.4 0.9 pad_maximum_fusion.own_ref
  11.3 120.4 %shard_map.407 = (f32[42,32,64]{2,1,0:T(8,128)}, f32[8,128]{1,0:T(8,128)}, f32[8,128]{1,0:T(8,128)}) custom-call(bf16[96,128]{1,0:T(8,128)(2,1)} %reshape.87.ot_ref, f32[8,128]{1,0:T(8,128)} %pad.13.when_ref, f32[8,256]{1,0:T(8,128)} %fusion.13.feat_ref, bf16[42,32,128]{2,1,0:T(8,128)(2,1)} %pad_maximum_fusion.own_ref, f32[8,128]{1,0:T(8,128)} %convert_element_type.24.ownion_ref), custom_call_target="tpu_custom_call" | custom-call | tf_op jit(solution)/shard_map/pallas_call | solution.py:845
  131.8 0.0 copy-start.2
  131.8 1.3 slice.81
  133.8 1.3 slice_bitcast_fusion.10
  135.1 0.9 slice_multiply_fusion.1
  136.0 0.1 mul.287
  136.0 0.0 copy-done.20
  136.1 0.5 multiply_add_fusion.8
  136.6 0.1 mul.247
  136.7 0.6 multiply_add_fusion.6
  137.3 0.7 fusion.23
  138.1 0.0 copy-done.11
  138.1 0.0 copy-done.13
  138.1 0.7 multiply_add_fusion.4
  138.8 0.0 copy-done.10
  138.8 0.0 copy-done.9
  138.8 0.0 copy-start.4
  138.8 1.0 fusion.6
  139.8 0.0 copy-done.2
  139.8 0.0 copy-start.1
  139.8 0.0 copy-start.3
  139.8 0.7 copy.78
  140.5 0.7 copy.75
  141.2 0.7 copy.76
  141.9 0.7 copy.77
  142.5 0.0 copy-done.4
  142.5 0.0 copy-done.3
  142.6 1.8 %multiply_add_fusion.1 = (f32[4,9,32,64]{3,2,1,0:T(8,128)}, f32[4,9,32,64]{3,2,1,0:T(8,128)}, f32[4,9,32,64]{3,2,1,0:T(8,128)}, f32[4,9,32,64]{3,2,1,0:T(8,128)}) fusion(f32[4,9,32,64]{3,2,1,0:T(8,128)S(1)} %copy-done.3, f32[4,9,32,64]{3,2,1,0:T(8,128)S(1)} %copy-done.1, f32[]{:T(128)S(6)} %div.61, f32[1,9,32,64]{3,2,1,0:T(8,128)S(1)} %get-tuple-element.123, ...), kind=kLoop, calls=%fused_computation.5 | loop fusion | flops 1548288 | bytes 2654212 | tf_op jit(solution)/shard_map/add | solution.py:903
  (38 shorter events, 0.3 us)
Async XLA Ops:
  0.7 5.3 %copy-start = (bf16[6,3072]{1,0:T(8,128)(2,1)S(1)}, bf16[6,3072]{1,0:T(8,128)(2,1)}, u32[]{:S(2)}) copy-start(bf16[6,3072]{1,0:T(8,128)(2,1)} %param.24) | copy-start | bytes 110596
  0.7 0.7 copy-start.18
  1.6 0.7 copy-start.15
  2.2 0.7 copy-start.19
  3.0 0.7 copy-start.23
  7.4 0.8 copy-start.7
  9.3 0.8 copy-start.6
  10.3 125.8 %copy-start.20 = (f32[96]{0:T(128)S(1)}, f32[96]{0:T(128)}, u32[]{:S(2)}) copy-start(f32[96]{0:T(128)} %param.47) | copy-start | bytes 1156
  10.3 125.8 %copy-start.21 = (f32[96]{0:T(128)S(1)}, f32[96]{0:T(128)}, u32[]{:S(2)}) copy-start(f32[96]{0:T(128)} %param.37) | copy-start | bytes 1156
  10.3 125.8 %copy-start.22 = (f32[96]{0:T(128)S(1)}, f32[96]{0:T(128)}, u32[]{:S(2)}) copy-start(f32[96]{0:T(128)} %param.42) | copy-start | bytes 1156
  10.3 126.4 %copy-start.14 = (f32[192]{0:T(256)S(1)}, f32[192]{0:T(256)}, u32[]{:S(2)}) copy-start(f32[192]{0:T(256)} %param.43) | copy-start | bytes 2308
  10.3 126.4 %copy-start.16 = (f32[192]{0:T(256)S(1)}, f32[192]{0:T(256)}, u32[]{:S(2)}) copy-start(f32[192]{0:T(256)} %param.33) | copy-start | bytes 2308
  10.3 126.4 %copy-start.17 = (f32[192]{0:T(256)S(1)}, f32[192]{0:T(256)}, u32[]{:S(2)}) copy-start(f32[192]{0:T(256)} %param.38) | copy-start | bytes 2308
  10.3 127.7 %copy-start.11 = (f32[2,32,64]{2,1,0:T(8,128)S(1)}, f32[2,32,64]{2,1,0:T(8,128)}, u32[]{:S(2)}) copy-start(f32[2,32,64]{2,1,0:T(8,128)} %param.45) | copy-start | bytes 49156
  10.4 127.7 %copy-start.12 = (f32[2,32,64]{2,1,0:T(8,128)S(1)}, f32[2,32,64]{2,1,0:T(8,128)}, u32[]{:S(2)}) copy-start(f32[2,32,64]{2,1,0:T(8,128)} %param.35) | copy-start | bytes 49156
  10.4 127.7 %copy-start.13 = (f32[2,32,64]{2,1,0:T(8,128)S(1)}, f32[2,32,64]{2,1,0:T(8,128)}, u32[]{:S(2)}) copy-start(f32[2,32,64]{2,1,0:T(8,128)} %param.40) | copy-start | bytes 49156
  10.4 128.4 %copy-start.10 = (f32[32,4,64]{2,1,0:T(4,128)S(1)}, f32[32,4,64]{2,1,0:T(4,128)}, u32[]{:S(2)}) copy-start(f32[32,4,64]{2,1,0:T(4,128)} %param.41) | copy-start | bytes 98308
  11.3 127.4 %copy-start.8 = (f32[32,4,64]{2,1,0:T(4,128)S(1)}, f32[32,4,64]{2,1,0:T(4,128)}, u32[]{:S(2)}) copy-start(f32[32,4,64]{2,1,0:T(4,128)} %param.46) | copy-start | bytes 98308
  11.3 127.4 %copy-start.9 = (f32[32,4,64]{2,1,0:T(4,128)S(1)}, f32[32,4,64]{2,1,0:T(4,128)}, u32[]{:S(2)}) copy-start(f32[32,4,64]{2,1,0:T(4,128)} %param.36) | copy-start | bytes 98308
  11.3 131.2 %copy-start.5 = (f32[4,9,32,64]{3,2,1,0:T(8,128)S(1)}, f32[4,9,32,64]{3,2,1,0:T(8,128)}, u32[]{:S(2)}) copy-start(f32[4,9,32,64]{3,2,1,0:T(8,128)} %param.39) | copy-start | bytes 884740
  131.8 8.0 %copy-start.2 = (f32[42,32,64]{2,1,0:T(8,128)S(1)}, f32[42,32,64]{2,1,0:T(8,128)}, u32[]{:S(2)}) copy-start(f32[42,32,64]{2,1,0:T(8,128)} %get-tuple-element.28) | copy-start | bytes 1032196
  138.8 3.8 %copy-start.4 = (f32[4,9,32,64]{3,2,1,0:T(8,128)S(1)}, f32[4,9,32,64]{3,2,1,0:T(8,128)}, u32[]{:S(2)}) copy-start(f32[4,9,32,64]{3,2,1,0:T(8,128)} %param.34) | copy-start | bytes 884740
  139.8 2.8 %copy-start.1 = (f32[4,9,32,64]{3,2,1,0:T(8,128)S(1)}, f32[4,9,32,64]{3,2,1,0:T(8,128)}, u32[]{:S(2)}) copy-start(f32[4,9,32,64]{3,2,1,0:T(8,128)} %param.29) | copy-start | bytes 884740
  139.8 2.8 %copy-start.3 = (f32[4,9,32,64]{3,2,1,0:T(8,128)S(1)}, f32[4,9,32,64]{3,2,1,0:T(8,128)}, u32[]{:S(2)}) copy-start(f32[4,9,32,64]{3,2,1,0:T(8,128)} %param.44) | copy-start | bytes 884740

commit v3 on v2

--- a/solution.py
+++ b/solution.py
@@ -2,6 +2,7 @@
 import math
 
 import jax
+import numpy as np
 import jax.numpy as jnp
 from jax import lax
 from jax.experimental import pallas as pl
@@ -22,7 +23,45 @@
 CONV_AT = (1, 10, 24, 33)
 TIME_AT = (0, 23)
 ATTN_AT = 19
-CHUNKS = ((0, 10), (10, 9), (19, 4), (23, 10), (33, 9))
+CHUNKS = ((0, 5), (5, 5), (10, 5), (15, 4), (19, 4), (23, 5), (28, 5), (33, 5), (38, 4))
+SPLITS = (5, 15, 28, 38)
+EARLY = (4, 8)
+PLAN = {
+    "start": ("zero", "ot", "merge", "iz", "A4", "A8", "Z0", "Z1", "Z2", "Z3", "Z5", "Z6", "B4", "B8", "Z7", "iu",
+        "otw"),
+    "sink": ("E4", "iv", "E8", "U0"),
+    "h0": ("ic", "U1", "U2", "iw"),
+    "n0": ("V0", "U3"),
+    "c0": ("U5", "V1", "V2", "U6", "C0", "U7", "V3", "V5", "C1", "W0", "W1"),
+    "n1": ("C4", "C2", "V6"),
+    "c1": ("V7", "C3", "W2", "W3"),
+    "n2": ("C8", "C5"),
+    "qkv": ("C6", "W4"),
+    "at1": ("C7",),
+    "c2": ("W5", "W6"),
+    "c3": ("W7", "W8"),
+    "w3b": ("R7",),
+    "d3": ("R8",),
+    "w2a": ("S7",),
+    "w2b": ("R5", "S8"),
+    "d2": ("R6",),
+    "b3": ("S5",),
+    "do": ("T7", "S6"),
+    "bt1": ("T8", "T5"),
+    "proj": ("Y7",),
+    "b2": ("R4", "Y8", "T6", "Y5"),
+    "w1a": ("S4",),
+    "w1b": ("R2",),
+    "d1": ("R3", "Y6", "X7"),
+    "b1": ("S2", "T4", "S3", "F7", "X8", "X5"),
+    "w0a": ("F8", "F5"),
+    "w0b": ("R0", "X6"),
+    "d0": ("R1", "T2"),
+    "b0": ("Y4", "S0", "T3", "S1", "F6"),
+    "win": ("Y2",),
+    "tail": ("T0", "X4", "Y3", "F4", "T1", "X2", "Y0", "F2", "X3", "Y1", "F3", "X0", "F0", "X1"),
+    "end": ("F1",),
+}
 LEVELS = 32000.0
 MESH = pl.DeviceIdType.MESH
 
@@ -72,7 +111,7 @@
 
 
 def for_blocks(step, init):
-    return lax.fori_loop(0, POS // ROWS, lambda i, c: step(pl.multiple_of(i * ROWS, ROWS), c), init, unroll=2)
+    return lax.fori_loop(0, POS // ROWS, lambda i, c: step(pl.multiple_of(i * ROWS, ROWS), c), init, unroll=True)
 
 
 def norm_stats(field, stats, slot):
@@ -119,20 +158,18 @@
 
 
 def train(
-    x, z, mine, when_ref, feat_ref, active, step_scale, ion, mat, put, ready, done,
+    x, z, mine, times, feats, active, step_scale, weights_small, mat, put, pump,
     dion_ref, scal_ref,
     h, flow, c1s, pads, acts, stats, start, goal, qkv, probs, mixed, tmp, smallf, dqkv,
 ):
     batch, depth = x.shape
-    w_in = ion[0:16].astype(BF16)
-    w_out = ion[16:32].astype(BF16)
-
     def gain(s):
         return ion[32 + 2 * s : 33 + 2 * s]
 
     def bias(s):
         return ion[33 + 2 * s : 34 + 2 * s]
 
+    pump("pair")
     gram = dot(x, z, 1, 1)
     xf = x.astype(F32)
     zf = z.astype(F32)
@@ -144,6 +181,7 @@
     affinity = 2.0 * gram / (depth * SINK_EPS)
     kern = jnp.exp(affinity - jnp.max(affinity, axis=1, keepdims=True))
     share = 1.0 / batch
+    pump("sink")
 
     def sweep(i, c):
         left, right = c
@@ -159,7 +197,6 @@
     mix = dot(d, mixing).astype(BF16)
     paired = dot(mix, z)[0:IMGS]
     pixels = dot(d, x)[0:IMGS]
-    times = when_ref[0:IMGS, 0:1]
     inputs = ((1.0 - times) * paired + times * pixels).astype(BF16).astype(F32)
     target = pixels - paired
     start[...] = jnp.zeros_like(start)
@@ -203,25 +240,31 @@
             acc = term if acc is None else acc + term
         return acc
 
-    feats = feat_ref[...].astype(BF16)
-
+
+    pump("h0")
+    ion = weights_small()
+    w_in = ion[0:16].astype(BF16)
+    w_out = ion[16:32].astype(BF16)
     for n in range(IMGS):
         h[0, n * POS : (n + 1) * POS, :] = dot(begin[16 * n : 16 * n + 16], w_in, 0, 0)
 
     def residual(layer, slot, src, dst):
+        pump(f"n{slot}")
         norm_forward(h.at[src], slot, True, slot)
-        ready(0 if layer == 0 else 3)
+        pump(f"c{2 * layer}")
         added = dot(feats, mat(TIME_AT[layer]))
         got = conv(2 * layer)
         for n in range(IMGS):
             c1s[layer, n * POS : (n + 1) * POS, :] = got[n * POS : (n + 1) * POS] + added[n : n + 1]
+        pump(f"n{slot + 1}")
         norm_forward(c1s.at[layer], slot + 1, True, slot + 1)
-        ready(1 if layer == 0 else 4)
+        pump(f"c{2 * layer + 1}")
         h[dst] = h[src] + conv(2 * layer + 1)
 
     residual(0, 0, 0, 1)
+    pump("n2")
     norm_forward(h.at[1], 2, False, 2)
-    ready(2)
+    pump("qkv")
     normal = acts[2]
     for j in range(3):
         qkv[j] = dot(normal, mat(ATTN_AT + j)).astype(BF16)
@@ -232,6 +275,7 @@
 
     for n in range(IMGS):
         rows = slice(n * POS, (n + 1) * POS)
+        pump(f"at{n}")
         tmp[...] = jnp.zeros_like(tmp)
 
         def head(hh, c):
@@ -245,11 +289,14 @@
             tmp[...] = jnp.where(mask, o, tmp[...])
             return c
 
-        lax.fori_loop(0, HEADS, head, 0)
+        lax.fori_loop(0, HEADS, head, 0, unroll=HEADS)
         mixed[rows, :] = tmp[...].astype(BF16)
+    pump("ao")
     h[2] = h[1] + dot(mixed[...], mat(ATTN_AT + 3), 1, 1)
     residual(1, 3, 2, 3)
+    pump("n5")
     norm_forward(h.at[3], 5, False, 5)
+    pump("head")
 
     dion_ref[...] = jnp.zeros_like(dion_ref)
     loss = jnp.zeros((), F32)
@@ -310,11 +357,15 @@
 
     def conv_backward(layer, keep):
         turned = acts[keep].T
+        pump(f"w{layer}a")
+        for k, (r, c) in enumerate(OFFSETS):
+            put(CONV_AT[layer] + k, dot(turned, tap(pads, -r, -c)))
+            if CONV_AT[layer] + k + 1 in SPLITS:
+                pump(f"w{layer}b")
+        pump(f"d{layer}")
         acc = None
         for k, (r, c) in enumerate(OFFSETS):
-            there = tap(pads, -r, -c)
-            put(CONV_AT[layer] + k, dot(turned, there))
-            term = dot(there, mat(CONV_AT[layer] + k), 1, 1)
+            term = dot(tap(pads, -r, -c), mat(CONV_AT[layer] + k), 1, 1)
             acc = term if acc is None else acc + term
         smallf[...] = acc
 
@@ -338,7 +389,7 @@
 
     def residual_backward(layer, slot, src, last_one):
         conv_backward(2 * layer + 1, slot + 1)
-        done(4 if layer == 1 else 1)
+        pump(f"b{slot + 1}")
         norm_backward(c1s.at[layer], slot + 1, smallf, only_shifts)
         sums = []
         for n in range(IMGS):
@@ -349,17 +400,20 @@
         feats3 = jnp.concatenate([feats.astype(F32)] * 3, axis=0).astype(BF16)
         put(TIME_AT[layer], dot(feats3, stack, 0, 0))
         conv_backward(2 * layer, slot)
-        done(3 if layer == 1 else 0)
+        pump(f"b{slot}")
         norm_backward(h.at[src], slot, smallf, add_flow(False))
 
+    pump("b5")
     norm_backward(h.at[3], 5, flow, set_flow)
     residual_backward(1, 3, 2, False)
 
+    pump("do")
     dy = flow[...].astype(BF16)
     put(ATTN_AT + 3, dot(dy.T, mixed[...]))
     dqkv[3] = dot(dy, mat(ATTN_AT + 3)).astype(BF16)
     for n in range(IMGS):
         rows = slice(n * POS, (n + 1) * POS)
+        pump(f"bt{n}")
         for j in range(3):
             smallf[j % 2 * POS : j % 2 * POS + POS, :] = jnp.zeros((POS, CH), F32)
         tmp[...] = jnp.zeros_like(tmp)
@@ -376,10 +430,11 @@
             smallf[POS:, :] += dot(p.astype(BF16), do, 0, 0)
             return c
 
-        lax.fori_loop(0, HEADS, head, 0)
+        lax.fori_loop(0, HEADS, head, 0, unroll=HEADS)
         dqkv[0, rows, :] = (tmp[...] * scale).astype(BF16)
         dqkv[1, rows, :] = (smallf[0:POS, :] * scale).astype(BF16)
         dqkv[2, rows, :] = smallf[POS:, :].astype(BF16)
+    pump("proj")
     turned = acts[2].T
     acc = None
     for j in range(3):
@@ -387,9 +442,10 @@
         term = dot(dqkv[j], mat(ATTN_AT + j), 1, 1)
         acc = term if acc is None else acc + term
     smallf[...] = acc
-    done(2)
+    pump("b2")
     norm_backward(h.at[1], 2, smallf, add_flow(True))
     residual_backward(0, 0, 0, True)
+    pump("win")
     for n in range(IMGS):
         rows = slice(n * POS, (n + 1) * POS)
         dion_ref[0:16, :] += dot(begin[16 * n : 16 * n + 16], flow[rows, :].astype(BF16))
@@ -419,8 +475,9 @@
         dmats[m] = value
 
     train(
-        x_ref[...], z_ref[...], mine_ref[...], when_ref, feat_ref, flag_ref[0, 0], flag_ref[0, 1],
-        ion_ref[...].T, lambda m: mats[m], put, lambda chunk: None, lambda chunk: None,
+        x_ref[...], z_ref[...], mine_ref[...], when_ref[0:IMGS, 0:1], feat_ref[...].astype(BF16),
+        flag_ref[0, 0], flag_ref[0, 1],
+        lambda: ion_ref[...].T, lambda m: mats[m], put, lambda name: None,
         dion_ref, scal_ref, *work,
     )
 
@@ -447,9 +504,9 @@
 
 def fused_kernel(
     micro, batch,
-    ot_ref, when_ref, feat_ref, own_ref, ownion_ref,
+    order_ref, when_ref, images_ref, noises_ref, freq_ref, conv_ref, time_ref, attn_ref, io_ref, norm_ref,
     grads_ref, gion_ref, total_ref,
-    mats, dmats, other, land, otbuf, otwide, xz, ionbuf, dion, diont, ionr, scal, scalr,
+    mats, dmats, other, give, land, ottmp, ot_ref, otbuf, otwide, xz, ionbuf, dion, diont, ionr, scal, scalr,
     s1q, s1r, s2q, s2r, zq, zr, expo, kept, gother,
     ot_s, ot_r, ion_s, ion_r, g_s, g_r, r_s, r_r, d_s, d_r, n_s, n_r,
     *work,
@@ -483,36 +540,81 @@
         return carry
 
     lax.fori_loop(1, DEVICES, greet, 0)
+
+    def wide(v):
+        v = v.astype(BF16).astype(F32)
+        none = jnp.zeros_like(v)
+        return jnp.where(c == 0, jnp.concatenate([v, none], axis=1), jnp.concatenate([none, v], axis=1)).astype(BF16)
+
+    def pack(m, whole):
+        mats[m, x, z, y, c] = wide(jnp.where(c == 0, whole[0:16], whole[16:32]))
+        give[m] = wide(jnp.where(c == 0, whole[16:32], whole[0:16]))
+
+    for layer, at in enumerate(CONV_AT):
+
+        def pack_step(k, carry):
+            pack(at + k, conv_ref[layer, k])
+            return carry
+
+        lax.fori_loop(0, 9, pack_step, 0)
+    for layer, at in enumerate(TIME_AT):
+        pack(at, time_ref[layer])
+    for j in range(4):
+        pack(ATTN_AT + j, attn_ref[:, j, :])
+
+    turn = mp - (mp // micro) * (mp - micro + 1)
+    row = lax.broadcasted_iota(jnp.int32, (8, images_ref.shape[0]), 0)
+    column = lax.broadcasted_iota(jnp.int32, (8, images_ref.shape[0]), 1)
+    pick = jnp.zeros(row.shape, F32)
+    for n in range(IMGS):
+        pick = jnp.where((row == n) & (column == order_ref[turn * IMGS + n]), 1.0, pick)
+    own_x = dot(pick.astype(BF16), images_ref[...])
+    own_z = noises_ref[turn].astype(F32)
+    lines = SUB * POS // 128
+    for k in range(lines):
+        ottmp[2 * IMGS * k : 2 * IMGS * k + IMGS, :] = own_x[0:IMGS, 128 * k : 128 * k + 128]
+        ottmp[2 * IMGS * k + IMGS : 2 * IMGS * (k + 1), :] = own_z[:, 128 * k : 128 * k + 128]
+    ot_ref[...] = ottmp[...].astype(BF16)
+    io = io_ref[...].reshape(1, io_ref.shape[0])
+    norm = norm_ref[...].reshape(1, norm_ref.shape[0])
+    zero_row = jnp.zeros((1, 128), F32)
+    packed = []
+    for r in range(8):
+        gap = zero_row[:, 0 : 16 - SUB]
+        at = 2 * SUB * r
+        packed.append(
+            jnp.concatenate(
+                [io[:, at : at + SUB], gap, io[:, at + SUB : at + 2 * SUB], gap,
+                 norm[:, SUB * r : SUB * r + SUB], zero_row[:, 0 : 128 - 32 - SUB]], axis=1
+            )
+        )
+    ionbuf[x, c, z, y] = jnp.concatenate(packed, axis=0).astype(BF16).astype(F32)
     pl.semaphore_wait(barrier, DEVICES - 1)
 
-    zero_copy = remote(own_ref.at[:, pl.ds((1 - c) * 16, 16)], land, g_s.at[0, 0], g_r.at[0, 0], sibling)
-    zero_copy.start()
-
+    zero_copy = remote(give, land, g_s.at[0, 0], g_r.at[0, 0], sibling)
     def ot_copy(j):
         there = (dp + j) % (Z * Y)
         return remote(ot_ref, otbuf.at[dp], ot_s.at[j], ot_r.at[j], (there, mp))
 
-    for j in range(1, Z * Y):
-        ot_copy(j).start()
-    otbuf[dp] = ot_ref[...]
-
-    def ion_copy(j):
-        return remote(ownion_ref, ionbuf.at[flat], ion_s.at[j], ion_r.at[j], from_flat((flat + j) % DEVICES))
-
-    def ion_start(j, carry):
-        ion_copy(j).start()
+    def ion_z(j):
+        part = ionbuf.at[x, c, z, y]
+        return remote(part, part, ion_s.at[j], ion_r.at[j], place((z + j) % Z, y, x, c))
+
+    def ion_u(core):
+        part = ionbuf.at[x, c, :, y]
+        return remote(part, part, ion_s.at[4], ion_r.at[4], first)
+
+    def ion_v(core):
+        part = ionbuf.at[x, 0] if core == 0 else ionbuf.at[:, 1, :, y]
+        return remote(part, part, ion_s.at[5], ion_r.at[5], second)
+
+    def ion_c(core):
+        part = ionbuf.at[:, c]
+        return remote(part, part, ion_s.at[6], ion_r.at[6], sibling)
+
+    def merge(m, carry):
+        mats[m, x, z, y, c] = mats[m, x, z, y, c] + land[m]
         return carry
-
-    lax.fori_loop(1, DEVICES, ion_start, 0)
-    ionbuf[flat] = ownion_ref[...]
-
-    zero_copy.wait()
-
-    def merge(m, carry):
-        mats[m, x, z, y, c] = own_ref[m, pl.ds(pl.multiple_of(c * 16, 16), 16), :] + land[m]
-        return carry
-
-    lax.fori_loop(0, MATS, merge, 0)
 
     def span(i):
         return pl.ds(CHUNKS[i][0], CHUNKS[i][1])
@@ -529,6 +631,18 @@
         part = mats.at[span(i), x, :, :, 0] if core == 0 else mats.at[span(i), :, :, y, 1]
         return remote(part, part, g_s.at[i + 1, 5], g_r.at[i + 1, 5], second)
 
+    def e_copy(i, j):
+        part = mats.at[span(i), :, z, :, c]
+        return remote(part, part, g_s.at[i + 1, j], g_r.at[i + 1, j], place((z + j) % Z, y, x, c))
+
+    def a_copy(i):
+        part = mats.at[span(i), x, z, y, c]
+        return remote(part, part, g_s.at[i + 1, 4], g_r.at[i + 1, 4], first)
+
+    def b_copy(i, core):
+        part = mats.at[span(i), x, z, :, 0] if core == 0 else mats.at[span(i), :, z, y, 1]
+        return remote(part, part, g_s.at[i + 1, 5], g_r.at[i + 1, 5], second)
+
     def c_copy(i):
         part = mats.at[span(i), :, :, :, c]
         return remote(part, part, g_s.at[i + 1, 6], g_r.at[i + 1, 6], sibling)
@@ -537,49 +651,90 @@
         for core in range(C):
             pl.when(c == core)(functools.partial(act, core))
 
-    def gather_step(stage, i):
-        if i < 0 or i >= len(CHUNKS):
-            return
-        if stage == 0:
-            for j in range(1, Z):
-                z_copy(i, j).start()
-        elif stage == 1:
-            for j in range(1, Z):
-                z_copy(i, j).wait()
+    def start_all(copies):
+        for copy in copies:
+            copy.start()
+
+    def wait_all(copies):
+        for copy in copies:
+            copy.wait()
+
+    peers = range(1, Z)
+
+    def gather_step(kind, i):
+        if kind == "A":
+            a_copy(i).start()
+        elif kind == "B":
+            a_copy(i).wait()
+            on_core(lambda core: b_copy(i, core).start())
+        elif kind == "E":
+            on_core(lambda core: b_copy(i, core).wait())
+            start_all(e_copy(i, j) for j in peers)
+        elif kind == "Z":
+            start_all(z_copy(i, j) for j in peers)
+        elif kind == "U":
+            wait_all(z_copy(i, j) for j in peers)
             u_copy(i).start()
-        elif stage == 2:
+        elif kind == "V":
             u_copy(i).wait()
             on_core(lambda core: v_copy(i, core).start())
-        elif stage == 3:
-            on_core(lambda core: v_copy(i, core).wait())
+        elif kind == "C":
+            if i in EARLY:
+                wait_all(e_copy(i, j) for j in peers)
+            else:
+                on_core(lambda core: v_copy(i, core).wait())
             c_copy(i).start()
-        else:
+        elif kind == "W":
             c_copy(i).wait()
 
-    for i in range(len(CHUNKS)):
-        gather_step(0, i)
-    gather_step(1, 0)
-
-    for j in range(1, Z * Y):
-        ot_copy(j).wait()
+    def other_step(kind):
+        if kind == "zero":
+            zero_copy.start()
+        elif kind == "merge":
+            zero_copy.wait()
+            lax.fori_loop(0, MATS, merge, 0, unroll=6)
+        elif kind == "ot":
+            start_all(ot_copy(j) for j in range(1, Z * Y))
+            otbuf[dp] = ot_ref[...]
+        elif kind == "otw":
+            wait_all(ot_copy(j) for j in range(1, Z * Y))
+        elif kind == "iz":
+            start_all(ion_z(j) for j in peers)
+        elif kind == "iu":
+            wait_all(ion_z(j) for j in peers)
+            ion_u(0).start()
+        elif kind == "iv":
+            ion_u(0).wait()
+            on_core(lambda core: ion_v(core).start())
+        elif kind == "ic":
+            on_core(lambda core: ion_v(core).wait())
+            ion_c(0).start()
+        elif kind == "iw":
+            ion_c(0).wait()
+
+    def do(steps):
+        for kind in steps:
+            if kind[1:].isdigit():
+                i = int(kind[1:])
+                if kind[0] in "RSTYXF":
+                    reduce_step(kind[0], i)
+                else:
+                    gather_step(kind[0], i)
+            else:
+                other_step(kind)
+
+    def pump(name):
+        do(PLAN.get(name, ()))
+
+    pump("start")
     rows = ot_ref.shape[0]
     for j in range(Z * Y):
         otwide[pl.ds(j * rows, rows), :] = otbuf[j].astype(F32)
-    lines = rows // (2 * IMGS)
     for r in range(2 * IMGS):
         for k in range(lines):
             xz[r // IMGS, (r % IMGS) * Z * Y : (r % IMGS + 1) * Z * Y, k * 128 : (k + 1) * 128] = otwide[
-                pl.ds(r * lines + k, Z * Y, stride=rows), :
+                pl.ds(k * 2 * IMGS + r, Z * Y, stride=rows), :
             ]
-    gather_step(2, 0)
-    gather_step(1, 1)
-
-    def ion_wait(j, carry):
-        ion_copy(j).wait()
-        return carry
-
-    lax.fori_loop(1, DEVICES, ion_wait, 0)
-    ion = ionbuf[...].reshape(CH, 128).T
     spot = lax.broadcasted_iota(jnp.int32, (8, batch), 0)
     column = lax.broadcasted_iota(jnp.int32, (8, batch), 1)
     mine = jnp.where((column == spot * (Z * Y) + dp) & (spot < IMGS), 1.0, 0.0)
@@ -591,12 +746,6 @@
     def put(m, value):
         for k in range(X):
             dmats[m, k] = value[:, 128 * k : 128 * k + 128].reshape(Z, Y, C, 16, 128)
-
-    def ready(i):
-        gather_step(3, i)
-        gather_step(2, i + 1)
-        gather_step(1, i + 2)
-        gather_step(4, i)
 
     mine_a = x * (1 - c) + y * c
     mine_b = y * (1 - c) + x * c
@@ -665,7 +814,7 @@
                 s1q[start + k * 8 + t] = coded(tile, power)
             return carry
 
-        lax.fori_loop(0, count, step, 0)
+        lax.fori_loop(0, count, step, 0, unroll=True)
         powers(s1q, start + count * 8)
         one_copy(i).start()
 
@@ -689,7 +838,7 @@
                 s2q[start + k * 4 + t] = coded(tile, power)
             return carry
 
-        lax.fori_loop(0, count, step, 0)
+        lax.fori_loop(0, count, step, 0, unroll=True)
         powers(s2q, start + count * 4)
         two_copy(i).start()
 
@@ -721,7 +870,7 @@
             kept[m] = tile(z)
             return carry
 
-        lax.fori_loop(0, count, step, 0)
+        lax.fori_loop(0, count, step, 0, unroll=True)
         for j in range(1, Z):
             powers(zq.at[j - 1], start + count)
         for j in range(1, Z):
@@ -743,36 +892,48 @@
             kept[m] = total
             return carry + total * total
 
-        square = lax.fori_loop(0, count, step, jnp.zeros((16, 128), F32))
+        square = lax.fori_loop(0, count, step, jnp.zeros((16, 128), F32), unroll=True)
         four_copy(i).start()
         return square
 
     squares = []
-    order = (4, 3, 2, 1, 0)
-
-    def reduce_step(stage, turn):
-        if turn < 0 or turn >= len(order):
-            return
-        i = order[turn]
-        if stage == 0:
+
+    def reduce_step(kind, i):
+        if kind == "R":
             r_copy(i).start()
-        elif stage == 1:
+        elif kind == "S":
             stage_one(i)
-        elif stage == 2:
+        elif kind == "T":
             stage_two(i)
-        elif stage == 3:
+        elif kind == "Y":
             stage_three(i)
+        elif kind == "X":
+            squares.append(stage_four(i))
         else:
-            squares.append(stage_four(i))
-
-    def done(i):
-        turn = order.index(i)
-        for stage in range(5):
-            reduce_step(stage, turn - stage)
-
+            finish(i)
+
+    def finish(i):
+        four_copy(i).wait()
+
+        def step(k, carry):
+            m = CHUNKS[i][0] + k
+            for half in range(C):
+                tile = jnp.where(c == half, kept[m], gother[m])
+                grads_ref[m, half * 16 : half * 16 + 16, :] = jnp.where(c == 0, tile[:, 0:64], tile[:, 64:128])
+            return carry
+
+        lax.fori_loop(0, CHUNKS[i][1], step, 0, unroll=True)
+
+    seat = lax.broadcasted_iota(jnp.int32, (8, 1), 0)
+    times = jnp.zeros((8, 1), F32)
+    for n in range(IMGS):
+        index = when_ref[pl.ds(turn, 1), n : n + 1].astype(F32)
+        times = jnp.where(seat == n, (index + 0.5) / NT, times)
+    angles = 1000.0 * times * freq_ref[...]
+    feats = jnp.where(seat < IMGS, jnp.concatenate([jnp.sin(angles), jnp.cos(angles)], axis=1), 0.0).astype(BF16)
     train(
-        xz[0].astype(BF16), xz[1].astype(BF16), mine, when_ref, feat_ref, active, 2.0 / (micro * batch),
-        ion, mat, put, ready, done, dion, scal, *work,
+        xz[0].astype(BF16), xz[1].astype(BF16), mine, times[0:IMGS], feats, active, 2.0 / (micro * batch),
+        lambda: ionbuf[...].reshape(CH, 128).T, mat, put, pump, dion, scal, *work,
     )
 
     diont[...] = jnp.concatenate([dion[...], jnp.zeros((128 - 48, CH), F32)], axis=0).T.reshape(DEVICES, 8, 128)
@@ -787,9 +948,7 @@
 
     lax.fori_loop(1, DEVICES, dion_start, 0)
     ionr[flat] = diont[flat]
-    for turn in range(len(order), len(order) + 4):
-        for stage in range(5):
-            reduce_step(stage, turn - stage)
+    pump("tail")
 
     def dion_wait(j, carry):
         dion_copy(j).wait()
@@ -823,25 +982,21 @@
         return carry
 
     lax.fori_loop(1, DEVICES, n_start, 0)
-    for i in order:
-        four_copy(i).wait()
-
-    def finish(m, carry):
-        for half in range(C):
-            tile = jnp.where(c == half, kept[m], gother[m])
-            grads_ref[m, half * 16 : half * 16 + 16, :] = jnp.where(c == 0, tile[:, 0:64], tile[:, 64:128])
-        return carry
-
-    lax.fori_loop(0, MATS, finish, 0)
+    pump("end")
     lax.fori_loop(1, DEVICES, n_wait, 0)
     total_ref[...] = jnp.sum(scalr[...], axis=0)
 
 
-def fused_network(micro, batch, ot, when, feat, own, ownion):
+def fused_network(micro, batch, order, when, images, noises, conv, time, attn, io, norm):
     whole = pl.BlockSpec(memory_space=pltpu.VMEM)
+    scalar = pl.BlockSpec(memory_space=pltpu.SMEM)
     blocks = (X, Z, Y)
+    rows = 2 * IMGS * SUB * POS // 128
     dma = pltpu.SemaphoreType.DMA
     count = len(CHUNKS)
+    half = CH // 2
+    freq = np.exp(np.float32(-math.log(10000.0)) * np.arange(half, dtype=np.float32) / np.float32(half))
+    freq = jnp.asarray(freq.reshape(1, half))
     return pl.pallas_call(
         functools.partial(fused_kernel, micro, batch),
         out_shape=(
@@ -849,17 +1004,20 @@
             jax.ShapeDtypeStruct((8, 128), F32),
             jax.ShapeDtypeStruct((8, 128), F32),
         ),
-        in_specs=[whole] * 5,
+        in_specs=[scalar] + [whole] * 9,
         out_specs=(whole, whole, whole),
         scratch_shapes=[
             pltpu.VMEM((MATS,) + blocks + (C, 16, 128), BF16),
             pltpu.VMEM((MATS,) + blocks + (C, 16, 128), F32),
             pltpu.VMEM((MATS,) + blocks + (16, 128), F32),
             pltpu.VMEM((MATS, 16, 128), BF16),
-            pltpu.VMEM((Z * Y,) + ot.shape, BF16),
-            pltpu.VMEM((Z * Y * ot.shape[0], 128), F32),
+            pltpu.VMEM((MATS, 16, 128), BF16),
+            pltpu.VMEM((rows, 128), F32),
+            pltpu.VMEM((rows, 128), BF16),
+            pltpu.VMEM((Z * Y, rows, 128), BF16),
+            pltpu.VMEM((Z * Y * rows, 128), F32),
             pltpu.VMEM((2, batch, SUB * POS), F32),
-            pltpu.VMEM((DEVICES, 8, 128), F32),
+            pltpu.VMEM((X, C, Z, Y, 8, 128), F32),
             pltpu.VMEM((48, CH), F32),
             pltpu.VMEM((DEVICES, 8, 128), F32),
             pltpu.VMEM((DEVICES, 8, 128), F32),
@@ -875,7 +1033,7 @@
             pltpu.VMEM((MATS, 16, 128), F32),
             pltpu.VMEM((MATS, 16, 128), F32),
             dma((Z * Y,)), dma((Z * Y,)),
-            dma((DEVICES,)), dma((DEVICES,)),
+            dma((7,)), dma((7,)),
             dma((count + 1, 7)), dma((count + 1, 7)),
             dma((count, 7)), dma((count, 7)),
             dma((DEVICES,)), dma((DEVICES,)),
@@ -884,7 +1042,7 @@
         compiler_params=pltpu.CompilerParams(
             vmem_limit_bytes=60 * 2**20, collective_id=0, has_side_effects=True
         ),
-    )(ot, when, feat, own, ownion)
+    )(order, when, images, noises, freq, conv, time, attn, io, norm)
 
 
 def time_features(time_index):
@@ -904,8 +1062,69 @@
     return (weight, first, second, average)
 
 
+def adam_kernel(grads_ref, gion_ref, total_ref, *refs):
+    step = pl.program_id(0)
+    old, new = refs[:20], refs[20:40]
+    loss_ref, cost_ref, norm_ref = refs[40:]
+    norm = jnp.sqrt(total_ref[0:1, 0:1])
+    scale = CLIP_NORM / jnp.maximum(norm, CLIP_NORM)
+
+    def update(kind, at, gradient):
+        got = adam_update(*[old[5 * part + kind][at] for part in range(4)], gradient * scale, RATES[kind])
+        for part in range(4):
+            new[5 * part + kind][at] = got[part]
+
+    for layer, start in enumerate(CONV_AT):
+
+        @pl.when(step == layer)
+        def conv_step():
+            update(1, (0,), grads_ref[start : start + 9])
+
+    @pl.when(step == 0)
+    def others():
+        for layer, start in enumerate(TIME_AT):
+            update(2, (layer,), grads_ref[start])
+        for j in range(4):
+            update(3, (slice(None), j), grads_ref[ATTN_AT + j])
+        tile = gion_ref[...]
+        own = old[0].shape[0] // (2 * SUB)
+        for kind, pieces in ((0, (0, 16)), (4, (32,))):
+            flat = [tile[r : r + 1, at : at + SUB] for r in range(own) for at in pieces]
+            flat = jnp.concatenate(flat, axis=1)
+            got = adam_update(
+                *[old[5 * part + kind][...].reshape(flat.shape) for part in range(4)], flat * scale, RATES[kind]
+            )
+            for part in range(4):
+                new[5 * part + kind][...] = got[part].reshape(old[kind].shape)
+        micro = loss_ref.shape[0]
+        for m in range(micro):
+            loss_ref[m] = total_ref[0, 1 + m]
+            cost_ref[m] = total_ref[0, 1 + micro + m]
+        norm_ref[0] = norm[0, 0]
+
+
+def adam(micro, grads, gion, total, state):
+    whole = pl.BlockSpec(memory_space=pltpu.VMEM)
+    scalar = pl.BlockSpec(memory_space=pltpu.SMEM)
+
+    def spec(v):
+        if v.ndim == 4:
+            return pl.BlockSpec((1,) + v.shape[1:], lambda i: (i, 0, 0, 0))
+        return pl.BlockSpec(v.shape, lambda i: (0,) * v.ndim)
+
+    return pl.pallas_call(
+        adam_kernel,
+        grid=(len(CONV_AT),),
+        out_shape=tuple(jax.ShapeDtypeStruct(v.shape, F32) for v in state)
+        + (jax.ShapeDtypeStruct((micro,), F32),) * 2
+        + (jax.ShapeDtypeStruct((1,), F32),),
+        in_specs=[spec(v) for v in (grads, gion, total)] + [spec(v) for v in state],
+        out_specs=tuple(spec(v) for v in state) + (scalar,) * 3,
+        compiler_params=pltpu.CompilerParams(vmem_limit_bytes=60 * 2**20),
+    )(grads, gion, total, *state)
+
+
 def pack_mats(conv, time, attn):
-    kinds = 9
     return jnp.concatenate(
         [time[0:1], conv[0], conv[1], attn.transpose(1, 0, 2), time[1:2], conv[2], conv[3]], axis=0
     )
@@ -939,8 +1158,16 @@
     micro, count, depth = noises.shape
     batch = count * lax.axis_size("dp")
     turn = jnp.minimum(rank, micro - 1)
-    mats = pack_mats(conv_weight, time_weight, attn_weight).astype(BF16)
-    ion = pack_small(io_weight, norm_param).astype(BF16)
+    weights = (io_weight, conv_weight, time_weight, attn_weight, norm_param)
+    firsts = (io_first, conv_first, time_first, attn_first, norm_first)
+    seconds = (io_second, conv_second, time_second, attn_second, norm_second)
+    averages = (io_average, conv_average, time_average, attn_average, norm_average)
+    if fused:
+        grads, gion, total = fused_network(
+            micro, batch, order, time_index, images, noises, conv_weight, time_weight, attn_weight, io_weight, norm_param
+        )
+        out = adam(micro, grads, gion, total, weights + firsts + seconds + averages)
+        return out[:22] + (out[22].reshape(()),)
     chosen = lax.dynamic_slice_in_dim(order, turn * count, count, 0)
     own_x = jnp.take(images, chosen, axis=0)
     own_z = lax.dynamic_index_in_dim(noises, turn, 0, keepdims=False)
@@ -948,32 +1175,24 @@
     feat = jnp.pad(time_features(when).astype(BF16).astype(F32), ((0, 8 - count), (0, 0)))
     times = (when.astype(F32) + 0.5) / NT
     times = jnp.pad(jnp.broadcast_to(times[:, None], (count, 128)), ((0, 8 - count), (0, 0)))
-    if fused:
-        ot = jnp.concatenate([own_x, own_z]).reshape(-1, 128)
-        none = jnp.zeros_like(mats)
-        low = rank % 2 == 0
-        own = jnp.concatenate([jnp.where(low, mats, none), jnp.where(low, none, mats)], axis=2)
-        dmats, dion, total = fused_network(micro, batch, ot, times, feat, own, ion.astype(F32))
-        total_sq = total[0, 0]
-        loss_sum = total[0, 1 : 1 + micro]
-        cost_sum = total[0, 1 + micro : 1 + 2 * micro]
-    else:
-        mats = lax.all_gather(lax.all_gather(mats, "dp", axis=1, tiled=True), "mp", axis=2, tiled=True)
-        ion = lax.all_gather(ion, ("mp", "dp"), axis=0, tiled=True).astype(F32)
-        both = lax.all_gather(jnp.stack([own_x, own_z]), "dp", axis=1, tiled=True)
-        spot = jnp.arange(8)[:, None]
-        mine = ((jnp.arange(batch)[None, :] == place * count + spot) & (spot < count)).astype(F32)
-        active = (rank < micro).astype(F32)
-        flag = jnp.stack([active, jnp.float32(2.0 / (micro * batch))]).reshape(1, 2)
-        dmats, dion, scal = local_network(both[0], both[1], mine, times, feat, flag, mats, ion)
-        dmats = lax.psum_scatter(dmats, "dp", scatter_dimension=1, tiled=True)
-        dmats = lax.psum_scatter(dmats, "mp", scatter_dimension=2, tiled=True)
-        dion = lax.psum_scatter(dion.T, ("mp", "dp"), scatter_dimension=0, tiled=True)
-        hot = (jnp.arange(micro) == rank).astype(F32)
-        squares = jnp.sum(dmats * dmats) + jnp.sum(dion * dion)
-        total_sq, loss_sum, cost_sum = lax.psum(
-            (squares, hot * scal[0, 0], jnp.where(place == 0, hot * scal[0, 1], 0.0)), ("dp", "mp")
-        )
+    mats = pack_mats(conv_weight, time_weight, attn_weight).astype(BF16)
+    mats = lax.all_gather(lax.all_gather(mats, "dp", axis=1, tiled=True), "mp", axis=2, tiled=True)
+    ion = pack_small(io_weight, norm_param).astype(BF16)
+    ion = lax.all_gather(ion, ("mp", "dp"), axis=0, tiled=True).astype(F32)
+    both = lax.all_gather(jnp.stack([own_x, own_z]), "dp", axis=1, tiled=True)
+    spot = jnp.arange(8)[:, None]
+    mine = ((jnp.arange(batch)[None, :] == place * count + spot) & (spot < count)).astype(F32)
+    active = (rank < micro).astype(F32)
+    flag = jnp.stack([active, jnp.float32(2.0 / (micro * batch))]).reshape(1, 2)
+    dmats, dion, scal = local_network(both[0], both[1], mine, times, feat, flag, mats, ion)
+    dmats = lax.psum_scatter(dmats, "dp", scatter_dimension=1, tiled=True)
+    dmats = lax.psum_scatter(dmats, "mp", scatter_dimension=2, tiled=True)
+    dion = lax.psum_scatter(dion.T, ("mp", "dp"), scatter_dimension=0, tiled=True)
+    hot = (jnp.arange(micro) == rank).astype(F32)
+    squares = jnp.sum(dmats * dmats) + jnp.sum(dion * dion)
+    total_sq, loss_sum, cost_sum = lax.psum(
+        (squares, hot * scal[0, 0], jnp.where(place == 0, hot * scal[0, 1], 0.0)), ("dp", "mp")
+    )
     grad_norm = jnp.sqrt(total_sq)
     scale = CLIP_NORM / jnp.maximum(grad_norm, CLIP_NORM)
     conv_grad, time_grad, attn_grad = unpack_mats(dmats)
@@ -984,10 +1203,6 @@
         attn_grad,
         dion[:, 32 : 32 + SUB].reshape(-1),
     )
-    weights = (io_weight, conv_weight, time_weight, attn_weight, norm_param)
-    firsts = (io_first, conv_first, time_first, attn_first, norm_first)
-    seconds = (io_second, conv_second, time_second, attn_second, norm_second)
-    averages = (io_average, conv_average, time_average, attn_average, norm_average)
     results = [
         adam_update(weights[kind], firsts[kind], seconds[kind], averages[kind], grads[kind] * scale, RATES[kind])
         for kind in range(5)

time: 146 us -> 113 us (0.77)
  local copies, waits for them, and re-layouts: 12.9 us -> 1.34 us
  other arithmetic: 9.29 us -> 0 us
  Pallas kernels: 120 us -> 111 us
  between operations: 2.89 us -> 0.85 us
    pallas_call x1, Pallas kernels: 120 us -> 105 us  [fused_network(): pl.pallas_call(functools.partial(fused_kernel, micro, batch), out_shape=(...]
    pallas_call x0 -> x1, Pallas kernels: none -> 5.87 us  [adam(): pl.pallas_call(adam_kernel, grid=(len(CONV_AT),), out_shape=tuple((jax.Sh...]
    unnamed x59 -> x1, local copies, waits for them, and re-layouts: 6.46 us -> 1.34 us
    add x6 -> x0, other arithmetic: 4.8 us -> none  [the longest x5 4.62 us: adam_update(): average = EMA_DECAY * average + (1 - EMA_DECAY) * weight]
    squeeze x2 -> x0, local copies, waits for them, and re-layouts: 2.06 us -> none  [the longest x1 1.34 us: body(): cost_sum = total[0, 1 + micro:1 + 2 * micro]]
    slice x3 -> x0, local copies, waits for them, and re-layouts: 2 us -> none  [the longest x1 1.26 us: body(): total_sq = total[0, 0]]
where the time goes in v3:
time: 113 us
  Pallas kernels  111 us (98%)
  local copies, waits for them, and re-layouts  1.34 us (1%)
    pallas_call x1, Pallas kernels, fused_network(): pl.pallas_call(functools.partial(fused_kernel, micro, batch), out_shape=(...  105 us
    pallas_call x1, Pallas kernels, adam(): pl.pallas_call(adam_kernel, grid=(len(CONV_AT),), out_shape=tuple((jax.Sh...  5.87 us

profile of v3, /device:TPU:0, one launch (start us, length us, event | category | flops | bytes accessed | tf_op | source)
XLA Modules:
  0.0 112.7 jit_solution(13248366248655822987)
XLA Ops:
  0.7 1.3 %copy.48.when_ref = s32[3,2]{1,0:T(4,128)} copy(s32[3,2]{0,1:T(2,128)} %param.28) | data formatting | bytes 48 | tf_op args[3]
  2.0 104.6 %shard_map.416 = (f32[42,32,64]{2,1,0:T(8,128)}, f32[8,128]{1,0:T(8,128)}, f32[8,128]{1,0:T(8,128)}) custom-call(s32[6]{0:T(128)} %order_ref.1, s32[3,2]{1,0:T(4,128)} %copy.48.when_ref, bf16[6,3072]{1,0:T(8,128)(2,1)} %images_ref.1, bf16[3,2,3072]{2,1,0:T(2,128)(2,1)} %noises_ref.1, f32[1,128]{1,0:T(1,128)} %constant.2.clone.freq_ref, ...), custom_call_target="tpu_custom_call" | custom-call | tf_op jit(solution)/shard_map/pallas_call | solution.py:1000
  106.7 5.9 %shard_map.417 = (f32[192]{0:T(256)}, f32[4,9,32,64]{3,2,1,0:T(8,128)}, f32[2,32,64]{2,1,0:T(8,128)}, f32[32,4,64]{2,1,0:T(4,128)}, f32[96]{0:T(128)}, /*index=5...) custom-call(f32[42,32,64]{2,1,0:T(8,128)} %get-tuple-element.49.grad, ...), custom_call_target="tpu_custom_call" | custom-call | tf_op jit(solution)/shard_map/pallas_call | solution.py:1115

commit v4 on v3

--- a/solution.py
+++ b/solution.py
@@ -25,42 +25,40 @@
 ATTN_AT = 19
 CHUNKS = ((0, 5), (5, 5), (10, 5), (15, 4), (19, 4), (23, 5), (28, 5), (33, 5), (38, 4))
 SPLITS = (5, 15, 28, 38)
-EARLY = (4, 8)
+EARLY = (3, 8)
 PLAN = {
-    "start": ("zero", "ot", "merge", "iz", "A4", "A8", "Z0", "Z1", "Z2", "Z3", "Z5", "Z6", "B4", "B8", "Z7", "iu",
-        "otw"),
-    "sink": ("E4", "iv", "E8", "U0"),
-    "h0": ("ic", "U1", "U2", "iw"),
-    "n0": ("V0", "U3"),
-    "c0": ("U5", "V1", "V2", "U6", "C0", "U7", "V3", "V5", "C1", "W0", "W1"),
-    "n1": ("C4", "C2", "V6"),
-    "c1": ("V7", "C3", "W2", "W3"),
-    "n2": ("C8", "C5"),
-    "qkv": ("C6", "W4"),
-    "at1": ("C7",),
-    "c2": ("W5", "W6"),
+    "start": ("zero", "merge", "Z1", "Z7", "A3", "ot", "A8", "Z0", "Z2", "iz", "U1", "B8", "U7", "iu", "B3", "Z5",
+        "Z4", "U0", "Z6", "otw", "V1"),
+    "sink": ("U2", "iv", "U5", "E3", "V0", "U4", "V2", "U6", "ic", "iw", "C1", "V4"),
+    "h0": ("E8", "V5", "C0"),
+    "n0": ("V6", "C3", "W1", "C2", "V7"),
+    "c0": ("W0",),
+    "n1": ("C4",),
+    "c1": ("W3", "W2"),
+    "n2": ("C5",),
+    "qkv": ("W4",),
+    "at0": ("C6",),
+    "ao": ("C8", "W5"),
+    "n3": ("C7",),
+    "c2": ("W6",),
     "c3": ("W7", "W8"),
     "w3b": ("R7",),
     "d3": ("R8",),
-    "w2a": ("S7",),
-    "w2b": ("R5", "S8"),
-    "d2": ("R6",),
-    "b3": ("S5",),
-    "do": ("T7", "S6"),
-    "bt1": ("T8", "T5"),
-    "proj": ("Y7",),
-    "b2": ("R4", "Y8", "T6", "Y5"),
-    "w1a": ("S4",),
-    "w1b": ("R2",),
-    "d1": ("R3", "Y6", "X7"),
-    "b1": ("S2", "T4", "S3", "F7", "X8", "X5"),
-    "w0a": ("F8", "F5"),
-    "w0b": ("R0", "X6"),
-    "d0": ("R1", "T2"),
-    "b0": ("Y4", "S0", "T3", "S1", "F6"),
-    "win": ("Y2",),
-    "tail": ("T0", "X4", "Y3", "F4", "T1", "X2", "Y0", "F2", "X3", "Y1", "F3", "X0", "F0", "X1"),
-    "end": ("F1",),
+    "w2b": ("R5", "S7"),
+    "d2": ("R6", "S8"),
+    "do": ("S5",),
+    "bt1": ("S6",),
+    "b2": ("R4", "T8", "T7"),
+    "w1b": ("T5", "R2"),
+    "b1": ("S4", "R3", "T6"),
+    "w0a": ("S2",),
+    "w0b": ("R0", "Y5", "Y7"),
+    "d0": ("S3", "R1", "S0", "Y6"),
+    "b0": ("T4", "T2", "Y8", "S1"),
+    "win": ("T0", "Y4"),
+    "tail": ("X8", "T3", "Y2", "T1", "da", "X6", "X5", "Y0", "Y3", "Y1", "X2", "X7", "F8", "X0", "X3", "F5",
+        "X4", "F6", "db", "X1"),
+    "end": ("F0", "F2", "F3", "F4", "F7", "F1"),
 }
 LEVELS = 32000.0
 MESH = pl.DeviceIdType.MESH
@@ -506,7 +504,7 @@
     micro, batch,
     order_ref, when_ref, images_ref, noises_ref, freq_ref, conv_ref, time_ref, attn_ref, io_ref, norm_ref,
     grads_ref, gion_ref, total_ref,
-    mats, dmats, other, give, land, ottmp, ot_ref, otbuf, otwide, xz, ionbuf, dion, diont, ionr, scal, scalr,
+    mats, dmats, other, give, land, ottmp, ot_ref, otbuf, otwide, xz, ionbuf, dion, diont, ionr, ions, ionq, scal, scalr,
     s1q, s1r, s2q, s2r, zq, zr, expo, kept, gother,
     ot_s, ot_r, ion_s, ion_r, g_s, g_r, r_s, r_r, d_s, d_r, n_s, n_r,
     *work,
@@ -711,6 +709,14 @@
             ion_c(0).start()
         elif kind == "iw":
             ion_c(0).wait()
+        elif kind == "da":
+            wait_all(dion_copy(j) for j in range(1, X * C))
+            ionr[mp] = diont[mp]
+            ions[...] = ionr[0] + ionr[1] + ionr[2] + ionr[3]
+            start_all(dion_again(j) for j in range(1, Z * Y))
+            ionq[dp] = ions[dp]
+        elif kind == "db":
+            wait_all(dion_again(j) for j in range(1, Z * Y))
 
     def do(steps):
         for kind in steps:
@@ -927,7 +933,7 @@
     seat = lax.broadcasted_iota(jnp.int32, (8, 1), 0)
     times = jnp.zeros((8, 1), F32)
     for n in range(IMGS):
-        index = when_ref[pl.ds(turn, 1), n : n + 1].astype(F32)
+        index = when_ref[pl.ds(turn, 1), n : n + 1]
         times = jnp.where(seat == n, (index + 0.5) / NT, times)
     angles = 1000.0 * times * freq_ref[...]
     feats = jnp.where(seat < IMGS, jnp.concatenate([jnp.sin(angles), jnp.cos(angles)], axis=1), 0.0).astype(BF16)
@@ -936,37 +942,32 @@
         lambda: ionbuf[...].reshape(CH, 128).T, mat, put, pump, dion, scal, *work,
     )
 
-    diont[...] = jnp.concatenate([dion[...], jnp.zeros((128 - 48, CH), F32)], axis=0).T.reshape(DEVICES, 8, 128)
+    diont[...] = (
+        jnp.concatenate([dion[...], jnp.zeros((128 - 48, CH), F32)], axis=0).T.reshape(X * C, Z * Y, 8, 128)
+    )
 
     def dion_copy(j):
-        there = (flat + j) % DEVICES
-        return remote(diont.at[there], ionr.at[flat], d_s.at[j], d_r.at[j], from_flat(there))
-
-    def dion_start(j, carry):
-        dion_copy(j).start()
-        return carry
-
-    lax.fori_loop(1, DEVICES, dion_start, 0)
-    ionr[flat] = diont[flat]
+        there = (mp + j) % (X * C)
+        return remote(diont.at[there], ionr.at[mp], d_s.at[j], d_r.at[j], (dp, there))
+
+    def dion_again(j):
+        there = (dp + j) % (Z * Y)
+        return remote(ions.at[there], ionq.at[dp], d_s.at[X * C + j], d_r.at[X * C + j], (there, mp))
+
+    start_all(dion_copy(j) for j in range(1, X * C))
     pump("tail")
-
-    def dion_wait(j, carry):
-        dion_copy(j).wait()
-        return carry
-
-    lax.fori_loop(1, DEVICES, dion_wait, 0)
-    small = jnp.sum(ionr[...], axis=0)
+    small = jnp.sum(ionq[...], axis=0)
     gion_ref[...] = small
-    square = jnp.sum(small * small)
+    square = small * small
     for part in squares:
-        square = square + jnp.sum(part)
+        square = square + part[0:8] + part[8:16]
 
     loss, plan_cost = scal[0:1, 0:1], scal[0:1, 1:2]
     lane = lax.broadcasted_iota(jnp.int32, (8, 128), 1)
-    tile = jnp.where(lane == 0, square, 0.0)
-    tile = jnp.where(lane == 1 + mp, loss, tile)
-    tile = jnp.where((lane == 1 + micro + mp) & (mp < micro) & (dp == 0), plan_cost, tile)
-    tile = jnp.where((mp >= micro) & (lane > 0), 0.0, tile)
+    line = lax.broadcasted_iota(jnp.int32, (8, 128), 0)
+    tile = jnp.where(line == 7, 0.0, square) + jnp.where(line == 0, pltpu.roll(square, 1, 0), 0.0)
+    tile = jnp.where((line == 7) & (lane == mp) & (mp < micro), loss, tile)
+    tile = jnp.where((line == 7) & (lane == micro + mp) & (mp < micro) & (dp == 0), plan_cost, tile)
     scal[...] = tile
     scalr[flat] = tile
 
@@ -1019,8 +1020,10 @@
             pltpu.VMEM((2, batch, SUB * POS), F32),
             pltpu.VMEM((X, C, Z, Y, 8, 128), F32),
             pltpu.VMEM((48, CH), F32),
-            pltpu.VMEM((DEVICES, 8, 128), F32),
-            pltpu.VMEM((DEVICES, 8, 128), F32),
+            pltpu.VMEM((X * C, Z * Y, 8, 128), F32),
+            pltpu.VMEM((X * C, Z * Y, 8, 128), F32),
+            pltpu.VMEM((Z * Y, 8, 128), F32),
+            pltpu.VMEM((Z * Y, 8, 128), F32),
             pltpu.VMEM((8, 128), F32),
             pltpu.VMEM((DEVICES, 8, 128), F32),
             pltpu.VMEM((MATS * 8 + count, 16, 128), jnp.int16),
@@ -1036,7 +1039,7 @@
             dma((7,)), dma((7,)),
             dma((count + 1, 7)), dma((count + 1, 7)),
             dma((count, 7)), dma((count, 7)),
-            dma((DEVICES,)), dma((DEVICES,)),
+            dma((X * C + Z * Y,)), dma((X * C + Z * Y,)),
             dma((DEVICES,)), dma((DEVICES,)),
         ] + work_space(),
         compiler_params=pltpu.CompilerParams(
@@ -1063,10 +1066,9 @@
 
 
 def adam_kernel(grads_ref, gion_ref, total_ref, *refs):
-    step = pl.program_id(0)
     old, new = refs[:20], refs[20:40]
     loss_ref, cost_ref, norm_ref = refs[40:]
-    norm = jnp.sqrt(total_ref[0:1, 0:1])
+    norm = jnp.sqrt(jnp.sum(total_ref[0:7], axis=(0, 1), keepdims=True))
     scale = CLIP_NORM / jnp.maximum(norm, CLIP_NORM)
 
     def update(kind, at, gradient):
@@ -1075,51 +1077,39 @@
             new[5 * part + kind][at] = got[part]
 
     for layer, start in enumerate(CONV_AT):
-
-        @pl.when(step == layer)
-        def conv_step():
-            update(1, (0,), grads_ref[start : start + 9])
-
-    @pl.when(step == 0)
-    def others():
-        for layer, start in enumerate(TIME_AT):
-            update(2, (layer,), grads_ref[start])
-        for j in range(4):
-            update(3, (slice(None), j), grads_ref[ATTN_AT + j])
-        tile = gion_ref[...]
-        own = old[0].shape[0] // (2 * SUB)
-        for kind, pieces in ((0, (0, 16)), (4, (32,))):
-            flat = [tile[r : r + 1, at : at + SUB] for r in range(own) for at in pieces]
-            flat = jnp.concatenate(flat, axis=1)
-            got = adam_update(
-                *[old[5 * part + kind][...].reshape(flat.shape) for part in range(4)], flat * scale, RATES[kind]
-            )
-            for part in range(4):
-                new[5 * part + kind][...] = got[part].reshape(old[kind].shape)
-        micro = loss_ref.shape[0]
-        for m in range(micro):
-            loss_ref[m] = total_ref[0, 1 + m]
-            cost_ref[m] = total_ref[0, 1 + micro + m]
-        norm_ref[0] = norm[0, 0]
+        update(1, (layer,), grads_ref[start : start + 9])
+    for layer, start in enumerate(TIME_AT):
+        update(2, (layer,), grads_ref[start])
+    for j in range(4):
+        update(3, (slice(None), j), grads_ref[ATTN_AT + j])
+    tile = gion_ref[...]
+    own = old[0].shape[0] // (2 * SUB)
+    for kind, pieces in ((0, (0, 16)), (4, (32,))):
+        flat = [tile[r : r + 1, at : at + SUB] for r in range(own) for at in pieces]
+        flat = jnp.concatenate(flat, axis=1)
+        got = adam_update(
+            *[old[5 * part + kind][...].reshape(flat.shape) for part in range(4)], flat * scale, RATES[kind]
+        )
+        for part in range(4):
+            new[5 * part + kind][...] = got[part].reshape(old[kind].shape)
+    micro = loss_ref.shape[0]
+    for m in range(micro):
+        loss_ref[m] = total_ref[7, m]
+        cost_ref[m] = total_ref[7, micro + m]
+    norm_ref[0] = norm[0, 0]
 
 
 def adam(micro, grads, gion, total, state):
     whole = pl.BlockSpec(memory_space=pltpu.VMEM)
     scalar = pl.BlockSpec(memory_space=pltpu.SMEM)
 
-    def spec(v):
-        if v.ndim == 4:
-            return pl.BlockSpec((1,) + v.shape[1:], lambda i: (i, 0, 0, 0))
-        return pl.BlockSpec(v.shape, lambda i: (0,) * v.ndim)
-
     return pl.pallas_call(
         adam_kernel,
-        grid=(len(CONV_AT),),
         out_shape=tuple(jax.ShapeDtypeStruct(v.shape, F32) for v in state)
         + (jax.ShapeDtypeStruct((micro,), F32),) * 2
         + (jax.ShapeDtypeStruct((1,), F32),),
-        in_specs=[spec(v) for v in (grads, gion, total)] + [spec(v) for v in state],
-        out_specs=tuple(spec(v) for v in state) + (scalar,) * 3,
+        in_specs=[whole] * (3 + len(state)),
+        out_specs=(whole,) * len(state) + (scalar,) * 3,
         compiler_params=pltpu.CompilerParams(vmem_limit_bytes=60 * 2**20),
     )(grads, gion, total, *state)
 
@@ -1164,7 +1154,7 @@
     averages = (io_average, conv_average, time_average, attn_average, norm_average)
     if fused:
         grads, gion, total = fused_network(
-            micro, batch, order, time_index, images, noises, conv_weight, time_weight, attn_weight, io_weight, norm_param
+            micro, batch, order, time_index.astype(F32), images, noises, conv_weight, time_weight, attn_weight, io_weight, norm_param
         )
         out = adam(micro, grads, gion, total, weights + firsts + seconds + averages)
         return out[:22] + (out[22].reshape(()),)

time: 113 us -> 105 us (0.929)
  Pallas kernels: 111 us -> 102 us
    pallas_call x1, Pallas kernels: 105 us -> 97.6 us  [fused_network(): pl.pallas_call(functools.partial(fused_kernel, micro, batch), out_shape=(...]
    pallas_call x1, Pallas kernels: 5.87 us -> 4.72 us  [adam(): pl.pallas_call(adam_kernel, out_shape=tuple((jax.ShapeDtypeStruct(v.shape...]
where the time goes in v4:
time: 105 us
  Pallas kernels  102 us (97%)
    pallas_call x1, Pallas kernels, fused_network(): pl.pallas_call(functools.partial(fused_kernel, micro, batch), out_shape=(...  97.6 us
    pallas_call x1, Pallas kernels, adam(): pl.pallas_call(adam_kernel, out_shape=tuple((jax.ShapeDtypeStruct(v.shape...  4.72 us

profile of v4, /device:TPU:0, one launch (start us, length us, event | category | flops | bytes accessed | tf_op | source)
XLA Modules:
  0.0 104.5 jit_solution(3559511280657727924)
XLA Ops:
  0.7 0.8 copy.48
  1.4 0.6 convert_element_type.3.when_ref
  2.0 97.6 %shard_map.416 = (f32[42,32,64]{2,1,0:T(8,128)}, f32[8,128]{1,0:T(8,128)}, f32[8,128]{1,0:T(8,128)}) custom-call(s32[6]{0:T(128)} %order_ref.1, f32[3,2]{1,0:T(4,128)} %convert_element_type.3.when_ref, bf16[6,3072]{1,0:T(8,128)(2,1)} %images_ref.1, bf16[3,2,3072]{2,1,0:T(2,128)(2,1)} %noises_ref.1, f32[1,128]{1,0:T(1,128)} %constant.2.clone.freq_ref, ...), custom_call_target="tpu_custom_call" | custom-call | tf_op jit(solution)/shard_map/pallas_call | solution.py:1001
  99.6 4.7 %shard_map.417 = (f32[192]{0:T(256)}, f32[4,9,32,64]{3,2,1,0:T(8,128)}, f32[2,32,64]{2,1,0:T(8,128)}, f32[32,4,64]{2,1,0:T(4,128)}, f32[96]{0:T(128)}, /*index=5...) custom-call(f32[42,32,64]{2,1,0:T(8,128)} %get-tuple-element.49.grad, ...), custom_call_target="tpu_custom_call" | custom-call | tf_op jit(solution)/shard_map/pallas_call | solution.py:1106

commit v5 on v4

--- a/solution.py
+++ b/solution.py
@@ -25,40 +25,38 @@
 ATTN_AT = 19
 CHUNKS = ((0, 5), (5, 5), (10, 5), (15, 4), (19, 4), (23, 5), (28, 5), (33, 5), (38, 4))
 SPLITS = (5, 15, 28, 38)
-EARLY = (3, 8)
+EARLY = (4, 8)
 PLAN = {
-    "start": ("zero", "merge", "Z1", "Z7", "A3", "ot", "A8", "Z0", "Z2", "iz", "U1", "B8", "U7", "iu", "B3", "Z5",
-        "Z4", "U0", "Z6", "otw", "V1"),
-    "sink": ("U2", "iv", "U5", "E3", "V0", "U4", "V2", "U6", "ic", "iw", "C1", "V4"),
-    "h0": ("E8", "V5", "C0"),
-    "n0": ("V6", "C3", "W1", "C2", "V7"),
-    "c0": ("W0",),
-    "n1": ("C4",),
-    "c1": ("W3", "W2"),
+    "start": ("zero", "merge", "Z2", "A4", "Z0", "iz", "A8", "Z1", "Z3", "ot", "Z7", "Z5", "U2", "B8", "Z6", "U0",
+        "B4", "U1", "V2", "iu", "U3", "V0", "E4", "V1", "iv", "U5", "otw", "C2", "V3", "U6"),
+    "h0": ("C0", "E8", "ic", "U7", "C1", "V5", "iw", "W0"),
+    "n0": ("W2", "V6", "C4", "C3"),
+    "c0": ("W1",),
+    "n1": ("V7",),
+    "c1": ("W3", "W4"),
     "n2": ("C5",),
-    "qkv": ("W4",),
     "at0": ("C6",),
     "ao": ("C8", "W5"),
     "n3": ("C7",),
     "c2": ("W6",),
-    "c3": ("W7", "W8"),
+    "c3": ("W8", "W7"),
     "w3b": ("R7",),
-    "d3": ("R8",),
+    "w2a": ("R8",),
     "w2b": ("R5", "S7"),
-    "d2": ("R6", "S8"),
-    "do": ("S5",),
-    "bt1": ("S6",),
-    "b2": ("R4", "T8", "T7"),
-    "w1b": ("T5", "R2"),
-    "b1": ("S4", "R3", "T6"),
-    "w0a": ("S2",),
-    "w0b": ("R0", "Y5", "Y7"),
-    "d0": ("S3", "R1", "S0", "Y6"),
-    "b0": ("T4", "T2", "Y8", "S1"),
-    "win": ("T0", "Y4"),
-    "tail": ("X8", "T3", "Y2", "T1", "da", "X6", "X5", "Y0", "Y3", "Y1", "X2", "X7", "F8", "X0", "X3", "F5",
-        "X4", "F6", "db", "X1"),
-    "end": ("F0", "F2", "F3", "F4", "F7", "F1"),
+    "b3": ("R6",),
+    "do": ("S8",),
+    "bt0": ("S5",),
+    "b2": ("T7",),
+    "w1b": ("T8", "R2", "S6", "R4"),
+    "d1": ("R3",),
+    "b1": ("T5",),
+    "w0a": ("S2", "Y7"),
+    "w0b": ("R0", "S4", "Y8"),
+    "d0": ("R1", "T6", "S3"),
+    "b0": ("Y5", "T2", "S1", "X7", "S0", "X8"),
+    "win": ("T4", "Y6", "Y2", "T3", "T1", "X6", "Y4", "T0", "F7", "Y3", "X2"),
+    "tail": ("Y1", "Y0", "F2", "X3", "da", "F3", "X1", "F6", "X5", "X4", "db", "X0"),
+    "end": ("F5", "F4", "F8", "F1", "F0"),
 }
 LEVELS = 32000.0
 MESH = pl.DeviceIdType.MESH
@@ -498,6 +496,7 @@
 
 Z, Y, X, C = 4, 2, 2, 2
 DEVICES = Z * Y * X * C
+PLANE = DEVICES // Z
 
 
 def fused_kernel(
@@ -969,22 +968,22 @@
     tile = jnp.where((line == 7) & (lane == mp) & (mp < micro), loss, tile)
     tile = jnp.where((line == 7) & (lane == micro + mp) & (mp < micro) & (dp == 0), plan_cost, tile)
     scal[...] = tile
-    scalr[flat] = tile
-
-    def n_copy(j):
-        return remote(scal, scalr.at[flat], n_s.at[j], n_r.at[j], from_flat((flat + j) % DEVICES))
+    spread = z * PLANE + y * (X * C) + mp
+    scalr[spread] = tile
 
     def n_start(j, carry):
-        n_copy(j).start()
+        there = (spread + j) % DEVICES
+        remote(
+            scal, scalr.at[spread], n_s.at[0], n_r.at[0],
+            (there // PLANE * Y + there % PLANE // (X * C), there % (X * C)),
+        ).start()
         return carry
 
-    def n_wait(j, carry):
-        n_copy(j).wait()
-        return carry
-
-    lax.fori_loop(1, DEVICES, n_start, 0)
+    for low, high in ((2 * PLANE, DEVICES), (PLANE, 2 * PLANE), (1, PLANE)):
+        lax.fori_loop(low, high, n_start, 0)
     pump("end")
-    lax.fori_loop(1, DEVICES, n_wait, 0)
+    rest = pl.ds(0, DEVICES - 1)
+    remote(scalr.at[rest], scalr.at[rest], n_s.at[0], n_r.at[0], sibling).wait()
     total_ref[...] = jnp.sum(scalr[...], axis=0)
 
 
@@ -1040,7 +1039,7 @@
             dma((count + 1, 7)), dma((count + 1, 7)),
             dma((count, 7)), dma((count, 7)),
             dma((X * C + Z * Y,)), dma((X * C + Z * Y,)),
-            dma((DEVICES,)), dma((DEVICES,)),
+            dma((1,)), dma((1,)),
         ] + work_space(),
         compiler_params=pltpu.CompilerParams(
             vmem_limit_bytes=60 * 2**20, collective_id=0, has_side_effects=True

time: 105 us -> 103 us (0.981)
    pallas_call x1, Pallas kernels: 97.6 us -> 96 us  [fused_network(): pl.pallas_call(functools.partial(fused_kernel, micro, batch), out_shape=(...]
where the time goes in v5:
time: 103 us
  Pallas kernels  101 us (98%)
    pallas_call x1, Pallas kernels, fused_network(): pl.pallas_call(functools.partial(fused_kernel, micro, batch), out_shape=(...  96 us
    pallas_call x1, Pallas kernels, adam(): pl.pallas_call(adam_kernel, out_shape=tuple((jax.ShapeDtypeStruct(v.shape...  4.72 us

profile of v5, /device:TPU:0, one launch (start us, length us, event | category | flops | bytes accessed | tf_op | source)
XLA Modules:
  0.0 102.9 jit_solution(17723395409418790293)
XLA Ops:
  0.7 0.8 copy.48
  1.4 0.6 convert_element_type.3.when_ref
  2.0 96.0 %shard_map.416 = (f32[42,32,64]{2,1,0:T(8,128)}, f32[8,128]{1,0:T(8,128)}, f32[8,128]{1,0:T(8,128)}) custom-call(s32[6]{0:T(128)} %order_ref.1, f32[3,2]{1,0:T(4,128)} %convert_element_type.3.when_ref, bf16[6,3072]{1,0:T(8,128)(2,1)} %images_ref.1, bf16[3,2,3072]{2,1,0:T(2,128)(2,1)} %noises_ref.1, f32[1,128]{1,0:T(1,128)} %constant.2.clone.freq_ref, ...), custom_call_target="tpu_custom_call" | custom-call | tf_op jit(solution)/shard_map/pallas_call | solution.py:1000
  98.0 4.7 %shard_map.417 = (f32[192]{0:T(256)}, f32[4,9,32,64]{3,2,1,0:T(8,128)}, f32[2,32,64]{2,1,0:T(8,128)}, f32[32,4,64]{2,1,0:T(4,128)}, f32[96]{0:T(128)}, /*index=5...) custom-call(f32[42,32,64]{2,1,0:T(8,128)} %get-tuple-element.49.grad, ...), custom_call_target="tpu_custom_call" | custom-call | tf_op jit(solution)/shard_map/pallas_call | solution.py:1105

commit v6 on v5

--- a/solution.py
+++ b/solution.py
@@ -27,36 +27,32 @@
 SPLITS = (5, 15, 28, 38)
 EARLY = (4, 8)
 PLAN = {
-    "start": ("zero", "merge", "Z2", "A4", "Z0", "iz", "A8", "Z1", "Z3", "ot", "Z7", "Z5", "U2", "B8", "Z6", "U0",
-        "B4", "U1", "V2", "iu", "U3", "V0", "E4", "V1", "iv", "U5", "otw", "C2", "V3", "U6"),
-    "h0": ("C0", "E8", "ic", "U7", "C1", "V5", "iw", "W0"),
-    "n0": ("W2", "V6", "C4", "C3"),
-    "c0": ("W1",),
-    "n1": ("V7",),
-    "c1": ("W3", "W4"),
-    "n2": ("C5",),
-    "at0": ("C6",),
-    "ao": ("C8", "W5"),
-    "n3": ("C7",),
-    "c2": ("W6",),
+    "start": ("zero", "ot", "merge", "Z3", "A4", "Z5", "Z0", "iz", "A8", "U3", "B4", "Z2", "Z1", "U5", "Z7", "iu",
+        "B8", "U0", "V3", "U2", "iv", "Z6", "U1", "V0", "otw", "E4", "U7", "U6", "V1", "ic", "C3"),
+    "sink": ("V2", "E8", "C0", "W3", "V6"),
+    "h0": ("V5", "iw", "C1"),
+    "c0": ("C4", "V7", "W0", "C2", "W1"),
+    "c1": ("C6", "W4", "W2"),
+    "at0": ("C5",),
+    "n3": ("C8", "W6", "C7"),
+    "c2": ("W5",),
     "c3": ("W8", "W7"),
     "w3b": ("R7",),
-    "w2a": ("R8",),
+    "d3": ("R8",),
     "w2b": ("R5", "S7"),
-    "b3": ("R6",),
-    "do": ("S8",),
-    "bt0": ("S5",),
-    "b2": ("T7",),
-    "w1b": ("T8", "R2", "S6", "R4"),
-    "d1": ("R3",),
-    "b1": ("T5",),
-    "w0a": ("S2", "Y7"),
-    "w0b": ("R0", "S4", "Y8"),
-    "d0": ("R1", "T6", "S3"),
-    "b0": ("Y5", "T2", "S1", "X7", "S0", "X8"),
-    "win": ("T4", "Y6", "Y2", "T3", "T1", "X6", "Y4", "T0", "F7", "Y3", "X2"),
-    "tail": ("Y1", "Y0", "F2", "X3", "da", "F3", "X1", "F6", "X5", "X4", "db", "X0"),
-    "end": ("F5", "F4", "F8", "F1", "F0"),
+    "d2": ("R6",),
+    "b3": ("S8",),
+    "do": ("S5",),
+    "bt1": ("S6",),
+    "b2": ("R4", "T7"),
+    "d1": ("T8", "R3", "T5", "R2", "S4"),
+    "w0a": ("T6",),
+    "w0b": ("S3",),
+    "d0": ("R1", "Y7", "S2", "R0"),
+    "b0": ("T4", "Y5", "S1", "Y6", "S0", "T3", "Y8"),
+    "win": ("X7", "Y4", "T2", "T1"),
+    "tail": ("X6", "Y3", "T0", "Y2", "da", "Y1", "X3", "Y0", "F6", "X4", "X5", "X1", "X2", "X8", "db", "X0"),
+    "end": ("F8", "F5", "F2", "F7", "F3", "F1", "F4", "F0"),
 }
 LEVELS = 32000.0
 MESH = pl.DeviceIdType.MESH

time: 103 us -> 103 us (level)
  no operation moved by 1% of the time
where the time goes in v6:
time: 103 us; the launch traced here: 102 us
  Pallas kernels  100 us (97%)
    pallas_call x1, Pallas kernels, fused_network(): pl.pallas_call(functools.partial(fused_kernel, micro, batch), out_shape=(...  95.5 us
    pallas_call x1, Pallas kernels, adam(): pl.pallas_call(adam_kernel, out_shape=tuple((jax.ShapeDtypeStruct(v.shape...  4.72 us

profile of v6, /device:TPU:0, one launch (start us, length us, event | category | flops | bytes accessed | tf_op | source)
XLA Modules:
  0.0 102.4 jit_solution(7295666844356977239)
XLA Ops:
  0.7 0.8 copy.48
  1.4 0.6 convert_element_type.3.when_ref
  2.0 95.5 %shard_map.416 = (f32[42,32,64]{2,1,0:T(8,128)}, f32[8,128]{1,0:T(8,128)}, f32[8,128]{1,0:T(8,128)}) custom-call(s32[6]{0:T(128)} %order_ref.1, f32[3,2]{1,0:T(4,128)} %convert_element_type.3.when_ref, bf16[6,3072]{1,0:T(8,128)(2,1)} %images_ref.1, bf16[3,2,3072]{2,1,0:T(2,128)(2,1)} %noises_ref.1, f32[1,128]{1,0:T(1,128)} %constant.2.clone.freq_ref, ...), custom_call_target="tpu_custom_call" | custom-call | tf_op jit(solution)/shard_map/pallas_call | solution.py:996
  97.5 4.7 %shard_map.417 = (f32[192]{0:T(256)}, f32[4,9,32,64]{3,2,1,0:T(8,128)}, f32[2,32,64]{2,1,0:T(8,128)}, f32[32,4,64]{2,1,0:T(4,128)}, f32[96]{0:T(128)}, /*index=5...) custom-call(f32[42,32,64]{2,1,0:T(8,128)} %get-tuple-element.49.grad, ...), custom_call_target="tpu_custom_call" | custom-call | tf_op jit(solution)/shard_map/pallas_call | solution.py:1101

commit v7 on v6

--- a/solution.py
+++ b/solution.py
@@ -532,7 +532,7 @@
         )
         return carry
 
-    lax.fori_loop(1, DEVICES, greet, 0)
+    lax.fori_loop(1, DEVICES, greet, 0, unroll=True)
 
     def wide(v):
         v = v.astype(BF16).astype(F32)
@@ -976,7 +976,7 @@
         return carry
 
     for low, high in ((2 * PLANE, DEVICES), (PLANE, 2 * PLANE), (1, PLANE)):
-        lax.fori_loop(low, high, n_start, 0)
+        lax.fori_loop(low, high, n_start, 0, unroll=True)
     pump("end")
     rest = pl.ds(0, DEVICES - 1)
     remote(scalr.at[rest], scalr.at[rest], n_s.at[0], n_r.at[0], sibling).wait()

time: 103 us -> 102 us (level)
  no operation moved by 1% of the time
where the time goes in v7:
time: 102 us
  Pallas kernels  99.5 us (98%)
    pallas_call x1, Pallas kernels, fused_network(): pl.pallas_call(functools.partial(fused_kernel, micro, batch), out_shape=(...  94.8 us
    pallas_call x1, Pallas kernels, adam(): pl.pallas_call(adam_kernel, out_shape=tuple((jax.ShapeDtypeStruct(v.shape...  4.72 us

profile of v7, /device:TPU:0, one launch (start us, length us, event | category | flops | bytes accessed | tf_op | source)
XLA Modules:
  0.0 101.7 jit_solution(9906920849829586415)
XLA Ops:
  0.7 0.8 copy.48
  1.4 0.6 convert_element_type.3.when_ref
  2.0 94.8 %shard_map.416 = (f32[42,32,64]{2,1,0:T(8,128)}, f32[8,128]{1,0:T(8,128)}, f32[8,128]{1,0:T(8,128)}) custom-call(s32[6]{0:T(128)} %order_ref.1, f32[3,2]{1,0:T(4,128)} %convert_element_type.3.when_ref, bf16[6,3072]{1,0:T(8,128)(2,1)} %images_ref.1, bf16[3,2,3072]{2,1,0:T(2,128)(2,1)} %noises_ref.1, f32[1,128]{1,0:T(1,128)} %constant.2.clone.freq_ref, ...), custom_call_target="tpu_custom_call" | custom-call | tf_op jit(solution)/shard_map/pallas_call | solution.py:996
  96.8 4.7 %shard_map.417 = (f32[192]{0:T(256)}, f32[4,9,32,64]{3,2,1,0:T(8,128)}, f32[2,32,64]{2,1,0:T(8,128)}, f32[32,4,64]{2,1,0:T(4,128)}, f32[96]{0:T(128)}, /*index=5...) custom-call(f32[42,32,64]{2,1,0:T(8,128)} %get-tuple-element.49.grad, ...), custom_call_target="tpu_custom_call" | custom-call | tf_op jit(solution)/shard_map/pallas_call | solution.py:1101
